TPU v7x, 512 devices: a whole 4x8x8 slice. The times are simulated.
512 devices in a mesh: space: 64 (over y, z_lo, core), eig: 8 (over x, z_hi).
Axes of the slice: x: 4, y: 8, z: 8 (z_hi: 2, z_lo: 4; z = z_hi * 4 + z_lo), core: 2. Of those that a mesh axis runs over, the one named last changes fastest.
Arguments:
- eigenvectors: bfloat16 [256, 3, 2, 64, 512], P('eig', None, None, 'space'), may hold values from -2.5 to 2.5
- gauge_links: float32 [3, 3, 3, 2, 64, 512], P(None, None, None, None, 'space'), may hold values from -6 to 6
- momenta: int32 [4, 3], replicated, may hold values from -2 to 2
Outputs:
- elementals: float32 [3, 4, 2, 256, 256], P(None, None, None, 'eig', 'space')
All inputs are finite; a program needn't handle non-finite values.
Results may differ from a plain program's by a relative error of at most 0.0029.
Values may be sent and summed in bfloat16 or wider, within the bound.
No kernel may reach another device: no remote copies, remote signals or barrier semaphores. Data moves between devices by JAX's collectives and lax.ppermute only.
A program may use at most 64 MiB of HBM per device.

v0:
```python
import math

import jax
import jax.numpy as jnp
from jax import lax
from jax.sharding import PartitionSpec as P

LX = 64
LY = 8


def passed_along(value, axis, steps):
    count = lax.axis_size(axis)
    pairs = [(source, (source + steps) % count) for source in range(count)]
    return lax.ppermute(value, axis, pairs)


def plane_phases(momenta, heights, extent):
    site_index = jnp.arange(LX * LY, dtype=jnp.int32)
    across_index = site_index % LX
    along_index = site_index // LX
    x_frac = jnp.mod(momenta[:, 0:1] * across_index[None, :], LX).astype(jnp.float32) / LX
    y_frac = jnp.mod(momenta[:, 1:2] * along_index[None, :], LY).astype(jnp.float32) / LY
    z_frac = jnp.mod(momenta[:, 2:3] * heights[None, :], extent).astype(jnp.float32) / extent
    angles = 2.0 * math.pi * (x_frac[:, None, :] + y_frac[:, None, :] + z_frac[:, :, None])
    return (jnp.cos(angles), jnp.sin(angles))


def left_operand(vectors, link, cosines, sines):
    real_vec = vectors[:, :, 0]
    imag_vec = vectors[:, :, 1]
    real_link = link[:, :, 0]
    imag_link = link[:, :, 1]
    real_base = jnp.sum(
        real_vec[:, :, None] * real_link[None] + imag_vec[:, :, None] * imag_link[None], axis=1
    )
    imag_base = jnp.sum(
        real_vec[:, :, None] * imag_link[None] - imag_vec[:, :, None] * real_link[None], axis=1
    )
    real_left = real_base[None] * cosines[:, None, None] + imag_base[None] * sines[:, None, None]
    imag_left = imag_base[None] * cosines[:, None, None] - real_base[None] * sines[:, None, None]
    return jnp.stack([real_left, imag_left], axis=3).astype(jnp.bfloat16)


def expand(left):
    real_part = left[:, :, :, 0]
    imag_part = left[:, :, :, 1]
    return jnp.stack(
        [jnp.stack([real_part, -imag_part], axis=3), jnp.stack([imag_part, real_part], axis=3)],
        axis=1,
    )


def roll_across(field):
    shaped = field.reshape(field.shape[:-1] + (LY, LX))
    return jnp.roll(shaped, -1, axis=-1).reshape(field.shape)


def roll_along(field):
    shaped = field.reshape(field.shape[:-1] + (LY, LX))
    return jnp.roll(shaped, -1, axis=-2).reshape(field.shape)


def product(left, right):
    return jnp.einsum("mqncrzs,jcrzs->mqnj", left, right, preferred_element_type=jnp.float32)


def body(eigenvectors, gauge_links, momenta):
    planes = eigenvectors.shape[3]
    extent = planes * lax.axis_size("space")
    heights = lax.axis_index("space") * planes + jnp.arange(planes, dtype=jnp.int32)
    cosines, sines = plane_phases(momenta, heights, extent)
    resident = eigenvectors.astype(jnp.float32)
    left_across = expand(left_operand(resident, gauge_links[0], cosines, sines))
    left_along = expand(left_operand(resident, gauge_links[1], cosines, sines))
    left_upward = left_operand(resident, gauge_links[2], cosines, sines)
    upper_block = passed_along(eigenvectors, "space", -1)
    raised_block = jnp.concatenate([eigenvectors[:, :, :, 1:], upper_block], axis=3)
    gathered, raised = (
        lax.all_gather(eigenvectors, "eig", axis=0, tiled=True),
        lax.all_gather(raised_block, "eig", axis=0, tiled=True),
    )
    partials = jnp.stack(
        [
            product(left_across, roll_across(gathered)),
            product(left_along, roll_along(gathered)),
            product(expand(left_upward), raised),
        ]
    )
    return lax.psum_scatter(partials, "space", scatter_dimension=4, tiled=True)


def solution(mesh):
    return jax.shard_map(
        body,
        mesh=mesh,
        in_specs=(
            P("eig", None, None, "space", None),
            P(None, None, None, None, "space", None),
            P(),
        ),
        out_specs=P(None, None, None, "eig", "space"),
        check_vma=False,
    )
```

profile of v0, /device:TPU:1, one launch (start us, length us, event | category | flops | bytes accessed | tf_op | source)
XLA Modules:
  0.0 722.9 jit_solution(1651313872407603743)
XLA Ops:
  6.5 0.7 all-gather.3.cloned.1.call-update
  7.3 1.0 copy.60
  8.3 8.8 %collective-permute-start = (bf16[32,3,2,1,512]{4,0,1,2,3:T(8,128)(2,1)S(1)}, bf16[32,3,2,1,512]{4,0,1,2,3:T(8,128)(2,1)S(1)}, u32[]{:S(2)}, u32[]{:S(2)}) collective-permute-start(bf16[32,3,2,1,512]{4,0,1,2,3:T(8,128)(2,1)S(1)} %copy.60), channel_id=1, source_target_pairs={{0,504},{8,0},{16,8},{24,16},{32,24},{40,32},{48,40},{56,48},{64,5... | collective-permute-start | bytes 589832 | tf_op jit(solution)/shard_map/ppermute | solution.py:15
  17.1 0.8 slice_bitcast_fusion.2
  18.0 1.0 slice_reduce_fusion.1
  19.0 1.0 copy_convert_fusion
  20.0 0.5 add_reduce_fusion.2
  20.5 0.7 copy-done.4
  21.3 0.2 fusion.46
  21.5 0.2 fusion.41
  21.6 0.7 fusion.20
  22.4 0.2 fusion.28
  22.7 0.9 maximum_bitcast_fusion.15
  23.7 0.9 maximum_bitcast_fusion.14
  24.8 1.3 maximum_bitcast_fusion.12
  26.1 63.4 %all-gather.3.cloned.1.call-done = bf16[256,3,2,1,512]{4,2,3,1,0:T(2,128)(2,1)} async-done(((bf16[32,3,2,1,512]{4,2,3,1,0:T(2,128)(2,1)}), bf16[256,3,2,1,512]{4,2,3,1,0:T(2,128)(2,1)}) %all-gather.3.cloned.1.call-update) | async-done | bytes 1572880 | tf_op jit(solution)/shard_map/all_gather | solution.py:80
  89.5 3.5 copy.52
  93.3 0.9 slice.90
  94.4 1.0 copy-done
  95.4 0.2 copy-done.1
  95.6 0.6 fusion.12
  96.3 0.3 pad_maximum_fusion
  96.5 0.8 copy-done.2
  97.4 0.2 copy-done.3
  97.6 0.6 fusion.18
  98.2 65.4 %all-gather.5.cloned.1.call-done = bf16[256,3,2,1,512]{4,0,1,2,3:T(8,128)(2,1)} async-done(((bf16[32,3,2,1,512]{4,0,1,2,3:T(8,128)(2,1)}), bf16[256,3,2,1,512]{4,0,1,2,3:T(8,128)(2,1)}) %all-gather.5.cloned.1.call-update) | async-done | bytes 1572880 | tf_op jit(solution)/shard_map/all_gather | solution.py:81
  163.5 2.0 fusion.15
  165.7 2.9 copy.62
  168.5 1.3 dynamic-slice
  170.5 544.5 %all-reduce.3.cloned.1.call-done = f32[3,4,2,32,256]{3,1,2,0,4:T(4,128)} async-done(((f32[3,4,2,32,256]{3,1,2,0,4:T(4,128)}), f32[3,4,2,32,256]{3,1,2,0,4:T(4,128)}) %all-reduce.3.cloned.1.call-update) | async-done | bytes 786448
  715.0 0.8 constant_dynamic-slice_fusion
  715.8 0.6 copy.63
  (32 shorter events, 1.0 us)
Async XLA Ops:
  6.5 83.0 %all-gather.3.cloned.1.call-start = ((), (), s32[]{:S(2)}) async-start(), calls=%async_computation | async-start | bytes 1769472 | tf_op jit(solution)/shard_map/all_gather | solution.py:80
  7.3 156.3 %all-gather.5.cloned.1.call-start = ((), (), s32[]{:S(2)}) async-start(), calls=%async_computation.1 | async-start | bytes 1769472 | tf_op jit(solution)/shard_map/all_gather | solution.py:81
  8.3 12.2 %collective-permute-start = (bf16[32,3,2,1,512]{4,0,1,2,3:T(8,128)(2,1)S(1)}, bf16[32,3,2,1,512]{4,0,1,2,3:T(8,128)(2,1)S(1)}, u32[]{:S(2)}, u32[]{:S(2)}) collective-permute-start(bf16[32,3,2,1,512]{4,0,1,2,3:T(8,128)(2,1)S(1)} %copy.60), channel_id=1, source_target_pairs={{0,504},{8,0},{16,8},{24,16},{32,24},{40,32},{48,40},{56,48},{64,5... | collective-permute-start | bytes 589832 | tf_op jit(solution)/shard_map/ppermute | solution.py:15
  19.0 2.3 copy-start.5
  20.5 0.7 copy-start.4
  21.2 693.8 %all-reduce.3.cloned.1.call-start = ((), (), s32[]{:S(2)}) async-start(), calls=%async_computation.2 | async-start | bytes 6291456
  94.3 1.1 copy-start
  94.3 1.4 copy-start.1
  96.2 1.1 copy-start.2
  96.2 1.4 copy-start.3
Sparse Core Ops, SparseCore 0:
  10.5 78.9 all-gather.2
  92.8 70.7 all-gather.4
  168.7 546.2 all-reduce.2
where the time goes:
time: 723 us
  waiting for transfers between devices  674 us (93%)
  local copies, waits for them, and re-layouts  16.1 us (2%)
  between operations  14.1 us (2%)
  starting transfers between devices  8.87 us (1%)
    unnamed x4, waiting for transfers between devices  545 us
    all_gather x1, waiting for transfers between devices, body(): lax.all_gather(raised_block, 'eig', axis=0, tiled=True)  65.4 us
    all_gather x1, waiting for transfers between devices, body(): lax.all_gather(eigenvectors, 'eig', axis=0, tiled=True)  63.4 us
  transfers between devices with their start and end apart: 4, of which 3 were waited for; matrix products, arithmetic and copies ran while one was open for 2% of the time, Pallas kernels for 0%

commit v1 on v0

v1 whole, which is shorter than its diff:
```python
import functools
import math

import jax
import jax.numpy as jnp
from jax import lax
from jax.experimental import pallas as pl
from jax.experimental.pallas import tpu as pltpu
from jax.sharding import PartitionSpec as P

LX = 64
LY = 8
SITES = LX * LY
ROWS = 32
DEPTH = 6 * SITES
VMEM_BYTES = 40 * 1024 * 1024


def moved_across(field):
    lane = lax.broadcasted_iota(jnp.int32, field.shape, 1)
    return jnp.where(
        lane % LX == 0, pltpu.roll(field, SITES - LX + 1, 1), pltpu.roll(field, 1, 1)
    )


def moved_along(field):
    return pltpu.roll(field, LX, 1)


MOVES = (moved_across, moved_along, lambda field: field)


def left_kernel(momenta_ref, height_ref, block_ref, link_ref, left_ref, table_ref):
    row = lax.broadcasted_iota(jnp.int32, (8, SITES), 0) % 4
    site = lax.broadcasted_iota(jnp.int32, (8, SITES), 1)

    def component(k):
        value = jnp.full((8, SITES), momenta_ref[3, k], jnp.int32)
        for p in range(3):
            value = jnp.where(row == p, momenta_ref[p, k], value)
        return value

    x_frac = ((component(0) * (site % LX)) & (LX - 1)).astype(jnp.float32) / LX
    y_frac = ((component(1) * (site // LX)) & (LY - 1)).astype(jnp.float32) / LY
    extent = height_ref[1]
    z_frac = ((component(2) * height_ref[0]) & (extent - 1)).astype(jnp.float32)
    z_frac = z_frac / extent.astype(jnp.float32)
    angles = 2.0 * math.pi * (x_frac + y_frac + z_frac)
    first = lax.broadcasted_iota(jnp.int32, (8, SITES), 0) < 4
    table = jnp.where(first, jnp.cos(angles), jnp.sin(angles))
    for d in range(3):
        table_ref[d] = MOVES[d](table)

    def rows_of(group, carry):
        rows = pl.ds(pl.multiple_of(group * 16, 16), 16)
        for d in range(3):
            for out_colour in range(3):
                real_base = jnp.zeros((16, SITES), jnp.float32)
                imag_base = jnp.zeros((16, SITES), jnp.float32)
                for colour in range(3):
                    at = 2 * SITES * colour
                    real_vec = block_ref[rows, at : at + SITES].astype(jnp.float32)
                    imag_vec = block_ref[rows, at + SITES : at + 2 * SITES].astype(jnp.float32)
                    real_link = link_ref[d, colour, out_colour, 0:1, :]
                    imag_link = link_ref[d, colour, out_colour, 1:2, :]
                    real_base += real_vec * real_link + imag_vec * imag_link
                    imag_base += real_vec * imag_link - imag_vec * real_link
                real_base, imag_base = MOVES[d](real_base), MOVES[d](imag_base)
                at = 2 * SITES * out_colour
                for p in range(4):
                    cosine = table_ref[d, p : p + 1, :]
                    sine = table_ref[d, p + 4 : p + 5, :]
                    left_ref[4 * d + p, rows, at : at + SITES] = (
                        real_base * cosine + imag_base * sine
                    ).astype(jnp.bfloat16)
                    left_ref[4 * d + p, rows, at + SITES : at + 2 * SITES] = (
                        imag_base * cosine - real_base * sine
                    ).astype(jnp.bfloat16)
        return carry

    lax.fori_loop(0, ROWS // 16, rows_of, 0)


def left_operand(momenta, height, block, links):
    return pl.pallas_call(
        left_kernel,
        out_shape=jax.ShapeDtypeStruct((12, ROWS, DEPTH), jnp.bfloat16),
        in_specs=[
            pl.BlockSpec(memory_space=pltpu.SMEM),
            pl.BlockSpec(memory_space=pltpu.SMEM),
            pl.BlockSpec(memory_space=pltpu.VMEM),
            pl.BlockSpec(memory_space=pltpu.VMEM),
        ],
        out_specs=pl.BlockSpec(memory_space=pltpu.VMEM),
        scratch_shapes=[pltpu.VMEM((3, 8, SITES), jnp.float32)],
        compiler_params=pltpu.CompilerParams(vmem_limit_bytes=VMEM_BYTES),
    )(momenta, height, block, links)


def product_kernel(half_ref, own_ref, other_ref, right_ref, raised_ref, out_ref, both_ref):
    def spread(source_ref):
        for colour in range(3):
            at = 2 * SITES * colour
            real_vec = source_ref[:, at : at + SITES]
            imag_vec = source_ref[:, at + SITES : at + 2 * SITES]
            both_ref[0:128, at : at + SITES] = real_vec
            both_ref[0:128, at + SITES : at + 2 * SITES] = -imag_vec
            both_ref[128:256, at : at + SITES] = imag_vec
            both_ref[128:256, at + SITES : at + 2 * SITES] = real_vec

    def multiply(left_ref, half, least, most):
        product = lax.dot_general(
            both_ref[...],
            left_ref[least:most, :],
            (((1,), (1,)), ((), ())),
            preferred_element_type=jnp.float32,
        )
        width = most - least
        real_part = product[0:128].reshape(16, 8, width)
        imag_part = product[128:256].reshape(16, 8, width)
        upper = lax.broadcasted_iota(jnp.int32, (16, 8, width), 1) < 4
        even = jnp.where(upper, real_part, pltpu.roll(imag_part, 4, 1)).astype(jnp.bfloat16)
        odd = jnp.where(upper, pltpu.roll(real_part, 4, 1), imag_part).astype(jnp.bfloat16)
        for block in range(4):
            for pair in range(4):
                out_ref[block, half, 2 * pair, :, least:most] = even[4 * block + pair]
                out_ref[block, half, 2 * pair + 1, :, least:most] = odd[4 * block + pair]

    half = half_ref[0]
    spread(right_ref)
    multiply(own_ref, half, 0, 256)
    multiply(other_ref, 1 - half, 0, 256)
    spread(raised_ref)
    multiply(own_ref, half, 256, 384)
    multiply(other_ref, 1 - half, 256, 384)


def products(half, own, other, right, raised):
    return pl.pallas_call(
        product_kernel,
        out_shape=jax.ShapeDtypeStruct((4, 2, 8, 8, 12 * ROWS), jnp.bfloat16),
        in_specs=[pl.BlockSpec(memory_space=pltpu.SMEM)]
        + [pl.BlockSpec(memory_space=pltpu.VMEM)] * 4,
        out_specs=pl.BlockSpec(memory_space=pltpu.VMEM),
        scratch_shapes=[pltpu.VMEM((256, DEPTH), jnp.bfloat16)],
        compiler_params=pltpu.CompilerParams(vmem_limit_bytes=VMEM_BYTES),
    )(half, own, other, right, raised)


def body(eigenvectors, gauge_links, momenta):
    space = lax.axis_size("space")
    eig = lax.axis_size("eig")
    s = lax.axis_index("space")
    zh = lax.axis_index("eig") % 2
    block = eigenvectors.reshape(ROWS, DEPTH)
    links = gauge_links.reshape(3, 3, 3, 2, SITES)
    height = jnp.stack([s, jnp.int32(space)]).astype(jnp.int32)
    half = zh.astype(jnp.int32).reshape(1)

    partner = lax.ppermute(block, "eig", [(a, a ^ 1) for a in range(eig)])
    right = lax.all_to_all(
        jnp.broadcast_to(block[None], (eig // 2, ROWS, DEPTH)),
        "eig",
        split_axis=0,
        concat_axis=0,
        axis_index_groups=[list(range(0, eig, 2)), list(range(1, eig, 2))],
        tiled=True,
    ).reshape(eig // 2 * ROWS, DEPTH)
    raised = lax.ppermute(right, "space", [((a + 1) % space, a) for a in range(space)])

    own = left_operand(momenta, height, block, links).reshape(12 * ROWS, DEPTH)
    other = left_operand(momenta, height, partner, links).reshape(12 * ROWS, DEPTH)
    chunks = products(half, own, other, right, raised).reshape(space, 8, 12 * ROWS)
    got = lax.all_to_all(chunks, "space", split_axis=0, concat_axis=0, tiled=True)
    total = jnp.sum(got.astype(jnp.float32), axis=0)

    pairs = []
    for a in range(space):
        for b in range(eig):
            if (a // 8) % 2 != b % 2:
                pairs.append((a * eig + b, (a ^ 8) * eig + (b ^ 1)))
    swapped = lax.ppermute(total, ("space", "eig"), pairs)
    final = jnp.where((s // 8) % 2 == zh, total, swapped)
    return final.reshape(2, 4, 3, 4, ROWS).transpose(2, 3, 0, 4, 1)


def solution(mesh):
    return jax.shard_map(
        body,
        mesh=mesh,
        in_specs=(
            P("eig", None, None, "space", None),
            P(None, None, None, None, "space", None),
            P(),
        ),
        out_specs=P(None, None, None, "eig", "space"),
        check_vma=False,
    )
```

time: 723 us -> 88.2 us (0.12)
  the two profiles are of different devices: /device:TPU:1 before, /device:TPU:8 now
where the time goes in v1:
time: 88.2 us; the launch traced here: 88 us
  blocking collectives  40.6 us (46%)
  waiting for transfers between devices  22.4 us (25%)
  starting transfers between devices  16.8 us (19%)
  Pallas kernels  5.9 us (7%)
  local copies, waits for them, and re-layouts  1.94 us (2%)
    all_to_all x1, blocking collectives, body(): lax.all_to_all(chunks, 'space', split_axis=0, concat_axis=0, tiled=True)  24.2 us
    all_to_all x1, blocking collectives, body(): lax.all_to_all(jnp.broadcast_to(block[None], (eig // 2, ROWS, DEPTH)), 'e...  16.4 us
    ppermute x1, waiting for transfers between devices, body(): partner = lax.ppermute(block, 'eig', [(a, a ^ 1) for a in range(eig)])  14.6 us
    ppermute x1, starting transfers between devices, body(): partner = lax.ppermute(block, 'eig', [(a, a ^ 1) for a in range(eig)])  8.22 us
    ppermute x1, waiting for transfers between devices, body(): swapped = lax.ppermute(total, ('space', 'eig'), pairs)  7.76 us
    ppermute x1, starting transfers between devices, body(): lax.ppermute(right, 'space', [((a + 1) % space, a) for a in range(space)])  6.02 us
    pallas_call x2, Pallas kernels, left_operand(): pl.pallas_call(left_kernel, out_shape=jax.ShapeDtypeStruct((12, ROWS, DEP...  4.04 us
    ppermute x1, starting transfers between devices, body(): swapped = lax.ppermute(total, ('space', 'eig'), pairs)  2.6 us
  transfers between devices with their start and end apart: 3, of which 2 were waited for; matrix products, arithmetic and copies ran while one was open for 0% of the time, Pallas kernels for 5%

profile of v1, /device:TPU:8, one launch (start us, length us, event | category | flops | bytes accessed | tf_op | source)
XLA Modules:
  0.0 88.0 jit_solution(9141616288889912557)
XLA Ops:
  0.0 0.0 copy-start.1
  0.0 0.0 copy-start
  0.0 1.1 %reshape.26.block_ref = bf16[32,3072]{1,0:T(8,128)(2,1)S(1)} reshape(bf16[32,3,2,1,512]{4,2,3,1,0:T(2,128)(2,1)} %param.3) | data formatting | bytes 393216 | tf_op jit(solution)/shard_map/reshape | solution.py:155
  1.1 0.1 broadcast_in_dim.2
  1.2 16.4 %all_to_all.10 = bf16[4,32,3072]{2,1,0:T(8,128)(2,1)S(1)} all-to-all(bf16[4,32,3072]{2,1,0:T(8,128)(2,1)S(1)} %broadcast_in_dim.2), channel_id=1, replica_groups={{0,2,4,6},{1,3,5,7},{8,10,12,14},{9,11,13,15},{16,18,20,22},{17,19,21,2..., dimensions={0} | all-to-all | bytes 1572864 | tf_op jit(solution)/shard_map/all_to_all | solution.py:161
  17.6 6.0 %collective-permute-start.1 = (bf16[128,3072]{1,0:T(8,128)(2,1)S(1)}, bf16[128,3072]{1,0:T(8,128)(2,1)S(1)}, u32[]{:S(2)}, u32[]{:S(2)}) collective-permute-start(bf16[128,3072]{1,0:T(8,128)(2,1)S(1)} %bitcast.14), channel_id=1, source_target_pairs={{8,0},{16,8},{24,16},{32,24},{40,32},{48,40},{56,48},{64,56},{72,6... | collective-permute-start | bytes 2359304 | tf_op jit(solution)/shard_map/ppermute | solution.py:169
  23.6 8.2 %collective-permute-start = (bf16[32,3072]{1,0:T(8,128)(2,1)S(1)}, bf16[32,3072]{1,0:T(8,128)(2,1)S(1)}, u32[]{:S(2)}, u32[]{:S(2)}) collective-permute-start(bf16[32,3072]{1,0:T(8,128)(2,1)S(1)} %reshape.26.block_ref), channel_id=1, source_target_pairs={{0,1},{1,0},{2,3},{3,2},{4,5},{5,4},{6,7},{7,6},{8,9},{9,8},{10,11... | collective-permute-start | bytes 589832 | tf_op jit(solution)/shard_map/ppermute | solution.py:160
  31.8 0.0 copy-done.1
  31.8 0.1 copy.7
  31.9 0.1 pad_add_fusion.height_ref
  32.0 0.0 copy-done
  32.0 2.0 %shard_map.37 = bf16[12,32,3072]{2,1,0:T(8,128)(2,1)S(1)} custom-call(s32[4,3]{1,0:T(4,128)S(1)} %copy-done, s32[2]{0:T(128)S(1)} %pad_add_fusion.height_ref, bf16[32,3072]{1,0:T(8,128)(2,1)S(1)} %reshape.26.block_ref, f32[3,3,3,2,512]{4,3,2,1,0:T(2,128)S(1)} %bitcast.17), custom_call_target="tpu_custom_call" | custom-call | tf_op jit(solution)/shard_map/pallas_call | solution.py:85
  34.0 14.6 %collective-permute-done.block_ref = bf16[32,3072]{1,0:T(8,128)(2,1)S(1)} collective-permute-done((bf16[32,3072]{1,0:T(8,128)(2,1)S(1)}, bf16[32,3072]{1,0:T(8,128)(2,1)S(1)}, u32[]{:S(2)}, u32[]{:S(2)}) %collective-permute-start) | collective-permute-done | bytes 196640 | tf_op jit(solution)/shard_map/ppermute | solution.py:160
  48.6 2.0 %shard_map.38 = bf16[12,32,3072]{2,1,0:T(8,128)(2,1)S(1)} custom-call(s32[4,3]{1,0:T(4,128)S(1)} %copy-done, s32[2]{0:T(128)S(1)} %pad_add_fusion.height_ref, bf16[32,3072]{1,0:T(8,128)(2,1)S(1)} %collective-permute-done.block_ref, f32[3,3,3,2,512]{4,3,2,1,0:T(2,128)S(1)} %bitcast.18), custom_call_target="tpu_custom_call" | custom-call | tf_op jit(solution)/shard_map/pallas_call | solution.py:85
  50.7 0.0 collective-permute-done.1.raised_ref
  50.7 1.9 %shard_map.39 = bf16[4,2,8,8,384]{4,3,2,1,0:T(8,128)(2,1)S(1)} custom-call(s32[1]{0:T(128)} %bitcast.half_ref, bf16[384,3072]{1,0:T(8,128)(2,1)S(1)} %bitcast.12, bf16[384,3072]{1,0:T(8,128)(2,1)S(1)} %bitcast.13, bf16[128,3072]{1,0:T(8,128)(2,1)S(1)} %bitcast.15, bf16[128,3072]{1,0:T(8,128)(2,1)S(1)} %collective-permute-done.1.raised_ref), custom_call_target="tpu_custom_call" | custom-call | tf_op jit(solution)/shard_map/pallas_call | solution.py:139
  52.5 24.2 %all_to_all.11 = bf16[64,8,384]{2,1,0:T(8,128)(2,1)S(1)} all-to-all(bf16[64,8,384]{2,1,0:T(8,128)(2,1)S(1)} %bitcast.16), channel_id=1, replica_groups=mesh['space'=64,'eig'=8] {'space'}, dimensions={0} | all-to-all | bytes 786432 | tf_op jit(solution)/shard_map/all_to_all | solution.py:174
  76.8 0.1 convert_reduce_fusion
  76.8 2.6 %collective-permute-start.2 = (f32[8,384]{1,0:T(8,128)S(1)}, f32[8,384]{1,0:T(8,128)S(1)}, u32[]{:S(2)}, u32[]{:S(2)}) collective-permute-start(f32[8,384]{1,0:T(8,128)S(1)} %convert_reduce_fusion), channel_id=1, source_target_pairs={{1,64},{3,66},{5,68},{7,70},{9,72},{11,74},{13,76},{15,78},{17,80}... | collective-permute-start | bytes 36872 | tf_op jit(solution)/shard_map/ppermute | solution.py:182
  79.5 7.8 %collective-permute-done.2 = f32[8,384]{1,0:T(8,128)S(1)} collective-permute-done((f32[8,384]{1,0:T(8,128)S(1)}, f32[8,384]{1,0:T(8,128)S(1)}, u32[]{:S(2)}, u32[]{:S(2)}) %collective-permute-start.2) | collective-permute-done | bytes 12320 | tf_op jit(solution)/shard_map/ppermute | solution.py:182
  87.2 0.1 reshape.32
  87.3 0.6 copy.4
  (1 shorter events, 0.0 us)
Async XLA Ops:
  0.0 31.8 %copy-start.1 = (f32[3,3,3,2,1,512]{5,4,3,2,1,0:T(1,128)S(1)}, f32[3,3,3,2,1,512]{5,4,3,2,1,0:T(1,128)}, u32[]{:S(2)}) copy-start(f32[3,3,3,2,1,512]{5,4,3,2,1,0:T(1,128)} %param.4) | copy-start | bytes 331780
  0.0 32.0 %copy-start = (s32[4,3]{1,0:T(4,128)S(1)}, s32[4,3]{1,0:T(4,128)}, u32[]{:S(2)}) copy-start(s32[4,3]{1,0:T(4,128)} %momenta_ref.3) | copy-start | bytes 148
  17.6 33.1 %collective-permute-start.1 = (bf16[128,3072]{1,0:T(8,128)(2,1)S(1)}, bf16[128,3072]{1,0:T(8,128)(2,1)S(1)}, u32[]{:S(2)}, u32[]{:S(2)}) collective-permute-start(bf16[128,3072]{1,0:T(8,128)(2,1)S(1)} %bitcast.14), channel_id=1, source_target_pairs={{8,0},{16,8},{24,16},{32,24},{40,32},{48,40},{56,48},{64,56},{72,6... | collective-permute-start | bytes 2359304 | tf_op jit(solution)/shard_map/ppermute | solution.py:169
  23.6 25.0 %collective-permute-start = (bf16[32,3072]{1,0:T(8,128)(2,1)S(1)}, bf16[32,3072]{1,0:T(8,128)(2,1)S(1)}, u32[]{:S(2)}, u32[]{:S(2)}) collective-permute-start(bf16[32,3072]{1,0:T(8,128)(2,1)S(1)} %reshape.26.block_ref), channel_id=1, source_target_pairs={{0,1},{1,0},{2,3},{3,2},{4,5},{5,4},{6,7},{7,6},{8,9},{9,8},{10,11... | collective-permute-start | bytes 589832 | tf_op jit(solution)/shard_map/ppermute | solution.py:160
  76.8 10.4 %collective-permute-start.2 = (f32[8,384]{1,0:T(8,128)S(1)}, f32[8,384]{1,0:T(8,128)S(1)}, u32[]{:S(2)}, u32[]{:S(2)}) collective-permute-start(f32[8,384]{1,0:T(8,128)S(1)} %convert_reduce_fusion), channel_id=1, source_target_pairs={{1,64},{3,66},{5,68},{7,70},{9,72},{11,74},{13,76},{15,78},{17,80}... | collective-permute-start | bytes 36872 | tf_op jit(solution)/shard_map/ppermute | solution.py:182

commit v2 on v1

--- a/solution.py
+++ b/solution.py
@@ -158,14 +158,13 @@
     half = zh.astype(jnp.int32).reshape(1)
 
     partner = lax.ppermute(block, "eig", [(a, a ^ 1) for a in range(eig)])
-    right = lax.all_to_all(
-        jnp.broadcast_to(block[None], (eig // 2, ROWS, DEPTH)),
+    right = lax.all_gather(
+        block,
         "eig",
-        split_axis=0,
-        concat_axis=0,
         axis_index_groups=[list(range(0, eig, 2)), list(range(1, eig, 2))],
         tiled=True,
-    ).reshape(eig // 2 * ROWS, DEPTH)
+    )
+    right, partner = lax.optimization_barrier((right, partner))
     raised = lax.ppermute(right, "space", [((a + 1) % space, a) for a in range(space)])
 
     own = left_operand(momenta, height, block, links).reshape(12 * ROWS, DEPTH)

time: 88.2 us -> 78.2 us (0.89)
  waiting for transfers between devices: 22.4 us -> 11.8 us
  local copies, waits for them, and re-layouts: 1.94 us -> 3.41 us
    all_to_all x1 -> x0, blocking collectives: 16.4 us -> none  [body(): lax.all_to_all(jnp.broadcast_to(block[None], (eig // 2, ROWS, DEPTH)), 'e...]
    ppermute x1, waiting for transfers between devices: 14.6 us -> 0.01 us  [body(): partner = lax.ppermute(block, 'eig', [(a, a ^ 1) for a in range(eig)])]
    all_gather x0 -> x1, blocking collectives: none -> 13.7 us  [body(): lax.all_gather(block, 'eig', axis_index_groups=[list(range(0, eig, 2)), l...]
    ppermute x1, waiting for transfers between devices: 0.01 us -> 3.69 us  [body(): lax.ppermute(right, 'space', [((a + 1) % space, a) for a in range(space)])]
    ppermute x1, starting transfers between devices: 6.02 us -> 2.95 us  [body(): lax.ppermute(right, 'space', [((a + 1) % space, a) for a in range(space)])]
    ppermute x1, starting transfers between devices: 8.22 us -> 10.9 us  [body(): partner = lax.ppermute(block, 'eig', [(a, a ^ 1) for a in range(eig)])]
    all_to_all x1, blocking collectives: 24.2 us -> 26.7 us  [body(): lax.all_to_all(chunks, 'space', split_axis=0, concat_axis=0, tiled=True)]
    unnamed x5 -> x3, local copies, waits for them, and re-layouts: 0.07 us -> 1.64 us
  transfers between devices with their start and end apart: 3 -> 3, of which waited for: 2 -> 2; matrix products, arithmetic and copies ran while one was open for 0% -> 1% of each run, Pallas kernels for 5% -> 5%
where the time goes in v2:
time: 78.2 us; the launch traced here: 77.9 us
  blocking collectives  40.4 us (52%)
  starting transfers between devices  16.1 us (21%)
  waiting for transfers between devices  11.8 us (15%)
  Pallas kernels  5.89 us (8%)
  local copies, waits for them, and re-layouts  3.41 us (4%)
    all_to_all x1, blocking collectives, body(): lax.all_to_all(chunks, 'space', split_axis=0, concat_axis=0, tiled=True)  26.7 us
    all_gather x1, blocking collectives, body(): lax.all_gather(block, 'eig', axis_index_groups=[list(range(0, eig, 2)), l...  13.7 us
    ppermute x1, starting transfers between devices, body(): partner = lax.ppermute(block, 'eig', [(a, a ^ 1) for a in range(eig)])  10.9 us
    ppermute x1, waiting for transfers between devices, body(): swapped = lax.ppermute(total, ('space', 'eig'), pairs)  8.08 us
    pallas_call x2, Pallas kernels, left_operand(): pl.pallas_call(left_kernel, out_shape=jax.ShapeDtypeStruct((12, ROWS, DEP...  4.04 us
    ppermute x1, waiting for transfers between devices, body(): lax.ppermute(right, 'space', [((a + 1) % space, a) for a in range(space)])  3.69 us
    ppermute x1, starting transfers between devices, body(): lax.ppermute(right, 'space', [((a + 1) % space, a) for a in range(space)])  2.95 us
    ppermute x1, starting transfers between devices, body(): swapped = lax.ppermute(total, ('space', 'eig'), pairs)  2.27 us
  transfers between devices with their start and end apart: 3, of which 2 were waited for; matrix products, arithmetic and copies ran while one was open for 1% of the time, Pallas kernels for 5%

profile of v2, /device:TPU:8, one launch (start us, length us, event | category | flops | bytes accessed | tf_op | source)
XLA Modules:
  0.0 77.9 jit_solution(13599120924362833935)
XLA Ops:
  0.0 1.1 %reshape.22.block_ref = bf16[32,3072]{1,0:T(8,128)(2,1)S(1)} reshape(bf16[32,3,2,1,512]{4,2,3,1,0:T(2,128)(2,1)} %param.3) | data formatting | bytes 393216 | tf_op jit(solution)/shard_map/reshape | solution.py:155
  1.1 10.9 %collective-permute-start = (bf16[32,3072]{1,0:T(8,128)(2,1)S(1)}, bf16[32,3072]{1,0:T(8,128)(2,1)S(1)}, u32[]{:S(2)}, u32[]{:S(2)}) collective-permute-start(bf16[32,3072]{1,0:T(8,128)(2,1)S(1)} %reshape.22.block_ref), channel_id=1, source_target_pairs={{0,1},{1,0},{2,3},{3,2},{4,5},{5,4},{6,7},{7,6},{8,9},{9,8},{10,11... | collective-permute-start | bytes 589832 | tf_op jit(solution)/shard_map/ppermute | solution.py:160
  12.0 13.7 %all_gather.3.right_ref = bf16[128,3072]{1,0:T(8,128)(2,1)S(1)} all-gather(bf16[32,3072]{1,0:T(8,128)(2,1)S(1)} %reshape.22.block_ref), channel_id=1, replica_groups={{0,2,4,6},{1,3,5,7},{8,10,12,14},{9,11,13,15},{16,18,20,22},{17,19,21,2..., dimensions={0}, use_global_device_ids=true | all-gather | bytes 983040 | tf_op jit(solution)/shard_map/all_gather | solution.py:161
  25.6 0.0 collective-permute-done.block_ref
  25.6 2.9 %collective-permute-start.1 = (bf16[128,3072]{1,0:T(8,128)(2,1)S(1)}, bf16[128,3072]{1,0:T(8,128)(2,1)S(1)}, u32[]{:S(2)}, u32[]{:S(2)}) collective-permute-start(bf16[128,3072]{1,0:T(8,128)(2,1)S(1)} %all_gather.3.right_ref), channel_id=1, source_target_pairs={{8,0},{16,8},{24,16},{32,24},{40,32},{48,40},{56,48},{64,56},{72,6... | collective-permute-start | bytes 2359304 | tf_op jit(solution)/shard_map/ppermute | solution.py:168
  28.6 1.0 %copy.7 = f32[3,3,3,2,1,512]{5,3,4,2,1,0:T(2,128)S(1)} copy(f32[3,3,3,2,1,512]{5,4,3,2,1,0:T(1,128)} %param.4) | data formatting | bytes 221184
  29.6 0.1 pad_add_fusion.height_ref
  29.7 0.0 copy-start
  29.7 0.7 copy-done
  30.3 2.0 %shard_map.37 = bf16[12,32,3072]{2,1,0:T(8,128)(2,1)S(1)} custom-call(s32[4,3]{1,0:T(4,128)S(1)} %copy-done, s32[2]{0:T(128)S(1)} %pad_add_fusion.height_ref, bf16[32,3072]{1,0:T(8,128)(2,1)S(1)} %reshape.22.block_ref, f32[3,3,3,2,512]{4,3,2,1,0:T(2,128)S(1)} %bitcast.14), custom_call_target="tpu_custom_call" | custom-call | tf_op jit(solution)/shard_map/pallas_call | solution.py:85
  32.3 2.0 %shard_map.38 = bf16[12,32,3072]{2,1,0:T(8,128)(2,1)S(1)} custom-call(s32[4,3]{1,0:T(4,128)S(1)} %copy-done, s32[2]{0:T(128)S(1)} %pad_add_fusion.height_ref, bf16[32,3072]{1,0:T(8,128)(2,1)S(1)} %collective-permute-done.block_ref, f32[3,3,3,2,512]{4,3,2,1,0:T(2,128)S(1)} %bitcast.15), custom_call_target="tpu_custom_call" | custom-call | tf_op jit(solution)/shard_map/pallas_call | solution.py:85
  34.4 3.7 %collective-permute-done.1.raised_ref = bf16[128,3072]{1,0:T(8,128)(2,1)S(1)} collective-permute-done((bf16[128,3072]{1,0:T(8,128)(2,1)S(1)}, bf16[128,3072]{1,0:T(8,128)(2,1)S(1)}, u32[]{:S(2)}, u32[]{:S(2)}) %collective-permute-start.1) | collective-permute-done | bytes 786464 | tf_op jit(solution)/shard_map/ppermute | solution.py:168
  38.1 1.9 %shard_map.39 = bf16[4,2,8,8,384]{4,3,2,1,0:T(8,128)(2,1)S(1)} custom-call(s32[1]{0:T(128)} %bitcast.half_ref, bf16[384,3072]{1,0:T(8,128)(2,1)S(1)} %bitcast.11, bf16[384,3072]{1,0:T(8,128)(2,1)S(1)} %bitcast.12, bf16[128,3072]{1,0:T(8,128)(2,1)S(1)} %all_gather.3.right_ref, bf16[128,3072]{1,0:T(8,128)(2,1)S(1)} %collective-permute-done.1.raised_ref), custom_call_target="tpu_custom_call" | custom-call | tf_op jit(solution)/shard_map/pallas_call | solution.py:139
  39.9 26.7 %all_to_all.5 = bf16[64,8,384]{2,1,0:T(8,128)(2,1)S(1)} all-to-all(bf16[64,8,384]{2,1,0:T(8,128)(2,1)S(1)} %bitcast.13), channel_id=1, replica_groups=mesh['space'=64,'eig'=8] {'space'}, dimensions={0} | all-to-all | bytes 786432 | tf_op jit(solution)/shard_map/all_to_all | solution.py:173
  66.7 0.1 convert_reduce_fusion
  66.8 2.3 %collective-permute-start.2 = (f32[8,384]{1,0:T(8,128)S(1)}, f32[8,384]{1,0:T(8,128)S(1)}, u32[]{:S(2)}, u32[]{:S(2)}) collective-permute-start(f32[8,384]{1,0:T(8,128)S(1)} %convert_reduce_fusion), channel_id=1, source_target_pairs={{1,64},{3,66},{5,68},{7,70},{9,72},{11,74},{13,76},{15,78},{17,80}... | collective-permute-start | bytes 36872 | tf_op jit(solution)/shard_map/ppermute | solution.py:181
  69.1 8.1 %collective-permute-done.2 = f32[8,384]{1,0:T(8,128)S(1)} collective-permute-done((f32[8,384]{1,0:T(8,128)S(1)}, f32[8,384]{1,0:T(8,128)S(1)}, u32[]{:S(2)}, u32[]{:S(2)}) %collective-permute-start.2) | collective-permute-done | bytes 12320 | tf_op jit(solution)/shard_map/ppermute | solution.py:181
  77.2 0.1 reshape.27
  77.3 0.6 copy.4
  (1 shorter events, 0.0 us)
Async XLA Ops:
  1.1 24.6 %collective-permute-start = (bf16[32,3072]{1,0:T(8,128)(2,1)S(1)}, bf16[32,3072]{1,0:T(8,128)(2,1)S(1)}, u32[]{:S(2)}, u32[]{:S(2)}) collective-permute-start(bf16[32,3072]{1,0:T(8,128)(2,1)S(1)} %reshape.22.block_ref), channel_id=1, source_target_pairs={{0,1},{1,0},{2,3},{3,2},{4,5},{5,4},{6,7},{7,6},{8,9},{9,8},{10,11... | collective-permute-start | bytes 589832 | tf_op jit(solution)/shard_map/ppermute | solution.py:160
  25.6 12.4 %collective-permute-start.1 = (bf16[128,3072]{1,0:T(8,128)(2,1)S(1)}, bf16[128,3072]{1,0:T(8,128)(2,1)S(1)}, u32[]{:S(2)}, u32[]{:S(2)}) collective-permute-start(bf16[128,3072]{1,0:T(8,128)(2,1)S(1)} %all_gather.3.right_ref), channel_id=1, source_target_pairs={{8,0},{16,8},{24,16},{32,24},{40,32},{48,40},{56,48},{64,56},{72,6... | collective-permute-start | bytes 2359304 | tf_op jit(solution)/shard_map/ppermute | solution.py:168
  29.7 0.7 copy-start
  66.8 10.4 %collective-permute-start.2 = (f32[8,384]{1,0:T(8,128)S(1)}, f32[8,384]{1,0:T(8,128)S(1)}, u32[]{:S(2)}, u32[]{:S(2)}) collective-permute-start(f32[8,384]{1,0:T(8,128)S(1)} %convert_reduce_fusion), channel_id=1, source_target_pairs={{1,64},{3,66},{5,68},{7,70},{9,72},{11,74},{13,76},{15,78},{17,80}... | collective-permute-start | bytes 36872 | tf_op jit(solution)/shard_map/ppermute | solution.py:181

commit v3 on v2

--- a/solution.py
+++ b/solution.py
@@ -123,8 +123,8 @@
         odd = jnp.where(upper, pltpu.roll(real_part, 4, 1), imag_part).astype(jnp.bfloat16)
         for block in range(4):
             for pair in range(4):
-                out_ref[block, half, 2 * pair, :, least:most] = even[4 * block + pair]
-                out_ref[block, half, 2 * pair + 1, :, least:most] = odd[4 * block + pair]
+                out_ref[2 * pair, block, half, :, least:most] = even[4 * block + pair]
+                out_ref[2 * pair + 1, block, half, :, least:most] = odd[4 * block + pair]
 
     half = half_ref[0]
     spread(right_ref)
@@ -138,7 +138,7 @@
 def products(half, own, other, right, raised):
     return pl.pallas_call(
         product_kernel,
-        out_shape=jax.ShapeDtypeStruct((4, 2, 8, 8, 12 * ROWS), jnp.bfloat16),
+        out_shape=jax.ShapeDtypeStruct((8, 4, 2, 8, 12 * ROWS), jnp.bfloat16),
         in_specs=[pl.BlockSpec(memory_space=pltpu.SMEM)]
         + [pl.BlockSpec(memory_space=pltpu.VMEM)] * 4,
         out_specs=pl.BlockSpec(memory_space=pltpu.VMEM),
@@ -169,9 +169,18 @@
 
     own = left_operand(momenta, height, block, links).reshape(12 * ROWS, DEPTH)
     other = left_operand(momenta, height, partner, links).reshape(12 * ROWS, DEPTH)
-    chunks = products(half, own, other, right, raised).reshape(space, 8, 12 * ROWS)
-    got = lax.all_to_all(chunks, "space", split_axis=0, concat_axis=0, tiled=True)
-    total = jnp.sum(got.astype(jnp.float32), axis=0)
+    chunks = products(half, own, other, right, raised)
+    near = [list(range(start, start + 8)) for start in range(0, space, 8)]
+    far = [list(range(start, space, 8)) for start in range(8)]
+    chunks = chunks.reshape(8, 64, 12 * ROWS)
+    got = lax.all_to_all(
+        chunks, "space", split_axis=0, concat_axis=0, axis_index_groups=near, tiled=True
+    )
+    sums = jnp.sum(got.astype(jnp.float32), axis=0).reshape(space // 8, 8, 12 * ROWS)
+    got = lax.all_to_all(
+        sums, "space", split_axis=0, concat_axis=0, axis_index_groups=far, tiled=True
+    )
+    total = jnp.sum(got, axis=0)
 
     pairs = []
     for a in range(space):

time: 78.2 us -> 84.4 us (1.079)
  blocking collectives: 40.4 us -> 46.6 us
  starting transfers between devices: 16.1 us -> 17 us
    all_to_all x1 -> x2, blocking collectives: 26.7 us -> 33 us  [the longest x1 18.3 us: body(): lax.all_to_all(chunks, 'space', split_axis=0, concat_axis=0, axis_index_g...]
where the time goes in v3:
time: 84.4 us; the launch traced here: 84.1 us
  blocking collectives  46.6 us (55%)
  starting transfers between devices  17 us (20%)
  waiting for transfers between devices  11 us (13%)
  Pallas kernels  5.9 us (7%)
  local copies, waits for them, and re-layouts  3.41 us (4%)
    all_to_all x1, blocking collectives, body(): lax.all_to_all(chunks, 'space', split_axis=0, concat_axis=0, axis_index_g...  18.3 us
    all_to_all x1, blocking collectives, body(): lax.all_to_all(sums, 'space', split_axis=0, concat_axis=0, axis_index_gro...  14.6 us
    all_gather x1, blocking collectives, body(): lax.all_gather(block, 'eig', axis_index_groups=[list(range(0, eig, 2)), l...  13.7 us
    ppermute x1, starting transfers between devices, body(): partner = lax.ppermute(block, 'eig', [(a, a ^ 1) for a in range(eig)])  10.9 us
    ppermute x1, waiting for transfers between devices, body(): swapped = lax.ppermute(total, ('space', 'eig'), pairs)  7.27 us
    pallas_call x2, Pallas kernels, left_operand(): pl.pallas_call(left_kernel, out_shape=jax.ShapeDtypeStruct((12, ROWS, DEP...  4.04 us
    ppermute x1, waiting for transfers between devices, body(): lax.ppermute(right, 'space', [((a + 1) % space, a) for a in range(space)])  3.69 us
    ppermute x1, starting transfers between devices, body(): swapped = lax.ppermute(total, ('space', 'eig'), pairs)  3.09 us
  transfers between devices with their start and end apart: 3, of which 2 were waited for; matrix products, arithmetic and copies ran while one was open for 1% of the time, Pallas kernels for 5%

profile of v3, /device:TPU:8, one launch (start us, length us, event | category | flops | bytes accessed | tf_op | source)
XLA Modules:
  0.0 84.1 jit_solution(16433798752916833591)
XLA Ops:
  0.0 1.1 %reshape.25.block_ref = bf16[32,3072]{1,0:T(8,128)(2,1)S(1)} reshape(bf16[32,3,2,1,512]{4,2,3,1,0:T(2,128)(2,1)} %param.3) | data formatting | bytes 393216 | tf_op jit(solution)/shard_map/reshape | solution.py:155
  1.1 10.9 %collective-permute-start = (bf16[32,3072]{1,0:T(8,128)(2,1)S(1)}, bf16[32,3072]{1,0:T(8,128)(2,1)S(1)}, u32[]{:S(2)}, u32[]{:S(2)}) collective-permute-start(bf16[32,3072]{1,0:T(8,128)(2,1)S(1)} %reshape.25.block_ref), channel_id=1, source_target_pairs={{0,1},{1,0},{2,3},{3,2},{4,5},{5,4},{6,7},{7,6},{8,9},{9,8},{10,11... | collective-permute-start | bytes 589832 | tf_op jit(solution)/shard_map/ppermute | solution.py:160
  12.0 13.7 %all_gather.3.right_ref = bf16[128,3072]{1,0:T(8,128)(2,1)S(1)} all-gather(bf16[32,3072]{1,0:T(8,128)(2,1)S(1)} %reshape.25.block_ref), channel_id=1, replica_groups={{0,2,4,6},{1,3,5,7},{8,10,12,14},{9,11,13,15},{16,18,20,22},{17,19,21,2..., dimensions={0}, use_global_device_ids=true | all-gather | bytes 983040 | tf_op jit(solution)/shard_map/all_gather | solution.py:161
  25.6 0.0 collective-permute-done.block_ref
  25.6 2.9 %collective-permute-start.1 = (bf16[128,3072]{1,0:T(8,128)(2,1)S(1)}, bf16[128,3072]{1,0:T(8,128)(2,1)S(1)}, u32[]{:S(2)}, u32[]{:S(2)}) collective-permute-start(bf16[128,3072]{1,0:T(8,128)(2,1)S(1)} %all_gather.3.right_ref), channel_id=1, source_target_pairs={{8,0},{16,8},{24,16},{32,24},{40,32},{48,40},{56,48},{64,56},{72,6... | collective-permute-start | bytes 2359304 | tf_op jit(solution)/shard_map/ppermute | solution.py:168
  28.6 1.0 %copy.8 = f32[3,3,3,2,1,512]{5,3,4,2,1,0:T(2,128)S(1)} copy(f32[3,3,3,2,1,512]{5,4,3,2,1,0:T(1,128)} %param.4) | data formatting | bytes 221184
  29.6 0.1 pad_add_fusion.height_ref
  29.7 0.0 copy-start
  29.7 0.7 copy-done
  30.3 2.0 %shard_map.37 = bf16[12,32,3072]{2,1,0:T(8,128)(2,1)S(1)} custom-call(s32[4,3]{1,0:T(4,128)S(1)} %copy-done, s32[2]{0:T(128)S(1)} %pad_add_fusion.height_ref, bf16[32,3072]{1,0:T(8,128)(2,1)S(1)} %reshape.25.block_ref, f32[3,3,3,2,512]{4,3,2,1,0:T(2,128)S(1)} %bitcast.15), custom_call_target="tpu_custom_call" | custom-call | tf_op jit(solution)/shard_map/pallas_call | solution.py:85
  32.3 2.0 %shard_map.38 = bf16[12,32,3072]{2,1,0:T(8,128)(2,1)S(1)} custom-call(s32[4,3]{1,0:T(4,128)S(1)} %copy-done, s32[2]{0:T(128)S(1)} %pad_add_fusion.height_ref, bf16[32,3072]{1,0:T(8,128)(2,1)S(1)} %collective-permute-done.block_ref, f32[3,3,3,2,512]{4,3,2,1,0:T(2,128)S(1)} %bitcast.16), custom_call_target="tpu_custom_call" | custom-call | tf_op jit(solution)/shard_map/pallas_call | solution.py:85
  34.4 3.7 %collective-permute-done.1.raised_ref = bf16[128,3072]{1,0:T(8,128)(2,1)S(1)} collective-permute-done((bf16[128,3072]{1,0:T(8,128)(2,1)S(1)}, bf16[128,3072]{1,0:T(8,128)(2,1)S(1)}, u32[]{:S(2)}, u32[]{:S(2)}) %collective-permute-start.1) | collective-permute-done | bytes 786464 | tf_op jit(solution)/shard_map/ppermute | solution.py:168
  38.1 1.9 %shard_map.39 = bf16[8,4,2,8,384]{4,3,2,1,0:T(8,128)(2,1)S(1)} custom-call(s32[1]{0:T(128)} %bitcast.half_ref, bf16[384,3072]{1,0:T(8,128)(2,1)S(1)} %bitcast.12, bf16[384,3072]{1,0:T(8,128)(2,1)S(1)} %bitcast.13, bf16[128,3072]{1,0:T(8,128)(2,1)S(1)} %all_gather.3.right_ref, bf16[128,3072]{1,0:T(8,128)(2,1)S(1)} %collective-permute-done.1.raised_ref), custom_call_target="tpu_custom_call" | custom-call | tf_op jit(solution)/shard_map/pallas_call | solution.py:139
  40.0 18.3 %all_to_all.10 = bf16[8,64,384]{2,1,0:T(8,128)(2,1)S(1)} all-to-all(bf16[8,64,384]{2,1,0:T(8,128)(2,1)S(1)} %bitcast.14), channel_id=1, replica_groups={{0,8,16,24,32,40,48,56},{64,72,80,88,96,104,112,120},{128,136,144,152,1..., dimensions={0} | all-to-all | bytes 786432 | tf_op jit(solution)/shard_map/all_to_all | solution.py:176
  58.3 0.1 convert_reduce_fusion
  58.4 14.6 %all_to_all.11 = f32[8,8,384]{2,1,0:T(8,128)S(1)} all-to-all(f32[8,8,384]{2,1,0:T(8,128)S(1)} %bitcast.17), channel_id=1, replica_groups={{0,64,128,192,256,320,384,448},{8,72,136,200,264,328,392,456},{16,80,14..., dimensions={0} | all-to-all | bytes 196608 | tf_op jit(solution)/shard_map/all_to_all | solution.py:180
  73.0 3.1 %collective-permute-start.2 = (f32[8,384]{1,0:T(8,128)S(1)}, f32[8,384]{1,0:T(8,128)S(1)}, u32[]{:S(2)}, u32[]{:S(2)}) collective-permute-start(f32[8,384]{1,0:T(8,128)S(1)} %reduce_sum.19), channel_id=1, source_target_pairs={{1,64},{3,66},{5,68},{7,70},{9,72},{11,74},{13,76},{15,78},{17,80}... | collective-permute-start | bytes 36872 | tf_op jit(solution)/shard_map/ppermute | solution.py:190
  76.1 7.3 %collective-permute-done.2 = f32[8,384]{1,0:T(8,128)S(1)} collective-permute-done((f32[8,384]{1,0:T(8,128)S(1)}, f32[8,384]{1,0:T(8,128)S(1)}, u32[]{:S(2)}, u32[]{:S(2)}) %collective-permute-start.2) | collective-permute-done | bytes 12320 | tf_op jit(solution)/shard_map/ppermute | solution.py:190
  83.4 0.1 reshape.31
  83.5 0.6 copy.5
  (2 shorter events, 0.0 us)
Async XLA Ops:
  1.1 24.6 %collective-permute-start = (bf16[32,3072]{1,0:T(8,128)(2,1)S(1)}, bf16[32,3072]{1,0:T(8,128)(2,1)S(1)}, u32[]{:S(2)}, u32[]{:S(2)}) collective-permute-start(bf16[32,3072]{1,0:T(8,128)(2,1)S(1)} %reshape.25.block_ref), channel_id=1, source_target_pairs={{0,1},{1,0},{2,3},{3,2},{4,5},{5,4},{6,7},{7,6},{8,9},{9,8},{10,11... | collective-permute-start | bytes 589832 | tf_op jit(solution)/shard_map/ppermute | solution.py:160
  25.6 12.4 %collective-permute-start.1 = (bf16[128,3072]{1,0:T(8,128)(2,1)S(1)}, bf16[128,3072]{1,0:T(8,128)(2,1)S(1)}, u32[]{:S(2)}, u32[]{:S(2)}) collective-permute-start(bf16[128,3072]{1,0:T(8,128)(2,1)S(1)} %all_gather.3.right_ref), channel_id=1, source_target_pairs={{8,0},{16,8},{24,16},{32,24},{40,32},{48,40},{56,48},{64,56},{72,6... | collective-permute-start | bytes 2359304 | tf_op jit(solution)/shard_map/ppermute | solution.py:168
  29.7 0.7 copy-start
  73.0 10.4 %collective-permute-start.2 = (f32[8,384]{1,0:T(8,128)S(1)}, f32[8,384]{1,0:T(8,128)S(1)}, u32[]{:S(2)}, u32[]{:S(2)}) collective-permute-start(f32[8,384]{1,0:T(8,128)S(1)} %reduce_sum.19), channel_id=1, source_target_pairs={{1,64},{3,66},{5,68},{7,70},{9,72},{11,74},{13,76},{15,78},{17,80}... | collective-permute-start | bytes 36872 | tf_op jit(solution)/shard_map/ppermute | solution.py:190

commit v4 on v2

v4 whole, which is shorter than its diff:
```python
import math

import jax
import jax.numpy as jnp
from jax import lax
from jax.experimental import pallas as pl
from jax.experimental.pallas import tpu as pltpu
from jax.sharding import PartitionSpec as P

LX = 64
LY = 8
SITES = LX * LY
ROWS = 32
DEPTH = 6 * SITES
VMEM_BYTES = 40 * 1024 * 1024


def moved_across(field):
    lane = lax.broadcasted_iota(jnp.int32, field.shape, 1)
    return jnp.where(
        lane % LX == 0, pltpu.roll(field, SITES - LX + 1, 1), pltpu.roll(field, 1, 1)
    )


def moved_along(field):
    return pltpu.roll(field, LX, 1)


MOVES = (moved_across, moved_along, lambda field: field)


def left_kernel(momenta_ref, height_ref, block_ref, below_ref, link_ref, link_below_ref, left_ref, table_ref):
    row = lax.broadcasted_iota(jnp.int32, (8, SITES), 0) % 4
    site = lax.broadcasted_iota(jnp.int32, (8, SITES), 1)

    def component(k):
        value = jnp.full((8, SITES), momenta_ref[3, k], jnp.int32)
        for p in range(3):
            value = jnp.where(row == p, momenta_ref[p, k], value)
        return value

    x_frac = ((component(0) * (site % LX)) & (LX - 1)).astype(jnp.float32) / LX
    y_frac = ((component(1) * (site // LX)) & (LY - 1)).astype(jnp.float32) / LY
    extent = height_ref[1]
    first = lax.broadcasted_iota(jnp.int32, (8, SITES), 0) < 4

    def plane_table(height):
        z_frac = ((component(2) * height) & (extent - 1)).astype(jnp.float32)
        z_frac = z_frac / extent.astype(jnp.float32)
        angles = 2.0 * math.pi * (x_frac + y_frac + z_frac)
        return jnp.where(first, jnp.cos(angles), jnp.sin(angles))

    here = plane_table(height_ref[0])
    table_ref[0] = moved_across(here)
    table_ref[1] = moved_along(here)
    table_ref[2] = plane_table((height_ref[0] - 1) & (extent - 1))

    def rows_of(group, carry):
        rows = pl.ds(pl.multiple_of(group * 16, 16), 16)
        for d in range(3):
            source_ref = below_ref if d == 2 else block_ref
            for out_colour in range(3):
                real_base = jnp.zeros((16, SITES), jnp.float32)
                imag_base = jnp.zeros((16, SITES), jnp.float32)
                for colour in range(3):
                    at = 2 * SITES * colour
                    real_vec = source_ref[rows, at : at + SITES].astype(jnp.float32)
                    imag_vec = source_ref[rows, at + SITES : at + 2 * SITES].astype(jnp.float32)
                    if d == 2:
                        real_link = link_below_ref[colour, out_colour, 0:1, :]
                        imag_link = link_below_ref[colour, out_colour, 1:2, :]
                    else:
                        real_link = link_ref[d, colour, out_colour, 0:1, :]
                        imag_link = link_ref[d, colour, out_colour, 1:2, :]
                    real_base += real_vec * real_link + imag_vec * imag_link
                    imag_base += real_vec * imag_link - imag_vec * real_link
                real_base, imag_base = MOVES[d](real_base), MOVES[d](imag_base)
                at = 2 * SITES * out_colour
                for p in range(4):
                    cosine = table_ref[d, p : p + 1, :]
                    sine = table_ref[d, p + 4 : p + 5, :]
                    left_ref[4 * d + p, rows, at : at + SITES] = (
                        real_base * cosine + imag_base * sine
                    ).astype(jnp.bfloat16)
                    left_ref[4 * d + p, rows, at + SITES : at + 2 * SITES] = (
                        imag_base * cosine - real_base * sine
                    ).astype(jnp.bfloat16)
        return carry

    lax.fori_loop(0, ROWS // 16, rows_of, 0)


def left_operand(momenta, height, block, below, links, link_below):
    return pl.pallas_call(
        left_kernel,
        out_shape=jax.ShapeDtypeStruct((12, ROWS, DEPTH), jnp.bfloat16),
        in_specs=[pl.BlockSpec(memory_space=pltpu.SMEM)] * 2
        + [pl.BlockSpec(memory_space=pltpu.VMEM)] * 4,
        out_specs=pl.BlockSpec(memory_space=pltpu.VMEM),
        scratch_shapes=[pltpu.VMEM((3, 8, SITES), jnp.float32)],
        compiler_params=pltpu.CompilerParams(vmem_limit_bytes=VMEM_BYTES),
    )(momenta, height, block, below, links, link_below)


def product_kernel(half_ref, left_ref, near_ref, far_ref, out_ref, both_ref):
    def spread(source_ref):
        for colour in range(3):
            at = 2 * SITES * colour
            real_vec = source_ref[:, at : at + SITES]
            imag_vec = source_ref[:, at + SITES : at + 2 * SITES]
            both_ref[0:128, at : at + SITES] = real_vec
            both_ref[0:128, at + SITES : at + 2 * SITES] = -imag_vec
            both_ref[128:256, at : at + SITES] = imag_vec
            both_ref[128:256, at + SITES : at + 2 * SITES] = real_vec

    def multiply(half):
        product = lax.dot_general(
            both_ref[...],
            left_ref[...],
            (((1,), (1,)), ((), ())),
            preferred_element_type=jnp.float32,
        )
        width = 12 * ROWS
        real_part = product[0:128].reshape(16, 8, width)
        imag_part = product[128:256].reshape(16, 8, width)
        upper = lax.broadcasted_iota(jnp.int32, (16, 8, width), 1) < 4
        even = jnp.where(upper, real_part, pltpu.roll(imag_part, 4, 1)).astype(jnp.bfloat16)
        odd = jnp.where(upper, pltpu.roll(real_part, 4, 1), imag_part).astype(jnp.bfloat16)
        for block in range(4):
            for pair in range(4):
                out_ref[block, half, 2 * pair] = even[4 * block + pair]
                out_ref[block, half, 2 * pair + 1] = odd[4 * block + pair]

    half = half_ref[0]
    spread(near_ref)
    multiply(half)
    spread(far_ref)
    multiply(1 - half)


def products(half, left, near, far):
    return pl.pallas_call(
        product_kernel,
        out_shape=jax.ShapeDtypeStruct((4, 2, 8, 8, 12 * ROWS), jnp.bfloat16),
        in_specs=[pl.BlockSpec(memory_space=pltpu.SMEM)]
        + [pl.BlockSpec(memory_space=pltpu.VMEM)] * 3,
        out_specs=pl.BlockSpec(memory_space=pltpu.VMEM),
        scratch_shapes=[pltpu.VMEM((256, DEPTH), jnp.bfloat16)],
        compiler_params=pltpu.CompilerParams(vmem_limit_bytes=VMEM_BYTES),
    )(half, left, near, far)


def body(eigenvectors, gauge_links, momenta):
    space = lax.axis_size("space")
    eig = lax.axis_size("eig")
    s = lax.axis_index("space")
    e = lax.axis_index("eig")
    block = eigenvectors.reshape(ROWS, DEPTH)
    links = gauge_links.reshape(3, 3, 3, 2, SITES)
    height = jnp.stack([s, jnp.int32(space)]).astype(jnp.int32)
    half = (e & 1).astype(jnp.int32).reshape(1)

    def from_below(value):
        return lax.ppermute(value, "space", [(a, (a + 1) % space) for a in range(space)])

    def around_x(value):
        groups = [list(range(0, eig, 2)), list(range(1, eig, 2))]
        return lax.all_gather(value, "eig", axis_index_groups=groups, tiled=True)

    partner = lax.ppermute(block, "eig", [(a, a ^ 1) for a in range(eig)])
    near = around_x(block)
    below = from_below(block)
    link_below = from_below(links[2])
    left = left_operand(momenta, height, block, below, links, link_below)
    left = left.reshape(12 * ROWS, DEPTH)

    partner, left, near = lax.optimization_barrier((partner, left, near))
    far = around_x(partner)
    chunks = products(half, left, near, far).reshape(space, 8, 12 * ROWS)
    got = lax.all_to_all(chunks, "space", split_axis=0, concat_axis=0, tiled=True)
    total = jnp.sum(got.astype(jnp.float32), axis=0)
    return total.reshape(2, 4, 3, 4, ROWS).transpose(2, 3, 0, 4, 1)


def solution(mesh):
    return jax.shard_map(
        body,
        mesh=mesh,
        in_specs=(
            P("eig", None, None, "space", None),
            P(None, None, None, None, "space", None),
            P(),
        ),
        out_specs=P(None, None, None, "eig", "space"),
        check_vma=False,
    )
```

time: 78.2 us -> 79 us (1.010)
  the two profiles are of different devices: /device:TPU:8 before, /device:TPU:1 now
where the time goes in v4:
time: 79 us; the launch traced here: 78.7 us
  blocking collectives  53 us (67%)
  starting transfers between devices  17.3 us (22%)
  local copies, waits for them, and re-layouts  4.2 us (5%)
  Pallas kernels  3.86 us (5%)
    all_to_all x1, blocking collectives, body(): lax.all_to_all(chunks, 'space', split_axis=0, concat_axis=0, tiled=True)  30.3 us
    all_gather x2, blocking collectives, around_x(): return lax.all_gather(value, 'eig', axis_index_groups=groups, tiled=True)  22.8 us
    ppermute x1, starting transfers between devices, body(): partner = lax.ppermute(block, 'eig', [(a, a ^ 1) for a in range(eig)])  9.74 us
    ppermute x2, starting transfers between devices, from_below(): lax.ppermute(value, 'space', [(a, (a + 1) % space) for a in range(space)])  7.59 us
    pallas_call x1, Pallas kernels, left_operand(): pl.pallas_call(left_kernel, out_shape=jax.ShapeDtypeStruct((12, ROWS, DEP...  2.05 us
    pallas_call x1, Pallas kernels, products(): pl.pallas_call(product_kernel, out_shape=jax.ShapeDtypeStruct((4, 2, 8, 8...  1.8 us
    unnamed x4, local copies, waits for them, and re-layouts  1.65 us
  transfers between devices with their start and end apart: 3, of which 0 were waited for; matrix products, arithmetic and copies ran while one was open for 2% of the time, Pallas kernels for 3%

profile of v4, /device:TPU:1, one launch (start us, length us, event | category | flops | bytes accessed | tf_op | source)
XLA Modules:
  0.0 78.7 jit_solution(11914677677811154047)
XLA Ops:
  0.0 1.1 %reshape.21.block_ref = bf16[32,3072]{1,0:T(8,128)(2,1)S(1)} reshape(bf16[32,3,2,1,512]{4,2,3,1,0:T(2,128)(2,1)} %param.3) | data formatting | bytes 393216 | tf_op jit(solution)/shard_map/reshape | solution.py:158
  1.1 5.4 %collective-permute-start.1 = (bf16[32,3072]{1,0:T(8,128)(2,1)S(1)}, bf16[32,3072]{1,0:T(8,128)(2,1)S(1)}, u32[]{:S(2)}, u32[]{:S(2)}) collective-permute-start(bf16[32,3072]{1,0:T(8,128)(2,1)S(1)} %reshape.21.block_ref), channel_id=1, source_target_pairs={{0,8},{8,16},{16,24},{24,32},{32,40},{40,48},{48,56},{56,64},{64,7... | collective-permute-start | bytes 589832 | tf_op jit(solution)/shard_map/ppermute | solution.py:164
  6.5 9.7 %collective-permute-start = (bf16[32,3072]{1,0:T(8,128)(2,1)S(1)}, bf16[32,3072]{1,0:T(8,128)(2,1)S(1)}, u32[]{:S(2)}, u32[]{:S(2)}) collective-permute-start(bf16[32,3072]{1,0:T(8,128)(2,1)S(1)} %reshape.21.block_ref), channel_id=1, source_target_pairs={{0,1},{1,0},{2,3},{3,2},{4,5},{5,4},{6,7},{7,6},{8,9},{9,8},{10,11... | collective-permute-start | bytes 589832 | tf_op jit(solution)/shard_map/ppermute | solution.py:170
  16.2 0.8 slice.4
  17.0 2.2 %collective-permute-start.2 = (f32[3,3,2,512]{3,2,1,0:T(2,128)S(1)}, f32[3,3,2,512]{3,2,1,0:T(2,128)S(1)}, u32[]{:S(2)}, u32[]{:S(2)}) collective-permute-start(f32[3,3,2,512]{3,2,1,0:T(2,128)S(1)} %bitcast.17), channel_id=1, source_target_pairs={{0,8},{8,16},{16,24},{24,32},{32,40},{40,48},{48,56},{56,64},{64,7... | collective-permute-start | bytes 110600 | tf_op jit(solution)/shard_map/ppermute | solution.py:164
  19.2 12.0 %all_gather.6.near_ref = bf16[128,3072]{1,0:T(8,128)(2,1)S(1)} all-gather(bf16[32,3072]{1,0:T(8,128)(2,1)S(1)} %reshape.21.block_ref), channel_id=1, replica_groups={{0,2,4,6},{1,3,5,7},{8,10,12,14},{9,11,13,15},{16,18,20,22},{17,19,21,2..., dimensions={0}, use_global_device_ids=true | all-gather | bytes 983040 | tf_op jit(solution)/shard_map/all_gather | solution.py:168
  31.2 0.1 pad_add_fusion.height_ref
  31.3 1.0 %copy.11 = f32[3,3,3,2,1,512]{5,3,4,2,1,0:T(2,128)S(1)} copy(f32[3,3,3,2,1,512]{5,4,3,2,1,0:T(1,128)} %param.4) | data formatting | bytes 221184
  32.3 0.0 collective-permute-done.2.link_below_ref
  32.3 0.0 collective-permute-done.1.below_ref
  32.3 0.0 copy-start
  32.3 0.7 copy-done
  33.0 2.1 %shard_map.37 = bf16[12,32,3072]{2,1,0:T(8,128)(2,1)S(1)} custom-call(s32[4,3]{1,0:T(4,128)S(1)} %copy-done, s32[2]{0:T(128)S(1)} %pad_add_fusion.height_ref, bf16[32,3072]{1,0:T(8,128)(2,1)S(1)} %reshape.21.block_ref, bf16[32,3072]{1,0:T(8,128)(2,1)S(1)} %collective-permute-done.1.below_ref, f32[3,3,3,2,512]{4,3,2,1,0:T(2,128)S(1)} %bitcast.15, ...), custom_call_target="tpu_custom_call" | custom-call | tf_op jit(solution)/shard_map/pallas_call | solution.py:94
  35.0 0.0 collective-permute-done
  35.0 10.7 %all_gather.7.far_ref = bf16[128,3072]{1,0:T(8,128)(2,1)S(1)} all-gather(bf16[32,3072]{1,0:T(8,128)(2,1)S(1)} %collective-permute-done), channel_id=1, replica_groups={{0,2,4,6},{1,3,5,7},{8,10,12,14},{9,11,13,15},{16,18,20,22},{17,19,21,2..., dimensions={0}, use_global_device_ids=true | all-gather | bytes 983040 | tf_op jit(solution)/shard_map/all_gather | solution.py:168
  45.8 1.8 %shard_map.38 = bf16[4,2,8,8,384]{4,3,2,1,0:T(8,128)(2,1)S(1)} custom-call(s32[1]{0:T(128)} %bitcast.half_ref, bf16[384,3072]{1,0:T(8,128)(2,1)S(1)} %bitcast.13, bf16[128,3072]{1,0:T(8,128)(2,1)S(1)} %all_gather.6.near_ref, bf16[128,3072]{1,0:T(8,128)(2,1)S(1)} %all_gather.7.far_ref), custom_call_target="tpu_custom_call" | custom-call | tf_op jit(solution)/shard_map/pallas_call | solution.py:142
  47.6 30.3 %all_to_all.5 = bf16[64,8,384]{2,1,0:T(8,128)(2,1)S(1)} all-to-all(bf16[64,8,384]{2,1,0:T(8,128)(2,1)S(1)} %bitcast.14), channel_id=1, replica_groups=mesh['space'=64,'eig'=8] {'space'}, dimensions={0} | all-to-all | bytes 786432 | tf_op jit(solution)/shard_map/all_to_all | solution.py:180
  77.9 0.1 convert_reduce_fusion
  77.9 0.1 reshape.25
  78.0 0.6 copy.6
  (1 shorter events, 0.0 us)
Async XLA Ops:
  1.1 31.2 %collective-permute-start.1 = (bf16[32,3072]{1,0:T(8,128)(2,1)S(1)}, bf16[32,3072]{1,0:T(8,128)(2,1)S(1)}, u32[]{:S(2)}, u32[]{:S(2)}) collective-permute-start(bf16[32,3072]{1,0:T(8,128)(2,1)S(1)} %reshape.21.block_ref), channel_id=1, source_target_pairs={{0,8},{8,16},{16,24},{24,32},{32,40},{40,48},{48,56},{56,64},{64,7... | collective-permute-start | bytes 589832 | tf_op jit(solution)/shard_map/ppermute | solution.py:164
  6.5 28.6 %collective-permute-start = (bf16[32,3072]{1,0:T(8,128)(2,1)S(1)}, bf16[32,3072]{1,0:T(8,128)(2,1)S(1)}, u32[]{:S(2)}, u32[]{:S(2)}) collective-permute-start(bf16[32,3072]{1,0:T(8,128)(2,1)S(1)} %reshape.21.block_ref), channel_id=1, source_target_pairs={{0,1},{1,0},{2,3},{3,2},{4,5},{5,4},{6,7},{7,6},{8,9},{9,8},{10,11... | collective-permute-start | bytes 589832 | tf_op jit(solution)/shard_map/ppermute | solution.py:170
  17.0 15.3 %collective-permute-start.2 = (f32[3,3,2,512]{3,2,1,0:T(2,128)S(1)}, f32[3,3,2,512]{3,2,1,0:T(2,128)S(1)}, u32[]{:S(2)}, u32[]{:S(2)}) collective-permute-start(f32[3,3,2,512]{3,2,1,0:T(2,128)S(1)} %bitcast.17), channel_id=1, source_target_pairs={{0,8},{8,16},{16,24},{24,32},{32,40},{40,48},{48,56},{56,64},{64,7... | collective-permute-start | bytes 110600 | tf_op jit(solution)/shard_map/ppermute | solution.py:164
  32.3 0.7 copy-start

commit v5 on v4

--- a/solution.py
+++ b/solution.py
@@ -67,11 +67,11 @@
                     real_vec = source_ref[rows, at : at + SITES].astype(jnp.float32)
                     imag_vec = source_ref[rows, at + SITES : at + 2 * SITES].astype(jnp.float32)
                     if d == 2:
-                        real_link = link_below_ref[colour, out_colour, 0:1, :]
-                        imag_link = link_below_ref[colour, out_colour, 1:2, :]
+                        real_link = link_below_ref[2, colour, out_colour, 0]
+                        imag_link = link_below_ref[2, colour, out_colour, 1]
                     else:
-                        real_link = link_ref[d, colour, out_colour, 0:1, :]
-                        imag_link = link_ref[d, colour, out_colour, 1:2, :]
+                        real_link = link_ref[d, colour, out_colour, 0]
+                        imag_link = link_ref[d, colour, out_colour, 1]
                     real_base += real_vec * real_link + imag_vec * imag_link
                     imag_base += real_vec * imag_link - imag_vec * real_link
                 real_base, imag_base = MOVES[d](real_base), MOVES[d](imag_base)
@@ -102,18 +102,20 @@
     )(momenta, height, block, below, links, link_below)
 
 
-def product_kernel(half_ref, left_ref, near_ref, far_ref, out_ref, both_ref):
-    def spread(source_ref):
+def product_kernel(where_ref, left_ref, *refs):
+    near_refs, (far_ref, out_ref, both_ref) = refs[:4], refs[4:]
+
+    def spread(source_ref, to, rows):
         for colour in range(3):
             at = 2 * SITES * colour
             real_vec = source_ref[:, at : at + SITES]
             imag_vec = source_ref[:, at + SITES : at + 2 * SITES]
-            both_ref[0:128, at : at + SITES] = real_vec
-            both_ref[0:128, at + SITES : at + 2 * SITES] = -imag_vec
-            both_ref[128:256, at : at + SITES] = imag_vec
-            both_ref[128:256, at + SITES : at + 2 * SITES] = real_vec
-
-    def multiply(half):
+            both_ref[to : to + rows, at : at + SITES] = real_vec
+            both_ref[to : to + rows, at + SITES : at + 2 * SITES] = -imag_vec
+            both_ref[to + 128 : to + 128 + rows, at : at + SITES] = imag_vec
+            both_ref[to + 128 : to + 128 + rows, at + SITES : at + 2 * SITES] = real_vec
+
+    def multiply(half, first):
         product = lax.dot_general(
             both_ref[...],
             left_ref[...],
@@ -127,27 +129,29 @@
         even = jnp.where(upper, real_part, pltpu.roll(imag_part, 4, 1)).astype(jnp.bfloat16)
         odd = jnp.where(upper, pltpu.roll(real_part, 4, 1), imag_part).astype(jnp.bfloat16)
         for block in range(4):
+            to = (first + block) & 3
             for pair in range(4):
-                out_ref[block, half, 2 * pair] = even[4 * block + pair]
-                out_ref[block, half, 2 * pair + 1] = odd[4 * block + pair]
-
-    half = half_ref[0]
-    spread(near_ref)
-    multiply(half)
-    spread(far_ref)
-    multiply(1 - half)
-
-
-def products(half, left, near, far):
+                out_ref[to, half, 2 * pair] = even[4 * block + pair]
+                out_ref[to, half, 2 * pair + 1] = odd[4 * block + pair]
+
+    half = where_ref[0]
+    for block in range(4):
+        spread(near_refs[block], ROWS * block, ROWS)
+    multiply(half, where_ref[1])
+    spread(far_ref, 0, 128)
+    multiply(1 - half, 0)
+
+
+def products(where, left, near, far):
     return pl.pallas_call(
         product_kernel,
         out_shape=jax.ShapeDtypeStruct((4, 2, 8, 8, 12 * ROWS), jnp.bfloat16),
         in_specs=[pl.BlockSpec(memory_space=pltpu.SMEM)]
-        + [pl.BlockSpec(memory_space=pltpu.VMEM)] * 3,
+        + [pl.BlockSpec(memory_space=pltpu.VMEM)] * 6,
         out_specs=pl.BlockSpec(memory_space=pltpu.VMEM),
         scratch_shapes=[pltpu.VMEM((256, DEPTH), jnp.bfloat16)],
         compiler_params=pltpu.CompilerParams(vmem_limit_bytes=VMEM_BYTES),
-    )(half, left, near, far)
+    )(where, left, *near, far)
 
 
 def body(eigenvectors, gauge_links, momenta):
@@ -156,27 +160,30 @@
     s = lax.axis_index("space")
     e = lax.axis_index("eig")
     block = eigenvectors.reshape(ROWS, DEPTH)
-    links = gauge_links.reshape(3, 3, 3, 2, SITES)
     height = jnp.stack([s, jnp.int32(space)]).astype(jnp.int32)
-    half = (e & 1).astype(jnp.int32).reshape(1)
+    where = jnp.stack([e & 1, e >> 1]).astype(jnp.int32)
 
     def from_below(value):
         return lax.ppermute(value, "space", [(a, (a + 1) % space) for a in range(space)])
 
-    def around_x(value):
-        groups = [list(range(0, eig, 2)), list(range(1, eig, 2))]
-        return lax.all_gather(value, "eig", axis_index_groups=groups, tiled=True)
+    def from_x(value, steps):
+        return lax.ppermute(value, "eig", [((a + 2 * steps) % eig, a) for a in range(eig)])
 
     partner = lax.ppermute(block, "eig", [(a, a ^ 1) for a in range(eig)])
-    near = around_x(block)
-    below = from_below(block)
-    link_below = from_below(links[2])
-    left = left_operand(momenta, height, block, below, links, link_below)
+    links_below = from_below(gauge_links)
+    later, links_below = lax.optimization_barrier((block, links_below))
+    below = from_below(later)
+    before, after, opposite = from_x(later, 3), from_x(later, 1), from_x(later, 2)
+    left = left_operand(momenta, height, block, below, gauge_links, links_below)
     left = left.reshape(12 * ROWS, DEPTH)
 
-    partner, left, near = lax.optimization_barrier((partner, left, near))
-    far = around_x(partner)
-    chunks = products(half, left, near, far).reshape(space, 8, 12 * ROWS)
+    partner, left = lax.optimization_barrier((partner, left))
+    partner, before, after, opposite = lax.optimization_barrier(
+        (partner, before, after, opposite)
+    )
+    groups = [list(range(0, eig, 2)), list(range(1, eig, 2))]
+    far = lax.all_gather(partner, "eig", axis_index_groups=groups, tiled=True)
+    chunks = products(where, left, (block, after, opposite, before), far).reshape(space, 8, 12 * ROWS)
     got = lax.all_to_all(chunks, "space", split_axis=0, concat_axis=0, tiled=True)
     total = jnp.sum(got.astype(jnp.float32), axis=0)
     return total.reshape(2, 4, 3, 4, ROWS).transpose(2, 3, 0, 4, 1)

time: 79 us -> 80.6 us (1.020)
  blocking collectives: 53 us -> 41.5 us
  starting transfers between devices: 17.3 us -> 28.1 us
  waiting for transfers between devices: 0.01 us -> 2.45 us
  local copies, waits for them, and re-layouts: 4.2 us -> 3.35 us
    all_gather x2 -> x1, blocking collectives: 22.8 us -> 11.1 us  [body(): far = lax.all_gather(partner, 'eig', axis_index_groups=groups, tiled=True)]
    ppermute x0 -> x3, starting transfers between devices: none -> 9.93 us  [from_x(): lax.ppermute(value, 'eig', [((a + 2 * steps) % eig, a) for a in range(eig)])]
    ppermute x2, waiting for transfers between devices: 0.01 us -> 2.44 us  [from_below(): lax.ppermute(value, 'space', [(a, (a + 1) % space) for a in range(space)])]
    ppermute x2, starting transfers between devices: 7.59 us -> 8.42 us  [from_below(): lax.ppermute(value, 'space', [(a, (a + 1) % space) for a in range(space)])]
  transfers between devices with their start and end apart: 3 -> 6, of which waited for: 0 -> 1; matrix products, arithmetic and copies ran while one was open for 2% -> 2% of each run, Pallas kernels for 3% -> 3%
where the time goes in v5:
time: 80.6 us; the launch traced here: 80.2 us
  blocking collectives  41.5 us (51%)
  starting transfers between devices  28.1 us (35%)
  Pallas kernels  4.43 us (5%)
  local copies, waits for them, and re-layouts  3.35 us (4%)
  waiting for transfers between devices  2.45 us (3%)
    all_to_all x1, blocking collectives, body(): lax.all_to_all(chunks, 'space', split_axis=0, concat_axis=0, tiled=True)  30.4 us
    all_gather x1, blocking collectives, body(): far = lax.all_gather(partner, 'eig', axis_index_groups=groups, tiled=True)  11.1 us
    ppermute x3, starting transfers between devices, from_x(): lax.ppermute(value, 'eig', [((a + 2 * steps) % eig, a) for a in range(eig)])  9.93 us
    ppermute x1, starting transfers between devices, body(): partner = lax.ppermute(block, 'eig', [(a, a ^ 1) for a in range(eig)])  9.74 us
    ppermute x2, starting transfers between devices, from_below(): lax.ppermute(value, 'space', [(a, (a + 1) % space) for a in range(space)])  8.42 us
    ppermute x2, waiting for transfers between devices, from_below(): lax.ppermute(value, 'space', [(a, (a + 1) % space) for a in range(space)])  2.44 us
    pallas_call x1, Pallas kernels, products(): pl.pallas_call(product_kernel, out_shape=jax.ShapeDtypeStruct((4, 2, 8, 8...  2.35 us
    pallas_call x1, Pallas kernels, left_operand(): pl.pallas_call(left_kernel, out_shape=jax.ShapeDtypeStruct((12, ROWS, DEP...  2.08 us
  transfers between devices with their start and end apart: 6, of which 1 were waited for; matrix products, arithmetic and copies ran while one was open for 2% of the time, Pallas kernels for 3%

profile of v5, /device:TPU:1, one launch (start us, length us, event | category | flops | bytes accessed | tf_op | source)
XLA Modules:
  0.0 80.2 jit_solution(14910787695740591493)
XLA Ops:
  0.0 5.4 %collective-permute-start.1 = (f32[3,3,3,2,1,512]{5,4,3,2,1,0:T(1,128)}, f32[3,3,3,2,1,512]{5,4,3,2,1,0:T(1,128)S(1)}, u32[]{:S(2)}, u32[]{:S(2)}) collective-permute-start(f32[3,3,3,2,1,512]{5,4,3,2,1,0:T(1,128)} %link_ref.1), channel_id=1, source_target_pairs={{0,8},{8,16},{16,24},{24,32},{32,40},{40,48},{48,56},{56,64},{64,7... | collective-permute-start | bytes 331784 | tf_op jit(solution)/shard_map/ppermute | solution.py:167
  5.4 1.1 %reshape.12.block_ref.refs_0_ = bf16[32,3072]{1,0:T(8,128)(2,1)S(1)} reshape(bf16[32,3,2,1,512]{4,2,3,1,0:T(2,128)(2,1)} %param.3) | data formatting | bytes 393216 | tf_op jit(solution)/shard_map/reshape | solution.py:162
  6.4 9.7 %collective-permute-start = (bf16[32,3072]{1,0:T(8,128)(2,1)S(1)}, bf16[32,3072]{1,0:T(8,128)(2,1)S(1)}, u32[]{:S(2)}, u32[]{:S(2)}) collective-permute-start(bf16[32,3072]{1,0:T(8,128)(2,1)S(1)} %reshape.12.block_ref.refs_0_), channel_id=1, source_target_pairs={{0,1},{1,0},{2,3},{3,2},{4,5},{5,4},{6,7},{7,6},{8,9},{9,8},{10,11... | collective-permute-start | bytes 589832 | tf_op jit(solution)/shard_map/ppermute | solution.py:172
  16.2 0.0 collective-permute-done.1.link_below_ref
  16.2 4.7 %collective-permute-start.5 = (bf16[32,3072]{1,0:T(8,128)(2,1)S(1)}, bf16[32,3072]{1,0:T(8,128)(2,1)S(1)}, u32[]{:S(2)}, u32[]{:S(2)}) collective-permute-start(bf16[32,3072]{1,0:T(8,128)(2,1)S(1)} %reshape.12.block_ref.refs_0_), channel_id=1, source_target_pairs={{4,0},{5,1},{6,2},{7,3},{0,4},{1,5},{2,6},{3,7},{12,8},{13,9},{14,... | collective-permute-start | bytes 589832 | tf_op jit(solution)/shard_map/ppermute | solution.py:170
  20.9 2.8 %collective-permute-start.4 = (bf16[32,3072]{1,0:T(8,128)(2,1)S(1)}, bf16[32,3072]{1,0:T(8,128)(2,1)S(1)}, u32[]{:S(2)}, u32[]{:S(2)}) collective-permute-start(bf16[32,3072]{1,0:T(8,128)(2,1)S(1)} %reshape.12.block_ref.refs_0_), channel_id=1, source_target_pairs={{2,0},{3,1},{4,2},{5,3},{6,4},{7,5},{0,6},{1,7},{10,8},{11,9},{12,... | collective-permute-start | bytes 589832 | tf_op jit(solution)/shard_map/ppermute | solution.py:170
  23.6 2.5 %collective-permute-start.3 = (bf16[32,3072]{1,0:T(8,128)(2,1)S(1)}, bf16[32,3072]{1,0:T(8,128)(2,1)S(1)}, u32[]{:S(2)}, u32[]{:S(2)}) collective-permute-start(bf16[32,3072]{1,0:T(8,128)(2,1)S(1)} %reshape.12.block_ref.refs_0_), channel_id=1, source_target_pairs={{6,0},{7,1},{0,2},{1,3},{2,4},{3,5},{4,6},{5,7},{14,8},{15,9},{8,1... | collective-permute-start | bytes 589832 | tf_op jit(solution)/shard_map/ppermute | solution.py:170
  26.2 3.0 %collective-permute-start.2 = (bf16[32,3072]{1,0:T(8,128)(2,1)S(1)}, bf16[32,3072]{1,0:T(8,128)(2,1)S(1)}, u32[]{:S(2)}, u32[]{:S(2)}) collective-permute-start(bf16[32,3072]{1,0:T(8,128)(2,1)S(1)} %reshape.12.block_ref.refs_0_), channel_id=1, source_target_pairs={{0,8},{8,16},{16,24},{24,32},{32,40},{40,48},{48,56},{56,64},{64,7... | collective-permute-start | bytes 589832 | tf_op jit(solution)/shard_map/ppermute | solution.py:167
  29.2 0.1 pad_add_fusion.where_ref
  29.3 0.1 pad_add_fusion.1.height_ref
  29.4 2.4 %collective-permute-done.2.below_ref = bf16[32,3072]{1,0:T(8,128)(2,1)S(1)} collective-permute-done((bf16[32,3072]{1,0:T(8,128)(2,1)S(1)}, bf16[32,3072]{1,0:T(8,128)(2,1)S(1)}, u32[]{:S(2)}, u32[]{:S(2)}) %collective-permute-start.2) | collective-permute-done | bytes 196640 | tf_op jit(solution)/shard_map/ppermute | solution.py:167
  31.8 0.0 copy-start
  31.8 0.9 %copy-done = f32[3,3,3,2,1,512]{5,4,3,2,1,0:T(1,128)S(1)} copy-done((f32[3,3,3,2,1,512]{5,4,3,2,1,0:T(1,128)S(1)}, f32[3,3,3,2,1,512]{5,4,3,2,1,0:T(1,128)}, u32[]{:S(2)}) %copy-start) | copy-done | bytes 110616
  32.7 0.0 copy-start.1
  32.7 0.7 copy-done.1
  33.4 2.1 %shard_map.37 = bf16[12,32,3072]{2,1,0:T(8,128)(2,1)S(1)} custom-call(s32[4,3]{1,0:T(4,128)S(1)} %copy-done.1, s32[2]{0:T(128)S(1)} %pad_add_fusion.1.height_ref, bf16[32,3072]{1,0:T(8,128)(2,1)S(1)} %reshape.12.block_ref.refs_0_, bf16[32,3072]{1,0:T(8,128)(2,1)S(1)} %collective-permute-done.2.below_ref, f32[3,3,3,2,1,512]{5,4,3,2,1,0:T(1,128)S(1)} %copy-done, ...), custom_call_target="tpu_custom_call" | custom-call | tf_op jit(solution)/shard_map/pallas_call | solution.py:94
  35.5 0.0 collective-permute-done
  35.5 0.0 collective-permute-done.5.refs_2_
  35.5 0.0 collective-permute-done.4.refs_1_
  35.5 0.0 collective-permute-done.3.refs_3_
  35.5 11.1 %all_gather.3.refs_4_ = bf16[128,3072]{1,0:T(8,128)(2,1)S(1)} all-gather(bf16[32,3072]{1,0:T(8,128)(2,1)S(1)} %collective-permute-done), channel_id=1, replica_groups={{0,2,4,6},{1,3,5,7},{8,10,12,14},{9,11,13,15},{16,18,20,22},{17,19,21,2..., dimensions={0}, use_global_device_ids=true | all-gather | bytes 983040 | tf_op jit(solution)/shard_map/all_gather | solution.py:185
  46.7 2.3 %shard_map.38 = bf16[4,2,8,8,384]{4,3,2,1,0:T(8,128)(2,1)S(1)} custom-call(s32[2]{0:T(128)S(1)} %pad_add_fusion.where_ref, bf16[384,3072]{1,0:T(8,128)(2,1)S(1)} %bitcast.8, bf16[32,3072]{1,0:T(8,128)(2,1)S(1)} %reshape.12.block_ref.refs_0_, bf16[32,3072]{1,0:T(8,128)(2,1)S(1)} %collective-permute-done.4.refs_1_, ...), custom_call_target="tpu_custom_call" | custom-call | tf_op jit(solution)/shard_map/pallas_call | solution.py:146
  49.0 30.4 %all_to_all.5 = bf16[64,8,384]{2,1,0:T(8,128)(2,1)S(1)} all-to-all(bf16[64,8,384]{2,1,0:T(8,128)(2,1)S(1)} %bitcast.9), channel_id=1, replica_groups=mesh['space'=64,'eig'=8] {'space'}, dimensions={0} | all-to-all | bytes 786432 | tf_op jit(solution)/shard_map/all_to_all | solution.py:187
  79.4 0.1 convert_reduce_fusion
  79.5 0.1 reshape.15
  79.6 0.6 copy.4
Async XLA Ops:
  0.0 16.2 %collective-permute-start.1 = (f32[3,3,3,2,1,512]{5,4,3,2,1,0:T(1,128)}, f32[3,3,3,2,1,512]{5,4,3,2,1,0:T(1,128)S(1)}, u32[]{:S(2)}, u32[]{:S(2)}) collective-permute-start(f32[3,3,3,2,1,512]{5,4,3,2,1,0:T(1,128)} %link_ref.1), channel_id=1, source_target_pairs={{0,8},{8,16},{16,24},{24,32},{32,40},{40,48},{48,56},{56,64},{64,7... | collective-permute-start | bytes 331784 | tf_op jit(solution)/shard_map/ppermute | solution.py:167
  6.4 29.0 %collective-permute-start = (bf16[32,3072]{1,0:T(8,128)(2,1)S(1)}, bf16[32,3072]{1,0:T(8,128)(2,1)S(1)}, u32[]{:S(2)}, u32[]{:S(2)}) collective-permute-start(bf16[32,3072]{1,0:T(8,128)(2,1)S(1)} %reshape.12.block_ref.refs_0_), channel_id=1, source_target_pairs={{0,1},{1,0},{2,3},{3,2},{4,5},{5,4},{6,7},{7,6},{8,9},{9,8},{10,11... | collective-permute-start | bytes 589832 | tf_op jit(solution)/shard_map/ppermute | solution.py:172
  16.2 19.3 %collective-permute-start.5 = (bf16[32,3072]{1,0:T(8,128)(2,1)S(1)}, bf16[32,3072]{1,0:T(8,128)(2,1)S(1)}, u32[]{:S(2)}, u32[]{:S(2)}) collective-permute-start(bf16[32,3072]{1,0:T(8,128)(2,1)S(1)} %reshape.12.block_ref.refs_0_), channel_id=1, source_target_pairs={{4,0},{5,1},{6,2},{7,3},{0,4},{1,5},{2,6},{3,7},{12,8},{13,9},{14,... | collective-permute-start | bytes 589832 | tf_op jit(solution)/shard_map/ppermute | solution.py:170
  20.9 14.6 %collective-permute-start.4 = (bf16[32,3072]{1,0:T(8,128)(2,1)S(1)}, bf16[32,3072]{1,0:T(8,128)(2,1)S(1)}, u32[]{:S(2)}, u32[]{:S(2)}) collective-permute-start(bf16[32,3072]{1,0:T(8,128)(2,1)S(1)} %reshape.12.block_ref.refs_0_), channel_id=1, source_target_pairs={{2,0},{3,1},{4,2},{5,3},{6,4},{7,5},{0,6},{1,7},{10,8},{11,9},{12,... | collective-permute-start | bytes 589832 | tf_op jit(solution)/shard_map/ppermute | solution.py:170
  23.6 11.9 %collective-permute-start.3 = (bf16[32,3072]{1,0:T(8,128)(2,1)S(1)}, bf16[32,3072]{1,0:T(8,128)(2,1)S(1)}, u32[]{:S(2)}, u32[]{:S(2)}) collective-permute-start(bf16[32,3072]{1,0:T(8,128)(2,1)S(1)} %reshape.12.block_ref.refs_0_), channel_id=1, source_target_pairs={{6,0},{7,1},{0,2},{1,3},{2,4},{3,5},{4,6},{5,7},{14,8},{15,9},{8,1... | collective-permute-start | bytes 589832 | tf_op jit(solution)/shard_map/ppermute | solution.py:170
  26.2 5.6 %collective-permute-start.2 = (bf16[32,3072]{1,0:T(8,128)(2,1)S(1)}, bf16[32,3072]{1,0:T(8,128)(2,1)S(1)}, u32[]{:S(2)}, u32[]{:S(2)}) collective-permute-start(bf16[32,3072]{1,0:T(8,128)(2,1)S(1)} %reshape.12.block_ref.refs_0_), channel_id=1, source_target_pairs={{0,8},{8,16},{16,24},{24,32},{32,40},{40,48},{48,56},{56,64},{64,7... | collective-permute-start | bytes 589832 | tf_op jit(solution)/shard_map/ppermute | solution.py:167
  31.8 0.9 %copy-start = (f32[3,3,3,2,1,512]{5,4,3,2,1,0:T(1,128)S(1)}, f32[3,3,3,2,1,512]{5,4,3,2,1,0:T(1,128)}, u32[]{:S(2)}) copy-start(f32[3,3,3,2,1,512]{5,4,3,2,1,0:T(1,128)} %link_ref.1) | copy-start | bytes 331780
  32.7 0.7 copy-start.1

commit v6 on v2

v6 whole, which is shorter than its diff:
```python
import math

import jax
import jax.numpy as jnp
from jax import lax
from jax.experimental import pallas as pl
from jax.experimental.pallas import tpu as pltpu
from jax.sharding import PartitionSpec as P

LX = 64
LY = 8
SITES = LX * LY
ROWS = 32
DEPTH = 6 * SITES
VMEM_BYTES = 40 * 1024 * 1024


def moved_across(field):
    lane = lax.broadcasted_iota(jnp.int32, field.shape, 1)
    return jnp.where(
        lane % LX == 0, pltpu.roll(field, SITES - LX + 1, 1), pltpu.roll(field, 1, 1)
    )


def moved_along(field):
    return pltpu.roll(field, LX, 1)


MOVES = (moved_across, moved_along, lambda field: field)


def left_kernel(plane_ref, block_ref, link_ref, left_ref, raised_ref, table_ref):
    row = lax.broadcasted_iota(jnp.int32, (8, SITES), 0) % 4
    site = lax.broadcasted_iota(jnp.int32, (8, SITES), 1)

    def component(k):
        value = jnp.full((8, SITES), plane_ref[3, k], jnp.int32)
        for p in range(3):
            value = jnp.where(row == p, plane_ref[p, k], value)
        return value

    x_frac = ((component(0) * (site % LX)) & (LX - 1)).astype(jnp.float32) / LX
    y_frac = ((component(1) * (site // LX)) & (LY - 1)).astype(jnp.float32) / LY
    extent = plane_ref[4, 1]
    z_frac = ((component(2) * plane_ref[4, 0]) & (extent - 1)).astype(jnp.float32)
    z_frac = z_frac / extent.astype(jnp.float32)
    angles = 2.0 * math.pi * (x_frac + y_frac + z_frac)
    first = lax.broadcasted_iota(jnp.int32, (8, SITES), 0) < 4
    table = jnp.where(first, jnp.cos(angles), jnp.sin(angles))
    for d in range(3):
        table_ref[d] = MOVES[d](table)

    def rows_of(group, carry):
        rows = pl.ds(pl.multiple_of(group * 16, 16), 16)
        for d in range(3):
            for out_colour in range(3):
                real_base = jnp.zeros((16, SITES), jnp.float32)
                imag_base = jnp.zeros((16, SITES), jnp.float32)
                for colour in range(3):
                    at = 2 * SITES * colour
                    real_vec = block_ref[rows, at : at + SITES].astype(jnp.float32)
                    imag_vec = block_ref[rows, at + SITES : at + 2 * SITES].astype(jnp.float32)
                    real_link = link_ref[d, colour, out_colour, 0]
                    imag_link = link_ref[d, colour, out_colour, 1]
                    real_base += real_vec * real_link + imag_vec * imag_link
                    imag_base += real_vec * imag_link - imag_vec * real_link
                real_base, imag_base = MOVES[d](real_base), MOVES[d](imag_base)
                at = 2 * SITES * out_colour
                to_ref, to = (raised_ref, 0) if d == 2 else (left_ref, 4 * d)
                for p in range(4):
                    cosine = table_ref[d, p : p + 1, :]
                    sine = table_ref[d, p + 4 : p + 5, :]
                    to_ref[to + p, rows, at : at + SITES] = (
                        real_base * cosine + imag_base * sine
                    ).astype(jnp.bfloat16)
                    to_ref[to + p, rows, at + SITES : at + 2 * SITES] = (
                        imag_base * cosine - real_base * sine
                    ).astype(jnp.bfloat16)
        return carry

    lax.fori_loop(0, ROWS // 16, rows_of, 0)


def left_operand(plane, block, links):
    return pl.pallas_call(
        left_kernel,
        out_shape=[
            jax.ShapeDtypeStruct((8, ROWS, DEPTH), jnp.bfloat16),
            jax.ShapeDtypeStruct((4, ROWS, DEPTH), jnp.bfloat16),
        ],
        in_specs=[pl.BlockSpec(memory_space=pltpu.SMEM)]
        + [pl.BlockSpec(memory_space=pltpu.VMEM)] * 2,
        out_specs=[pl.BlockSpec(memory_space=pltpu.VMEM)] * 2,
        scratch_shapes=[pltpu.VMEM((3, 8, SITES), jnp.float32)],
        compiler_params=pltpu.CompilerParams(vmem_limit_bytes=VMEM_BYTES),
    )(plane, block, links)


def product_kernel(half_ref, left_ref, raised_ref, near_ref, far_ref, out_ref, both_ref):
    def spread(source_ref):
        for colour in range(3):
            at = 2 * SITES * colour
            real_vec = source_ref[:, at : at + SITES]
            imag_vec = source_ref[:, at + SITES : at + 2 * SITES]
            both_ref[0:128, at : at + SITES] = real_vec
            both_ref[0:128, at + SITES : at + 2 * SITES] = -imag_vec
            both_ref[128:256, at : at + SITES] = imag_vec
            both_ref[128:256, at + SITES : at + 2 * SITES] = real_vec

    def multiply(source_ref, half, least, most):
        product = lax.dot_general(
            both_ref[...],
            source_ref[...],
            (((1,), (1,)), ((), ())),
            preferred_element_type=jnp.float32,
        )
        width = most - least
        real_part = product[0:128].reshape(16, 8, width)
        imag_part = product[128:256].reshape(16, 8, width)
        upper = lax.broadcasted_iota(jnp.int32, (16, 8, width), 1) < 4
        even = jnp.where(upper, real_part, pltpu.roll(imag_part, 4, 1)).astype(jnp.bfloat16)
        odd = jnp.where(upper, pltpu.roll(real_part, 4, 1), imag_part).astype(jnp.bfloat16)
        for block in range(4):
            for pair in range(4):
                out_ref[block, half, 2 * pair, :, least:most] = even[4 * block + pair]
                out_ref[block, half, 2 * pair + 1, :, least:most] = odd[4 * block + pair]

    for source_ref, half in ((near_ref, half_ref[0]), (far_ref, 1 - half_ref[0])):
        spread(source_ref)
        multiply(left_ref, half, 0, 8 * ROWS)
        multiply(raised_ref, half, 8 * ROWS, 12 * ROWS)


def products(half, left, raised, near, far):
    return pl.pallas_call(
        product_kernel,
        out_shape=jax.ShapeDtypeStruct((4, 2, 8, 8, 12 * ROWS), jnp.bfloat16),
        in_specs=[pl.BlockSpec(memory_space=pltpu.SMEM)]
        + [pl.BlockSpec(memory_space=pltpu.VMEM)] * 4,
        out_specs=pl.BlockSpec(memory_space=pltpu.VMEM),
        scratch_shapes=[pltpu.VMEM((256, DEPTH), jnp.bfloat16)],
        compiler_params=pltpu.CompilerParams(vmem_limit_bytes=VMEM_BYTES),
    )(half, left, raised, near, far)


def body(eigenvectors, gauge_links, momenta):
    space = lax.axis_size("space")
    eig = lax.axis_size("eig")
    s = lax.axis_index("space")
    e = lax.axis_index("eig")
    block = eigenvectors.reshape(ROWS, DEPTH)
    row = lax.broadcasted_iota(jnp.int32, (5, 3), 0)
    column = lax.broadcasted_iota(jnp.int32, (5, 3), 1)
    plane = jnp.where(column == 0, s, space).astype(jnp.int32)
    plane = jnp.where(row < 4, jnp.pad(momenta, ((0, 1), (0, 0))), plane)
    half = (e & 1).astype(jnp.int32).reshape(1)
    groups = [list(range(0, eig, 2)), list(range(1, eig, 2))]

    def around_x(value):
        return lax.all_gather(value, "eig", axis_index_groups=groups, tiled=True)

    partner = lax.ppermute(block, "eig", [(a, a ^ 1) for a in range(eig)])
    near = around_x(block)
    near, plane = lax.optimization_barrier((near, plane))
    left, raised = left_operand(plane, block, gauge_links)

    partner, near, left, raised = lax.optimization_barrier((partner, near, left, raised))
    raised = lax.ppermute(raised, "space", [(a, (a + 1) % space) for a in range(space)])
    far = around_x(partner)
    left, raised = left.reshape(8 * ROWS, DEPTH), raised.reshape(4 * ROWS, DEPTH)
    chunks = products(half, left, raised, near, far).reshape(space, 8, 12 * ROWS)
    got = lax.all_to_all(chunks, "space", split_axis=0, concat_axis=0, tiled=True)
    total = jnp.sum(got.astype(jnp.float32), axis=0)
    return total.reshape(2, 4, 3, 4, ROWS).transpose(2, 3, 0, 4, 1)


def solution(mesh):
    return jax.shard_map(
        body,
        mesh=mesh,
        in_specs=(
            P("eig", None, None, "space", None),
            P(None, None, None, None, "space", None),
            P(),
        ),
        out_specs=P(None, None, None, "eig", "space"),
        check_vma=False,
    )
```

time: 78.2 us -> 76.1 us (0.973)
  the two profiles are of different devices: /device:TPU:8 before, /device:TPU:1 now
where the time goes in v6:
time: 76.1 us; the launch traced here: 75.8 us
  blocking collectives  50.9 us (67%)
  starting transfers between devices  16.7 us (22%)
  Pallas kernels  4.6 us (6%)
  local copies, waits for them, and re-layouts  2.67 us (4%)
  other arithmetic  0.85 us (1%)
    all_to_all x1, blocking collectives, body(): lax.all_to_all(chunks, 'space', split_axis=0, concat_axis=0, tiled=True)  25.5 us
    all_gather x2, blocking collectives, around_x(): return lax.all_gather(value, 'eig', axis_index_groups=groups, tiled=True)  25.4 us
    ppermute x1, starting transfers between devices, body(): partner = lax.ppermute(block, 'eig', [(a, a ^ 1) for a in range(eig)])  11.5 us
    ppermute x1, starting transfers between devices, body(): lax.ppermute(raised, 'space', [(a, (a + 1) % space) for a in range(space)])  5.22 us
    pallas_call x1, Pallas kernels, left_operand(): pl.pallas_call(left_kernel, out_shape=[jax.ShapeDtypeStruct((8, ROWS, DEP...  2.79 us
    pallas_call x1, Pallas kernels, products(): pl.pallas_call(product_kernel, out_shape=jax.ShapeDtypeStruct((4, 2, 8, 8...  1.8 us
  transfers between devices with their start and end apart: 2, of which 0 were waited for; matrix products, arithmetic and copies ran while one was open for 1% of the time, Pallas kernels for 4%

profile of v6, /device:TPU:1, one launch (start us, length us, event | category | flops | bytes accessed | tf_op | source)
XLA Modules:
  0.0 75.8 jit_solution(15708157207728900935)
XLA Ops:
  0.0 1.1 %reshape.19.block_ref = bf16[32,3072]{1,0:T(8,128)(2,1)S(1)} reshape(bf16[32,3,2,1,512]{4,2,3,1,0:T(2,128)(2,1)} %param.3) | data formatting | bytes 393216 | tf_op jit(solution)/shard_map/reshape | solution.py:151
  1.1 11.5 %collective-permute-start = (bf16[32,3072]{1,0:T(8,128)(2,1)S(1)}, bf16[32,3072]{1,0:T(8,128)(2,1)S(1)}, u32[]{:S(2)}, u32[]{:S(2)}) collective-permute-start(bf16[32,3072]{1,0:T(8,128)(2,1)S(1)} %reshape.19.block_ref), channel_id=1, source_target_pairs={{0,1},{1,0},{2,3},{3,2},{4,5},{5,4},{6,7},{7,6},{8,9},{9,8},{10,11... | collective-permute-start | bytes 589832 | tf_op jit(solution)/shard_map/ppermute | solution.py:162
  12.5 12.4 %all_gather.6.near_ref = bf16[128,3072]{1,0:T(8,128)(2,1)S(1)} all-gather(bf16[32,3072]{1,0:T(8,128)(2,1)S(1)} %reshape.19.block_ref), channel_id=1, replica_groups={{0,2,4,6},{1,3,5,7},{8,10,12,14},{9,11,13,15},{16,18,20,22},{17,19,21,2..., dimensions={0}, use_global_device_ids=true | all-gather | bytes 983040 | tf_op jit(solution)/shard_map/all_gather | solution.py:160
  24.9 0.8 pad_select_fusion.plane_ref
  25.7 0.0 copy-start
  25.7 0.9 %copy-done = f32[3,3,3,2,1,512]{5,4,3,2,1,0:T(1,128)S(1)} copy-done((f32[3,3,3,2,1,512]{5,4,3,2,1,0:T(1,128)S(1)}, f32[3,3,3,2,1,512]{5,4,3,2,1,0:T(1,128)}, u32[]{:S(2)}) %copy-start) | copy-done | bytes 110616
  26.6 2.8 %shard_map.37 = (bf16[8,32,3072]{2,1,0:T(8,128)(2,1)S(1)}, bf16[4,32,3072]{2,1,0:T(8,128)(2,1)}) custom-call(s32[5,3]{1,0:T(8,128)S(1)} %pad_select_fusion.plane_ref, bf16[32,3072]{1,0:T(8,128)(2,1)S(1)} %reshape.19.block_ref, f32[3,3,3,2,1,512]{5,4,3,2,1,0:T(1,128)S(1)} %copy-done), custom_call_target="tpu_custom_call" | custom-call | tf_op jit(solution)/shard_map/pallas_call | solution.py:85
  29.4 0.0 collective-permute-done
  29.4 5.2 %collective-permute-start.1 = (bf16[4,32,3072]{2,1,0:T(8,128)(2,1)}, bf16[4,32,3072]{2,1,0:T(8,128)(2,1)S(1)}, u32[]{:S(2)}, u32[]{:S(2)}) collective-permute-start(bf16[4,32,3072]{2,1,0:T(8,128)(2,1)} %get-tuple-element.18), channel_id=1, source_target_pairs={{0,8},{8,16},{16,24},{24,32},{32,40},{40,48},{48,56},{56,64},{64,7... | collective-permute-start | bytes 2359304 | tf_op jit(solution)/shard_map/ppermute | solution.py:168
  34.6 13.0 %all_gather.7.far_ref = bf16[128,3072]{1,0:T(8,128)(2,1)S(1)} all-gather(bf16[32,3072]{1,0:T(8,128)(2,1)S(1)} %collective-permute-done), channel_id=1, replica_groups={{0,2,4,6},{1,3,5,7},{8,10,12,14},{9,11,13,15},{16,18,20,22},{17,19,21,2..., dimensions={0}, use_global_device_ids=true | all-gather | bytes 983040 | tf_op jit(solution)/shard_map/all_gather | solution.py:160
  47.6 0.0 collective-permute-done.1
  47.6 1.8 %shard_map.38 = bf16[4,2,8,8,384]{4,3,2,1,0:T(8,128)(2,1)S(1)} custom-call(s32[1]{0:T(128)} %bitcast.half_ref, bf16[256,3072]{1,0:T(8,128)(2,1)S(1)} %bitcast.7, bf16[128,3072]{1,0:T(8,128)(2,1)S(1)} %bitcast.9, bf16[128,3072]{1,0:T(8,128)(2,1)S(1)} %all_gather.6.near_ref, bf16[128,3072]{1,0:T(8,128)(2,1)S(1)} %all_gather.7.far_ref), custom_call_target="tpu_custom_call" | custom-call | tf_op jit(solution)/shard_map/pallas_call | solution.py:135
  49.5 25.5 %all_to_all.5 = bf16[64,8,384]{2,1,0:T(8,128)(2,1)S(1)} all-to-all(bf16[64,8,384]{2,1,0:T(8,128)(2,1)S(1)} %bitcast.8), channel_id=1, replica_groups=mesh['space'=64,'eig'=8] {'space'}, dimensions={0} | all-to-all | bytes 786432 | tf_op jit(solution)/shard_map/all_to_all | solution.py:172
  75.0 0.1 convert_reduce_fusion
  75.1 0.1 reshape.23
  75.2 0.6 copy.4
  (2 shorter events, 0.0 us)
Async XLA Ops:
  1.1 28.3 %collective-permute-start = (bf16[32,3072]{1,0:T(8,128)(2,1)S(1)}, bf16[32,3072]{1,0:T(8,128)(2,1)S(1)}, u32[]{:S(2)}, u32[]{:S(2)}) collective-permute-start(bf16[32,3072]{1,0:T(8,128)(2,1)S(1)} %reshape.19.block_ref), channel_id=1, source_target_pairs={{0,1},{1,0},{2,3},{3,2},{4,5},{5,4},{6,7},{7,6},{8,9},{9,8},{10,11... | collective-permute-start | bytes 589832 | tf_op jit(solution)/shard_map/ppermute | solution.py:162
  25.7 0.9 %copy-start = (f32[3,3,3,2,1,512]{5,4,3,2,1,0:T(1,128)S(1)}, f32[3,3,3,2,1,512]{5,4,3,2,1,0:T(1,128)}, u32[]{:S(2)}) copy-start(f32[3,3,3,2,1,512]{5,4,3,2,1,0:T(1,128)} %link_ref.1) | copy-start | bytes 331780
  29.4 18.3 %collective-permute-start.1 = (bf16[4,32,3072]{2,1,0:T(8,128)(2,1)}, bf16[4,32,3072]{2,1,0:T(8,128)(2,1)S(1)}, u32[]{:S(2)}, u32[]{:S(2)}) collective-permute-start(bf16[4,32,3072]{2,1,0:T(8,128)(2,1)} %get-tuple-element.18), channel_id=1, source_target_pairs={{0,8},{8,16},{16,24},{24,32},{32,40},{40,48},{48,56},{56,64},{64,7... | collective-permute-start | bytes 2359304 | tf_op jit(solution)/shard_map/ppermute | solution.py:168

commit v7 on v6

--- a/solution.py
+++ b/solution.py
@@ -96,18 +96,20 @@
     )(plane, block, links)
 
 
-def product_kernel(half_ref, left_ref, raised_ref, near_ref, far_ref, out_ref, both_ref):
-    def spread(source_ref):
+def product_kernel(where_ref, left_ref, raised_ref, *refs):
+    near_refs, (far_ref, out_ref, both_ref) = refs[:4], refs[4:]
+
+    def spread(source_ref, to, rows):
         for colour in range(3):
             at = 2 * SITES * colour
             real_vec = source_ref[:, at : at + SITES]
             imag_vec = source_ref[:, at + SITES : at + 2 * SITES]
-            both_ref[0:128, at : at + SITES] = real_vec
-            both_ref[0:128, at + SITES : at + 2 * SITES] = -imag_vec
-            both_ref[128:256, at : at + SITES] = imag_vec
-            both_ref[128:256, at + SITES : at + 2 * SITES] = real_vec
-
-    def multiply(source_ref, half, least, most):
+            both_ref[to : to + rows, at : at + SITES] = real_vec
+            both_ref[to : to + rows, at + SITES : at + 2 * SITES] = -imag_vec
+            both_ref[to + 128 : to + 128 + rows, at : at + SITES] = imag_vec
+            both_ref[to + 128 : to + 128 + rows, at + SITES : at + 2 * SITES] = real_vec
+
+    def multiply(source_ref, half, first, least, most):
         product = lax.dot_general(
             both_ref[...],
             source_ref[...],
@@ -122,25 +124,31 @@
         odd = jnp.where(upper, pltpu.roll(real_part, 4, 1), imag_part).astype(jnp.bfloat16)
         for block in range(4):
             for pair in range(4):
-                out_ref[block, half, 2 * pair, :, least:most] = even[4 * block + pair]
-                out_ref[block, half, 2 * pair + 1, :, least:most] = odd[4 * block + pair]
-
-    for source_ref, half in ((near_ref, half_ref[0]), (far_ref, 1 - half_ref[0])):
-        spread(source_ref)
-        multiply(left_ref, half, 0, 8 * ROWS)
-        multiply(raised_ref, half, 8 * ROWS, 12 * ROWS)
-
-
-def products(half, left, raised, near, far):
+                out_ref[first ^ block, half, 2 * pair, :, least:most] = even[4 * block + pair]
+                out_ref[first ^ block, half, 2 * pair + 1, :, least:most] = odd[4 * block + pair]
+
+    def multiply_all(half, first):
+        multiply(left_ref, half, first, 0, 8 * ROWS)
+        multiply(raised_ref, half, first, 8 * ROWS, 12 * ROWS)
+
+    half = where_ref[0]
+    for block in range(4):
+        spread(near_refs[block], ROWS * block, ROWS)
+    multiply_all(half, where_ref[1])
+    spread(far_ref, 0, 128)
+    multiply_all(1 - half, 0)
+
+
+def products(where, left, raised, near, far):
     return pl.pallas_call(
         product_kernel,
         out_shape=jax.ShapeDtypeStruct((4, 2, 8, 8, 12 * ROWS), jnp.bfloat16),
         in_specs=[pl.BlockSpec(memory_space=pltpu.SMEM)]
-        + [pl.BlockSpec(memory_space=pltpu.VMEM)] * 4,
+        + [pl.BlockSpec(memory_space=pltpu.VMEM)] * 7,
         out_specs=pl.BlockSpec(memory_space=pltpu.VMEM),
         scratch_shapes=[pltpu.VMEM((256, DEPTH), jnp.bfloat16)],
         compiler_params=pltpu.CompilerParams(vmem_limit_bytes=VMEM_BYTES),
-    )(half, left, raised, near, far)
+    )(where, left, raised, *near, far)
 
 
 def body(eigenvectors, gauge_links, momenta):
@@ -153,22 +161,26 @@
     column = lax.broadcasted_iota(jnp.int32, (5, 3), 1)
     plane = jnp.where(column == 0, s, space).astype(jnp.int32)
     plane = jnp.where(row < 4, jnp.pad(momenta, ((0, 1), (0, 0))), plane)
-    half = (e & 1).astype(jnp.int32).reshape(1)
+    where = jnp.stack([e & 1, e >> 1]).astype(jnp.int32)
     groups = [list(range(0, eig, 2)), list(range(1, eig, 2))]
 
-    def around_x(value):
-        return lax.all_gather(value, "eig", axis_index_groups=groups, tiled=True)
-
-    partner = lax.ppermute(block, "eig", [(a, a ^ 1) for a in range(eig)])
-    near = around_x(block)
-    near, plane = lax.optimization_barrier((near, plane))
+    def swapped(value, bits):
+        return lax.ppermute(value, "eig", [(a, a ^ bits) for a in range(eig)])
+
+    partner = swapped(block, 1)
+    first = swapped(block, 2)
+    third = swapped(block, 6)
     left, raised = left_operand(plane, block, gauge_links)
-
-    partner, near, left, raised = lax.optimization_barrier((partner, near, left, raised))
+    left, raised, first = lax.optimization_barrier((left, raised, first))
+    second = swapped(first, 6)
+    partner, first, second, third, raised = lax.optimization_barrier(
+        (partner, first, second, third, raised)
+    )
     raised = lax.ppermute(raised, "space", [(a, (a + 1) % space) for a in range(space)])
-    far = around_x(partner)
+    far = lax.all_gather(partner, "eig", axis_index_groups=groups, tiled=True)
     left, raised = left.reshape(8 * ROWS, DEPTH), raised.reshape(4 * ROWS, DEPTH)
-    chunks = products(half, left, raised, near, far).reshape(space, 8, 12 * ROWS)
+    near = (block, first, second, third)
+    chunks = products(where, left, raised, near, far).reshape(space, 8, 12 * ROWS)
     got = lax.all_to_all(chunks, "space", split_axis=0, concat_axis=0, tiled=True)
     total = jnp.sum(got.astype(jnp.float32), axis=0)
     return total.reshape(2, 4, 3, 4, ROWS).transpose(2, 3, 0, 4, 1)

time: 76.1 us -> 79.6 us (1.046)
  blocking collectives: 50.9 us -> 38.8 us
  starting transfers between devices: 16.7 us -> 26.5 us
  waiting for transfers between devices: 0.01 us -> 5.19 us
    all_gather x2 -> x1, blocking collectives: 25.4 us -> 12.8 us  [body(): far = lax.all_gather(partner, 'eig', axis_index_groups=groups, tiled=True)]
    ppermute x1 -> x4, starting transfers between devices: 11.5 us -> 21.1 us  [swapped(): return lax.ppermute(value, 'eig', [(a, a ^ bits) for a in range(eig)])]
    ppermute x1 -> x4, waiting for transfers between devices: 0.01 us -> 5.19 us  [swapped(): return lax.ppermute(value, 'eig', [(a, a ^ bits) for a in range(eig)])]
  transfers between devices with their start and end apart: 2 -> 5, of which waited for: 0 -> 1; matrix products, arithmetic and copies ran while one was open for 1% -> 1% of each run, Pallas kernels for 4% -> 3%
where the time goes in v7:
time: 79.6 us; the launch traced here: 79.3 us
  blocking collectives  38.8 us (49%)
  starting transfers between devices  26.5 us (33%)
  waiting for transfers between devices  5.19 us (7%)
  Pallas kernels  5.11 us (6%)
  local copies, waits for them, and re-layouts  2.67 us (3%)
  other arithmetic  0.92 us (1%)
    all_to_all x1, blocking collectives, body(): lax.all_to_all(chunks, 'space', split_axis=0, concat_axis=0, tiled=True)  26 us
    ppermute x4, starting transfers between devices, swapped(): return lax.ppermute(value, 'eig', [(a, a ^ bits) for a in range(eig)])  21.1 us
    all_gather x1, blocking collectives, body(): far = lax.all_gather(partner, 'eig', axis_index_groups=groups, tiled=True)  12.8 us
    ppermute x1, starting transfers between devices, body(): lax.ppermute(raised, 'space', [(a, (a + 1) % space) for a in range(space)])  5.42 us
    ppermute x4, waiting for transfers between devices, swapped(): return lax.ppermute(value, 'eig', [(a, a ^ bits) for a in range(eig)])  5.19 us
    pallas_call x1, Pallas kernels, left_operand(): pl.pallas_call(left_kernel, out_shape=[jax.ShapeDtypeStruct((8, ROWS, DEP...  2.77 us
    pallas_call x1, Pallas kernels, products(): pl.pallas_call(product_kernel, out_shape=jax.ShapeDtypeStruct((4, 2, 8, 8...  2.34 us
  transfers between devices with their start and end apart: 5, of which 1 were waited for; matrix products, arithmetic and copies ran while one was open for 1% of the time, Pallas kernels for 3%

profile of v7, /device:TPU:1, one launch (start us, length us, event | category | flops | bytes accessed | tf_op | source)
XLA Modules:
  0.0 79.3 jit_solution(2360974850468846066)
XLA Ops:
  0.0 1.1 %reshape.15.block_ref.refs_0_ = bf16[32,3072]{1,0:T(8,128)(2,1)S(1)} reshape(bf16[32,3,2,1,512]{4,2,3,1,0:T(2,128)(2,1)} %param.3) | data formatting | bytes 393216 | tf_op jit(solution)/shard_map/reshape | solution.py:159
  1.1 3.9 %collective-permute-start = (bf16[32,3072]{1,0:T(8,128)(2,1)S(1)}, bf16[32,3072]{1,0:T(8,128)(2,1)S(1)}, u32[]{:S(2)}, u32[]{:S(2)}) collective-permute-start(bf16[32,3072]{1,0:T(8,128)(2,1)S(1)} %reshape.15.block_ref.refs_0_), channel_id=1, source_target_pairs={{0,2},{1,3},{2,0},{3,1},{4,6},{5,7},{6,4},{7,5},{8,10},{9,11},{10,... | collective-permute-start | bytes 589832 | tf_op jit(solution)/shard_map/ppermute | solution.py:168
  5.0 10.6 %collective-permute-start.1 = (bf16[32,3072]{1,0:T(8,128)(2,1)S(1)}, bf16[32,3072]{1,0:T(8,128)(2,1)S(1)}, u32[]{:S(2)}, u32[]{:S(2)}) collective-permute-start(bf16[32,3072]{1,0:T(8,128)(2,1)S(1)} %reshape.15.block_ref.refs_0_), channel_id=1, source_target_pairs={{0,1},{1,0},{2,3},{3,2},{4,5},{5,4},{6,7},{7,6},{8,9},{9,8},{10,11... | collective-permute-start | bytes 589832 | tf_op jit(solution)/shard_map/ppermute | solution.py:168
  15.7 3.7 %collective-permute-start.3 = (bf16[32,3072]{1,0:T(8,128)(2,1)S(1)}, bf16[32,3072]{1,0:T(8,128)(2,1)S(1)}, u32[]{:S(2)}, u32[]{:S(2)}) collective-permute-start(bf16[32,3072]{1,0:T(8,128)(2,1)S(1)} %reshape.15.block_ref.refs_0_), channel_id=1, source_target_pairs={{0,6},{1,7},{2,4},{3,5},{4,2},{5,3},{6,0},{7,1},{8,14},{9,15},{10,... | collective-permute-start | bytes 589832 | tf_op jit(solution)/shard_map/ppermute | solution.py:168
  19.4 0.8 pad_select_fusion.plane_ref
  20.2 0.0 copy-start
  20.2 0.9 %copy-done = f32[3,3,3,2,1,512]{5,4,3,2,1,0:T(1,128)S(1)} copy-done((f32[3,3,3,2,1,512]{5,4,3,2,1,0:T(1,128)S(1)}, f32[3,3,3,2,1,512]{5,4,3,2,1,0:T(1,128)}, u32[]{:S(2)}) %copy-start) | copy-done | bytes 110616
  21.1 2.8 %shard_map.37 = (bf16[8,32,3072]{2,1,0:T(8,128)(2,1)S(1)}, bf16[4,32,3072]{2,1,0:T(8,128)(2,1)}) custom-call(s32[5,3]{1,0:T(8,128)S(1)} %pad_select_fusion.plane_ref, bf16[32,3072]{1,0:T(8,128)(2,1)S(1)} %reshape.15.block_ref.refs_0_, f32[3,3,3,2,1,512]{5,4,3,2,1,0:T(1,128)S(1)} %copy-done), custom_call_target="tpu_custom_call" | custom-call | tf_op jit(solution)/shard_map/pallas_call | solution.py:85
  23.8 0.0 collective-permute-done.refs_1_
  23.8 2.8 %collective-permute-start.2 = (bf16[32,3072]{1,0:T(8,128)(2,1)S(1)}, bf16[32,3072]{1,0:T(8,128)(2,1)S(1)}, u32[]{:S(2)}, u32[]{:S(2)}) collective-permute-start(bf16[32,3072]{1,0:T(8,128)(2,1)S(1)} %collective-permute-done.refs_1_), channel_id=1, source_target_pairs={{0,6},{1,7},{2,4},{3,5},{4,2},{5,3},{6,0},{7,1},{8,14},{9,15},{10,... | collective-permute-start | bytes 589832 | tf_op jit(solution)/shard_map/ppermute | solution.py:168
  26.6 0.0 collective-permute-done.1
  26.6 0.0 collective-permute-done.3.refs_3_
  26.6 5.2 %collective-permute-done.2.refs_2_ = bf16[32,3072]{1,0:T(8,128)(2,1)S(1)} collective-permute-done((bf16[32,3072]{1,0:T(8,128)(2,1)S(1)}, bf16[32,3072]{1,0:T(8,128)(2,1)S(1)}, u32[]{:S(2)}, u32[]{:S(2)}) %collective-permute-start.2) | collective-permute-done | bytes 196640 | tf_op jit(solution)/shard_map/ppermute | solution.py:168
  31.8 5.4 %collective-permute-start.4 = (bf16[4,32,3072]{2,1,0:T(8,128)(2,1)}, bf16[4,32,3072]{2,1,0:T(8,128)(2,1)S(1)}, u32[]{:S(2)}, u32[]{:S(2)}) collective-permute-start(bf16[4,32,3072]{2,1,0:T(8,128)(2,1)} %get-tuple-element.20), channel_id=1, source_target_pairs={{0,8},{8,16},{16,24},{24,32},{32,40},{40,48},{48,56},{56,64},{64,7... | collective-permute-start | bytes 2359304 | tf_op jit(solution)/shard_map/ppermute | solution.py:179
  37.2 0.1 pad_add_fusion.where_ref
  37.3 12.8 %all_gather.3.refs_4_ = bf16[128,3072]{1,0:T(8,128)(2,1)S(1)} all-gather(bf16[32,3072]{1,0:T(8,128)(2,1)S(1)} %collective-permute-done.1), channel_id=1, replica_groups={{0,2,4,6},{1,3,5,7},{8,10,12,14},{9,11,13,15},{16,18,20,22},{17,19,21,2..., dimensions={0}, use_global_device_ids=true | all-gather | bytes 983040 | tf_op jit(solution)/shard_map/all_gather | solution.py:180
  50.1 0.0 collective-permute-done.4
  50.1 2.3 %shard_map.38 = bf16[4,2,8,8,384]{4,3,2,1,0:T(8,128)(2,1)S(1)} custom-call(s32[2]{0:T(128)S(1)} %pad_add_fusion.where_ref, bf16[256,3072]{1,0:T(8,128)(2,1)S(1)} %bitcast.8, bf16[128,3072]{1,0:T(8,128)(2,1)S(1)} %bitcast.10, bf16[32,3072]{1,0:T(8,128)(2,1)S(1)} %reshape.15.block_ref.refs_0_, bf16[32,3072]{1,0:T(8,128)(2,1)S(1)} %collective-permute-done.refs_1_, ...), custom_call_target="tpu_custom_call" | custom-call | tf_op jit(solution)/shard_map/pallas_call | solution.py:143
  52.4 26.0 %all_to_all.5 = bf16[64,8,384]{2,1,0:T(8,128)(2,1)S(1)} all-to-all(bf16[64,8,384]{2,1,0:T(8,128)(2,1)S(1)} %bitcast.9), channel_id=1, replica_groups=mesh['space'=64,'eig'=8] {'space'}, dimensions={0} | all-to-all | bytes 786432 | tf_op jit(solution)/shard_map/all_to_all | solution.py:184
  78.5 0.1 convert_reduce_fusion
  78.5 0.1 reshape.19
  78.6 0.6 copy.4
  (2 shorter events, 0.0 us)
Async XLA Ops:
  1.1 22.8 %collective-permute-start = (bf16[32,3072]{1,0:T(8,128)(2,1)S(1)}, bf16[32,3072]{1,0:T(8,128)(2,1)S(1)}, u32[]{:S(2)}, u32[]{:S(2)}) collective-permute-start(bf16[32,3072]{1,0:T(8,128)(2,1)S(1)} %reshape.15.block_ref.refs_0_), channel_id=1, source_target_pairs={{0,2},{1,3},{2,0},{3,1},{4,6},{5,7},{6,4},{7,5},{8,10},{9,11},{10,... | collective-permute-start | bytes 589832 | tf_op jit(solution)/shard_map/ppermute | solution.py:168
  5.0 21.6 %collective-permute-start.1 = (bf16[32,3072]{1,0:T(8,128)(2,1)S(1)}, bf16[32,3072]{1,0:T(8,128)(2,1)S(1)}, u32[]{:S(2)}, u32[]{:S(2)}) collective-permute-start(bf16[32,3072]{1,0:T(8,128)(2,1)S(1)} %reshape.15.block_ref.refs_0_), channel_id=1, source_target_pairs={{0,1},{1,0},{2,3},{3,2},{4,5},{5,4},{6,7},{7,6},{8,9},{9,8},{10,11... | collective-permute-start | bytes 589832 | tf_op jit(solution)/shard_map/ppermute | solution.py:168
  15.7 11.0 %collective-permute-start.3 = (bf16[32,3072]{1,0:T(8,128)(2,1)S(1)}, bf16[32,3072]{1,0:T(8,128)(2,1)S(1)}, u32[]{:S(2)}, u32[]{:S(2)}) collective-permute-start(bf16[32,3072]{1,0:T(8,128)(2,1)S(1)} %reshape.15.block_ref.refs_0_), channel_id=1, source_target_pairs={{0,6},{1,7},{2,4},{3,5},{4,2},{5,3},{6,0},{7,1},{8,14},{9,15},{10,... | collective-permute-start | bytes 589832 | tf_op jit(solution)/shard_map/ppermute | solution.py:168
  20.2 0.9 %copy-start = (f32[3,3,3,2,1,512]{5,4,3,2,1,0:T(1,128)S(1)}, f32[3,3,3,2,1,512]{5,4,3,2,1,0:T(1,128)}, u32[]{:S(2)}) copy-start(f32[3,3,3,2,1,512]{5,4,3,2,1,0:T(1,128)} %link_ref.1) | copy-start | bytes 331780
  23.8 8.0 %collective-permute-start.2 = (bf16[32,3072]{1,0:T(8,128)(2,1)S(1)}, bf16[32,3072]{1,0:T(8,128)(2,1)S(1)}, u32[]{:S(2)}, u32[]{:S(2)}) collective-permute-start(bf16[32,3072]{1,0:T(8,128)(2,1)S(1)} %collective-permute-done.refs_1_), channel_id=1, source_target_pairs={{0,6},{1,7},{2,4},{3,5},{4,2},{5,3},{6,0},{7,1},{8,14},{9,15},{10,... | collective-permute-start | bytes 589832 | tf_op jit(solution)/shard_map/ppermute | solution.py:168
  31.8 18.3 %collective-permute-start.4 = (bf16[4,32,3072]{2,1,0:T(8,128)(2,1)}, bf16[4,32,3072]{2,1,0:T(8,128)(2,1)S(1)}, u32[]{:S(2)}, u32[]{:S(2)}) collective-permute-start(bf16[4,32,3072]{2,1,0:T(8,128)(2,1)} %get-tuple-element.20), channel_id=1, source_target_pairs={{0,8},{8,16},{16,24},{24,32},{32,40},{40,48},{48,56},{56,64},{64,7... | collective-permute-start | bytes 2359304 | tf_op jit(solution)/shard_map/ppermute | solution.py:179

commit v8 on v6

--- a/solution.py
+++ b/solution.py
@@ -157,7 +157,11 @@
     groups = [list(range(0, eig, 2)), list(range(1, eig, 2))]
 
     def around_x(value):
-        return lax.all_gather(value, "eig", axis_index_groups=groups, tiled=True)
+        copies = jnp.broadcast_to(value[None], (eig // 2, ROWS, DEPTH))
+        blocks = lax.all_to_all(
+            copies, "eig", split_axis=0, concat_axis=0, axis_index_groups=groups, tiled=True
+        )
+        return blocks.reshape(eig // 2 * ROWS, DEPTH)
 
     partner = lax.ppermute(block, "eig", [(a, a ^ 1) for a in range(eig)])
     near = around_x(block)

time: 76.1 us -> 76.1 us (level)
  blocking collectives: 50.9 us -> 27.3 us
  starting transfers between devices: 16.7 us -> 29.1 us
  waiting for transfers between devices: 0.01 us -> 9.66 us
  Pallas kernels: 4.6 us -> 5.71 us
  local copies, waits for them, and re-layouts: 2.67 us -> 3.76 us
    all_gather x2 -> x0, blocking collectives: 25.4 us -> none  [around_x(): return lax.all_gather(value, 'eig', axis_index_groups=groups, tiled=True)]
    all_to_all x0 -> x2, starting transfers between devices: none -> 9.08 us  [around_x(): lax.all_to_all(copies, 'eig', split_axis=0, concat_axis=0, axis_index_gro...]
    all_to_all x0 -> x2, waiting for transfers between devices: none -> 8.74 us  [around_x(): lax.all_to_all(copies, 'eig', split_axis=0, concat_axis=0, axis_index_gro...]
    ppermute x1, starting transfers between devices: 5.22 us -> 9.35 us  [body(): lax.ppermute(raised, 'space', [(a, (a + 1) % space) for a in range(space)])]
    broadcast_in_dim x0 -> x2, local copies, waits for them, and re-layouts: none -> 1.94 us  [around_x(): copies = jnp.broadcast_to(value[None], (eig // 2, ROWS, DEPTH))]
    all_to_all x1, blocking collectives: 25.5 us -> 27.3 us  [body(): lax.all_to_all(chunks, 'space', split_axis=0, concat_axis=0, tiled=True)]
    pallas_call x1, Pallas kernels: 1.8 us -> 2.93 us  [products(): pl.pallas_call(product_kernel, out_shape=jax.ShapeDtypeStruct((4, 2, 8, 8...]
    ppermute x1, waiting for transfers between devices: 0.01 us -> 0.92 us  [body(): partner = lax.ppermute(block, 'eig', [(a, a ^ 1) for a in range(eig)])]
  transfers between devices with their start and end apart: 2 -> 4, of which waited for: 0 -> 2; matrix products, arithmetic and copies ran while one was open for 1% -> 1% of each run, Pallas kernels for 4% -> 4%
where the time goes in v8:
time: 76.1 us; the launch traced here: 75.8 us
  starting transfers between devices  29.1 us (38%)
  blocking collectives  27.3 us (36%)
  waiting for transfers between devices  9.66 us (13%)
  Pallas kernels  5.71 us (8%)
  local copies, waits for them, and re-layouts  3.76 us (5%)
    all_to_all x1, blocking collectives, body(): lax.all_to_all(chunks, 'space', split_axis=0, concat_axis=0, tiled=True)  27.3 us
    ppermute x1, starting transfers between devices, body(): partner = lax.ppermute(block, 'eig', [(a, a ^ 1) for a in range(eig)])  10.6 us
    ppermute x1, starting transfers between devices, body(): lax.ppermute(raised, 'space', [(a, (a + 1) % space) for a in range(space)])  9.35 us
    all_to_all x2, starting transfers between devices, around_x(): lax.all_to_all(copies, 'eig', split_axis=0, concat_axis=0, axis_index_gro...  9.08 us
    all_to_all x2, waiting for transfers between devices, around_x(): lax.all_to_all(copies, 'eig', split_axis=0, concat_axis=0, axis_index_gro...  8.74 us
    pallas_call x1, Pallas kernels, products(): pl.pallas_call(product_kernel, out_shape=jax.ShapeDtypeStruct((4, 2, 8, 8...  2.93 us
    pallas_call x1, Pallas kernels, left_operand(): pl.pallas_call(left_kernel, out_shape=[jax.ShapeDtypeStruct((8, ROWS, DEP...  2.78 us
    broadcast_in_dim x2, local copies, waits for them, and re-layouts, around_x(): copies = jnp.broadcast_to(value[None], (eig // 2, ROWS, DEPTH))  1.94 us
  transfers between devices with their start and end apart: 4, of which 2 were waited for; matrix products, arithmetic and copies ran while one was open for 1% of the time, Pallas kernels for 4%

profile of v8, /device:TPU:1, one launch (start us, length us, event | category | flops | bytes accessed | tf_op | source)
XLA Modules:
  0.0 75.8 jit_solution(15031181229873690723)
XLA Ops:
  0.0 0.0 copy-start.1
  0.0 0.0 copy-start
  0.0 1.1 %reshape.27.block_ref = bf16[32,3072]{1,0:T(8,128)(2,1)S(1)} reshape(bf16[32,3,2,1,512]{4,2,3,1,0:T(2,128)(2,1)} %param.3) | data formatting | bytes 393216 | tf_op jit(solution)/shard_map/reshape | solution.py:151
  1.1 1.0 %broadcast_in_dim.19 = bf16[4,32,3072]{2,1,0:T(8,128)(2,1)} broadcast(bf16[32,3072]{1,0:T(8,128)(2,1)S(1)} %reshape.27.block_ref), dimensions={1,2} | broadcast | bytes 983040 | tf_op jit(solution)/shard_map/broadcast_in_dim | solution.py:160
  2.1 4.8 %all-to-all-start = ((bf16[4,32,3072]{2,1,0:T(8,128)(2,1)}), bf16[4,32,3072]{2,1,0:T(8,128)(2,1)S(1)}, u32[]{:S(2)}, u32[]{:S(2)}) async-start(bf16[4,32,3072]{2,1,0:T(8,128)(2,1)} %broadcast_in_dim.19), calls=%async_computation | async-start | bytes 1572864 | tf_op jit(solution)/shard_map/all_to_all | solution.py:161
  6.9 10.6 %collective-permute-start = (bf16[32,3072]{1,0:T(8,128)(2,1)S(1)}, bf16[32,3072]{1,0:T(8,128)(2,1)S(1)}, u32[]{:S(2)}, u32[]{:S(2)}) collective-permute-start(bf16[32,3072]{1,0:T(8,128)(2,1)S(1)} %reshape.27.block_ref), channel_id=1, source_target_pairs={{0,1},{1,0},{2,3},{3,2},{4,5},{5,4},{6,7},{7,6},{8,9},{9,8},{10,11... | collective-permute-start | bytes 589832 | tf_op jit(solution)/shard_map/ppermute | solution.py:166
  17.6 0.0 copy-done.1
  17.6 0.1 pad_select_fusion.plane_ref
  17.7 0.0 all-to-all-done
  17.7 0.0 copy-done
  17.7 2.8 %shard_map.37 = (bf16[8,32,3072]{2,1,0:T(8,128)(2,1)S(1)}, bf16[4,32,3072]{2,1,0:T(8,128)(2,1)}) custom-call(s32[5,3]{1,0:T(8,128)S(1)} %pad_select_fusion.plane_ref, bf16[32,3072]{1,0:T(8,128)(2,1)S(1)} %reshape.27.block_ref, f32[3,3,3,2,1,512]{5,4,3,2,1,0:T(1,128)S(1)} %copy-done), custom_call_target="tpu_custom_call" | custom-call | tf_op jit(solution)/shard_map/pallas_call | solution.py:85
  20.4 0.9 %collective-permute-done = bf16[32,3072]{1,0:T(8,128)(2,1)S(1)} collective-permute-done((bf16[32,3072]{1,0:T(8,128)(2,1)S(1)}, bf16[32,3072]{1,0:T(8,128)(2,1)S(1)}, u32[]{:S(2)}, u32[]{:S(2)}) %collective-permute-start) | collective-permute-done | bytes 196640 | tf_op jit(solution)/shard_map/ppermute | solution.py:166
  21.4 9.4 %collective-permute-start.1 = (bf16[4,32,3072]{2,1,0:T(8,128)(2,1)}, bf16[4,32,3072]{2,1,0:T(8,128)(2,1)}, u32[]{:S(2)}, u32[]{:S(2)}) collective-permute-start(bf16[4,32,3072]{2,1,0:T(8,128)(2,1)} %get-tuple-element.18), channel_id=1, source_target_pairs={{0,8},{8,16},{16,24},{24,32},{32,40},{40,48},{48,56},{56,64},{64,7... | collective-permute-start | bytes 2359304 | tf_op jit(solution)/shard_map/ppermute | solution.py:172
  30.7 1.0 %broadcast_in_dim.22 = bf16[4,32,3072]{2,1,0:T(8,128)(2,1)} broadcast(bf16[32,3072]{1,0:T(8,128)(2,1)S(1)} %collective-permute-done), dimensions={1,2} | broadcast | bytes 983040 | tf_op jit(solution)/shard_map/broadcast_in_dim | solution.py:160
  31.7 4.2 %all-to-all-start.1 = ((bf16[4,32,3072]{2,1,0:T(8,128)(2,1)}), bf16[4,32,3072]{2,1,0:T(8,128)(2,1)S(1)}, u32[]{:S(2)}, u32[]{:S(2)}) async-start(bf16[4,32,3072]{2,1,0:T(8,128)(2,1)} %broadcast_in_dim.22), calls=%async_computation.1 | async-start | bytes 1572864 | tf_op jit(solution)/shard_map/all_to_all | solution.py:161
  35.9 8.7 %all-to-all-done.1 = bf16[4,32,3072]{2,1,0:T(8,128)(2,1)S(1)} async-done(((bf16[4,32,3072]{2,1,0:T(8,128)(2,1)}), bf16[4,32,3072]{2,1,0:T(8,128)(2,1)S(1)}, u32[]{:S(2)}, u32[]{:S(2)}) %all-to-all-start.1) | async-done | bytes 786464 | tf_op jit(solution)/shard_map/all_to_all | solution.py:161
  44.7 0.0 collective-permute-done.1
  44.7 2.9 %shard_map.38 = bf16[4,2,8,8,384]{4,3,2,1,0:T(8,128)(2,1)S(1)} custom-call(s32[1]{0:T(128)} %bitcast.half_ref, bf16[256,3072]{1,0:T(8,128)(2,1)S(1)} %bitcast.11, bf16[128,3072]{1,0:T(8,128)(2,1)} %bitcast.3.raised_ref, bf16[128,3072]{1,0:T(8,128)(2,1)S(1)} %bitcast.9, bf16[128,3072]{1,0:T(8,128)(2,1)S(1)} %bitcast.10), custom_call_target="tpu_custom_call" | custom-call | tf_op jit(solution)/shard_map/pallas_call | solution.py:135
  47.6 27.3 %all_to_all.15 = bf16[64,8,384]{2,1,0:T(8,128)(2,1)S(1)} all-to-all(bf16[64,8,384]{2,1,0:T(8,128)(2,1)S(1)} %bitcast.12), channel_id=1, replica_groups=mesh['space'=64,'eig'=8] {'space'}, dimensions={0} | all-to-all | bytes 786432 | tf_op jit(solution)/shard_map/all_to_all | solution.py:176
  74.9 0.1 convert_reduce_fusion
  75.0 0.1 reshape.33
  75.1 0.6 copy.4
  (2 shorter events, 0.0 us)
Async XLA Ops:
  0.0 17.6 %copy-start.1 = (s32[4,3]{1,0:T(4,128)S(1)}, s32[4,3]{1,0:T(4,128)}, u32[]{:S(2)}) copy-start(s32[4,3]{1,0:T(4,128)} %param.5) | copy-start | bytes 148
  0.0 17.7 %copy-start = (f32[3,3,3,2,1,512]{5,4,3,2,1,0:T(1,128)S(1)}, f32[3,3,3,2,1,512]{5,4,3,2,1,0:T(1,128)}, u32[]{:S(2)}) copy-start(f32[3,3,3,2,1,512]{5,4,3,2,1,0:T(1,128)} %link_ref.1) | copy-start | bytes 331780
  2.1 15.6 %all-to-all-start = ((bf16[4,32,3072]{2,1,0:T(8,128)(2,1)}), bf16[4,32,3072]{2,1,0:T(8,128)(2,1)S(1)}, u32[]{:S(2)}, u32[]{:S(2)}) async-start(bf16[4,32,3072]{2,1,0:T(8,128)(2,1)} %broadcast_in_dim.19), calls=%async_computation | async-start | bytes 1572864 | tf_op jit(solution)/shard_map/all_to_all | solution.py:161
  6.9 14.5 %collective-permute-start = (bf16[32,3072]{1,0:T(8,128)(2,1)S(1)}, bf16[32,3072]{1,0:T(8,128)(2,1)S(1)}, u32[]{:S(2)}, u32[]{:S(2)}) collective-permute-start(bf16[32,3072]{1,0:T(8,128)(2,1)S(1)} %reshape.27.block_ref), channel_id=1, source_target_pairs={{0,1},{1,0},{2,3},{3,2},{4,5},{5,4},{6,7},{7,6},{8,9},{9,8},{10,11... | collective-permute-start | bytes 589832 | tf_op jit(solution)/shard_map/ppermute | solution.py:166
  21.4 23.3 %collective-permute-start.1 = (bf16[4,32,3072]{2,1,0:T(8,128)(2,1)}, bf16[4,32,3072]{2,1,0:T(8,128)(2,1)}, u32[]{:S(2)}, u32[]{:S(2)}) collective-permute-start(bf16[4,32,3072]{2,1,0:T(8,128)(2,1)} %get-tuple-element.18), channel_id=1, source_target_pairs={{0,8},{8,16},{16,24},{24,32},{32,40},{40,48},{48,56},{56,64},{64,7... | collective-permute-start | bytes 2359304 | tf_op jit(solution)/shard_map/ppermute | solution.py:172
  31.7 13.0 %all-to-all-start.1 = ((bf16[4,32,3072]{2,1,0:T(8,128)(2,1)}), bf16[4,32,3072]{2,1,0:T(8,128)(2,1)S(1)}, u32[]{:S(2)}, u32[]{:S(2)}) async-start(bf16[4,32,3072]{2,1,0:T(8,128)(2,1)} %broadcast_in_dim.22), calls=%async_computation.1 | async-start | bytes 1572864 | tf_op jit(solution)/shard_map/all_to_all | solution.py:161

commit v9 on v8

--- a/solution.py
+++ b/solution.py
@@ -96,8 +96,8 @@
     )(plane, block, links)
 
 
-def product_kernel(half_ref, left_ref, raised_ref, near_ref, far_ref, out_ref, both_ref):
-    def spread(source_ref):
+def multiply_blocks(left_ref, raised_ref, source_ref, both_ref, store):
+    def spread():
         for colour in range(3):
             at = 2 * SITES * colour
             real_vec = source_ref[:, at : at + SITES]
@@ -107,10 +107,10 @@
             both_ref[128:256, at : at + SITES] = imag_vec
             both_ref[128:256, at + SITES : at + 2 * SITES] = real_vec
 
-    def multiply(source_ref, half, least, most):
+    def multiply(operand_ref, least, most):
         product = lax.dot_general(
             both_ref[...],
-            source_ref[...],
+            operand_ref[...],
             (((1,), (1,)), ((), ())),
             preferred_element_type=jnp.float32,
         )
@@ -122,25 +122,42 @@
         odd = jnp.where(upper, pltpu.roll(real_part, 4, 1), imag_part).astype(jnp.bfloat16)
         for block in range(4):
             for pair in range(4):
-                out_ref[block, half, 2 * pair, :, least:most] = even[4 * block + pair]
-                out_ref[block, half, 2 * pair + 1, :, least:most] = odd[4 * block + pair]
-
-    for source_ref, half in ((near_ref, half_ref[0]), (far_ref, 1 - half_ref[0])):
-        spread(source_ref)
-        multiply(left_ref, half, 0, 8 * ROWS)
-        multiply(raised_ref, half, 8 * ROWS, 12 * ROWS)
-
-
-def products(half, left, raised, near, far):
+                store(block, 2 * pair, slice(least, most), even[4 * block + pair])
+                store(block, 2 * pair + 1, slice(least, most), odd[4 * block + pair])
+
+    spread()
+    multiply(left_ref, 0, 8 * ROWS)
+    multiply(raised_ref, 8 * ROWS, 12 * ROWS)
+
+
+def near_kernel(left_ref, raised_ref, near_ref, out_ref, both_ref):
+    def store(block, low, lanes, value):
+        out_ref[block, low, :, lanes] = value
+
+    multiply_blocks(left_ref, raised_ref, near_ref, both_ref, store)
+
+
+def far_kernel(half_ref, left_ref, raised_ref, far_ref, part_ref, out_ref, both_ref):
+    half = half_ref[0]
+
+    def store(block, low, lanes, value):
+        out_ref[block, 1 - half, low, :, lanes] = value
+
+    for block in range(4):
+        out_ref[block, half] = part_ref[block]
+    multiply_blocks(left_ref, raised_ref, far_ref, both_ref, store)
+
+
+def product_call(kernel, shape, scalars, *arrays):
     return pl.pallas_call(
-        product_kernel,
-        out_shape=jax.ShapeDtypeStruct((4, 2, 8, 8, 12 * ROWS), jnp.bfloat16),
-        in_specs=[pl.BlockSpec(memory_space=pltpu.SMEM)]
-        + [pl.BlockSpec(memory_space=pltpu.VMEM)] * 4,
+        kernel,
+        out_shape=jax.ShapeDtypeStruct(shape, jnp.bfloat16),
+        in_specs=[pl.BlockSpec(memory_space=pltpu.SMEM)] * len(scalars)
+        + [pl.BlockSpec(memory_space=pltpu.VMEM)] * len(arrays),
         out_specs=pl.BlockSpec(memory_space=pltpu.VMEM),
         scratch_shapes=[pltpu.VMEM((256, DEPTH), jnp.bfloat16)],
         compiler_params=pltpu.CompilerParams(vmem_limit_bytes=VMEM_BYTES),
-    )(half, left, raised, near, far)
+    )(*scalars, *arrays)
 
 
 def body(eigenvectors, gauge_links, momenta):
@@ -165,14 +182,16 @@
 
     partner = lax.ppermute(block, "eig", [(a, a ^ 1) for a in range(eig)])
     near = around_x(block)
-    near, plane = lax.optimization_barrier((near, plane))
     left, raised = left_operand(plane, block, gauge_links)
 
-    partner, near, left, raised = lax.optimization_barrier((partner, near, left, raised))
+    partner, left, raised = lax.optimization_barrier((partner, left, raised))
     raised = lax.ppermute(raised, "space", [(a, (a + 1) % space) for a in range(space)])
     far = around_x(partner)
     left, raised = left.reshape(8 * ROWS, DEPTH), raised.reshape(4 * ROWS, DEPTH)
-    chunks = products(half, left, raised, near, far).reshape(space, 8, 12 * ROWS)
+    part = product_call(near_kernel, (4, 8, 8, 12 * ROWS), (), left, raised, near)
+    chunks = product_call(
+        far_kernel, (4, 2, 8, 8, 12 * ROWS), (half,), left, raised, far, part
+    ).reshape(space, 8, 12 * ROWS)
     got = lax.all_to_all(chunks, "space", split_axis=0, concat_axis=0, tiled=True)
     total = jnp.sum(got.astype(jnp.float32), axis=0)
     return total.reshape(2, 4, 3, 4, ROWS).transpose(2, 3, 0, 4, 1)

time: 76.1 us -> 74.9 us (0.984)
  starting transfers between devices: 29.1 us -> 24.3 us
  Pallas kernels: 5.71 us -> 7.05 us
  blocking collectives: 27.3 us -> 28.6 us
  waiting for transfers between devices: 9.66 us -> 10.6 us
    ppermute x1, starting transfers between devices: 9.35 us -> 5.32 us  [body(): lax.ppermute(raised, 'space', [(a, (a + 1) % space) for a in range(space)])]
    ppermute x1, waiting for transfers between devices: 0.01 us -> 1.87 us  [body(): lax.ppermute(raised, 'space', [(a, (a + 1) % space) for a in range(space)])]
    all_to_all x2, starting transfers between devices: 9.08 us -> 7.51 us  [around_x(): lax.all_to_all(copies, 'eig', split_axis=0, concat_axis=0, axis_index_gro...]
    pallas_call x1 -> x2, Pallas kernels: 2.93 us -> 4.27 us  [product_call(): pl.pallas_call(kernel, out_shape=jax.ShapeDtypeStruct(shape, jnp.bfloat16...]
    all_to_all x1, blocking collectives: 27.3 us -> 28.6 us  [body(): lax.all_to_all(chunks, 'space', split_axis=0, concat_axis=0, tiled=True)]
    ppermute x1, waiting for transfers between devices: 0.92 us -> 0.01 us  [body(): partner = lax.ppermute(block, 'eig', [(a, a ^ 1) for a in range(eig)])]
    ppermute x1, starting transfers between devices: 10.6 us -> 11.5 us  [body(): partner = lax.ppermute(block, 'eig', [(a, a ^ 1) for a in range(eig)])]
  transfers between devices with their start and end apart: 4 -> 4, of which waited for: 2 -> 3; matrix products, arithmetic and copies ran while one was open for 1% -> 3% of each run, Pallas kernels for 4% -> 7%
where the time goes in v9:
time: 74.9 us; the launch traced here: 74.5 us
  blocking collectives  28.6 us (38%)
  starting transfers between devices  24.3 us (32%)
  waiting for transfers between devices  10.6 us (14%)
  Pallas kernels  7.05 us (9%)
  local copies, waits for them, and re-layouts  3.76 us (5%)
    all_to_all x1, blocking collectives, body(): lax.all_to_all(chunks, 'space', split_axis=0, concat_axis=0, tiled=True)  28.6 us
    ppermute x1, starting transfers between devices, body(): partner = lax.ppermute(block, 'eig', [(a, a ^ 1) for a in range(eig)])  11.5 us
    all_to_all x2, waiting for transfers between devices, around_x(): lax.all_to_all(copies, 'eig', split_axis=0, concat_axis=0, axis_index_gro...  8.7 us
    all_to_all x2, starting transfers between devices, around_x(): lax.all_to_all(copies, 'eig', split_axis=0, concat_axis=0, axis_index_gro...  7.51 us
    ppermute x1, starting transfers between devices, body(): lax.ppermute(raised, 'space', [(a, (a + 1) % space) for a in range(space)])  5.32 us
    pallas_call x2, Pallas kernels, product_call(): pl.pallas_call(kernel, out_shape=jax.ShapeDtypeStruct(shape, jnp.bfloat16...  4.27 us
    pallas_call x1, Pallas kernels, left_operand(): pl.pallas_call(left_kernel, out_shape=[jax.ShapeDtypeStruct((8, ROWS, DEP...  2.77 us
    broadcast_in_dim x2, local copies, waits for them, and re-layouts, around_x(): copies = jnp.broadcast_to(value[None], (eig // 2, ROWS, DEPTH))  1.94 us
  transfers between devices with their start and end apart: 4, of which 3 were waited for; matrix products, arithmetic and copies ran while one was open for 3% of the time, Pallas kernels for 7%

profile of v9, /device:TPU:1, one launch (start us, length us, event | category | flops | bytes accessed | tf_op | source)
XLA Modules:
  0.0 74.5 jit_solution(3998905264236496202)
XLA Ops:
  0.0 0.0 copy-start.1
  0.0 0.0 copy-start
  0.0 1.1 %reshape.27.block_ref = bf16[32,3072]{1,0:T(8,128)(2,1)S(1)} reshape(bf16[32,3,2,1,512]{4,2,3,1,0:T(2,128)(2,1)} %param.3) | data formatting | bytes 393216 | tf_op jit(solution)/shard_map/reshape | solution.py:168
  1.1 11.5 %collective-permute-start = (bf16[32,3072]{1,0:T(8,128)(2,1)S(1)}, bf16[32,3072]{1,0:T(8,128)(2,1)S(1)}, u32[]{:S(2)}, u32[]{:S(2)}) collective-permute-start(bf16[32,3072]{1,0:T(8,128)(2,1)S(1)} %reshape.27.block_ref), channel_id=1, source_target_pairs={{0,1},{1,0},{2,3},{3,2},{4,5},{5,4},{6,7},{7,6},{8,9},{9,8},{10,11... | collective-permute-start | bytes 589832 | tf_op jit(solution)/shard_map/ppermute | solution.py:183
  12.6 1.0 %broadcast_in_dim.22 = bf16[4,32,3072]{2,1,0:T(8,128)(2,1)} broadcast(bf16[32,3072]{1,0:T(8,128)(2,1)S(1)} %reshape.27.block_ref), dimensions={1,2} | broadcast | bytes 983040 | tf_op jit(solution)/shard_map/broadcast_in_dim | solution.py:177
  13.5 4.0 %all-to-all-start.1 = ((bf16[4,32,3072]{2,1,0:T(8,128)(2,1)}), bf16[4,32,3072]{2,1,0:T(8,128)(2,1)S(1)}, u32[]{:S(2)}, u32[]{:S(2)}) async-start(bf16[4,32,3072]{2,1,0:T(8,128)(2,1)} %broadcast_in_dim.22), calls=%async_computation.1 | async-start | bytes 1572864 | tf_op jit(solution)/shard_map/all_to_all | solution.py:178
  17.6 0.0 copy-done.1
  17.6 0.1 pad_select_fusion.plane_ref
  17.6 0.0 copy-done
  17.6 2.8 %shard_map.37 = (bf16[8,32,3072]{2,1,0:T(8,128)(2,1)S(1)}, bf16[4,32,3072]{2,1,0:T(8,128)(2,1)}) custom-call(s32[5,3]{1,0:T(8,128)S(1)} %pad_select_fusion.plane_ref, bf16[32,3072]{1,0:T(8,128)(2,1)S(1)} %reshape.27.block_ref, f32[3,3,3,2,1,512]{5,4,3,2,1,0:T(1,128)S(1)} %copy-done), custom_call_target="tpu_custom_call" | custom-call | tf_op jit(solution)/shard_map/pallas_call | solution.py:85
  20.4 0.0 collective-permute-done
  20.4 5.3 %collective-permute-start.1 = (bf16[4,32,3072]{2,1,0:T(8,128)(2,1)}, bf16[4,32,3072]{2,1,0:T(8,128)(2,1)}, u32[]{:S(2)}, u32[]{:S(2)}) collective-permute-start(bf16[4,32,3072]{2,1,0:T(8,128)(2,1)} %get-tuple-element.13), channel_id=1, source_target_pairs={{0,8},{8,16},{16,24},{24,32},{32,40},{40,48},{48,56},{56,64},{64,7... | collective-permute-start | bytes 2359304 | tf_op jit(solution)/shard_map/ppermute | solution.py:188
  25.8 2.9 %all-to-all-done.1 = bf16[4,32,3072]{2,1,0:T(8,128)(2,1)S(1)} async-done(((bf16[4,32,3072]{2,1,0:T(8,128)(2,1)}), bf16[4,32,3072]{2,1,0:T(8,128)(2,1)S(1)}, u32[]{:S(2)}, u32[]{:S(2)}) %all-to-all-start.1) | async-done | bytes 786464 | tf_op jit(solution)/shard_map/all_to_all | solution.py:178
  28.6 1.0 %broadcast_in_dim.21 = bf16[4,32,3072]{2,1,0:T(8,128)(2,1)} broadcast(bf16[32,3072]{1,0:T(8,128)(2,1)S(1)} %collective-permute-done), dimensions={1,2} | broadcast | bytes 983040 | tf_op jit(solution)/shard_map/broadcast_in_dim | solution.py:177
  29.6 3.5 %all-to-all-start = ((bf16[4,32,3072]{2,1,0:T(8,128)(2,1)}), bf16[4,32,3072]{2,1,0:T(8,128)(2,1)S(1)}, u32[]{:S(2)}, u32[]{:S(2)}) async-start(bf16[4,32,3072]{2,1,0:T(8,128)(2,1)} %broadcast_in_dim.21), calls=%async_computation | async-start | bytes 1572864 | tf_op jit(solution)/shard_map/all_to_all | solution.py:178
  33.1 1.9 %collective-permute-done.1 = bf16[4,32,3072]{2,1,0:T(8,128)(2,1)} collective-permute-done((bf16[4,32,3072]{2,1,0:T(8,128)(2,1)}, bf16[4,32,3072]{2,1,0:T(8,128)(2,1)}, u32[]{:S(2)}, u32[]{:S(2)}) %collective-permute-start.1) | collective-permute-done | bytes 786464 | tf_op jit(solution)/shard_map/ppermute | solution.py:188
  35.0 2.1 %shard_map.38.part_ref = bf16[4,8,8,384]{3,2,1,0:T(8,128)(2,1)S(1)} custom-call(bf16[256,3072]{1,0:T(8,128)(2,1)S(1)} %bitcast.9, bf16[128,3072]{1,0:T(8,128)(2,1)} %bitcast.2.raised_ref, bf16[128,3072]{1,0:T(8,128)(2,1)S(1)} %bitcast.11), custom_call_target="tpu_custom_call" | custom-call | tf_op jit(solution)/shard_map/pallas_call | solution.py:152
  37.1 5.8 %all-to-all-done = bf16[4,32,3072]{2,1,0:T(8,128)(2,1)S(1)} async-done(((bf16[4,32,3072]{2,1,0:T(8,128)(2,1)}), bf16[4,32,3072]{2,1,0:T(8,128)(2,1)S(1)}, u32[]{:S(2)}, u32[]{:S(2)}) %all-to-all-start) | async-done | bytes 786464 | tf_op jit(solution)/shard_map/all_to_all | solution.py:178
  42.9 2.1 %shard_map.39 = bf16[4,2,8,8,384]{4,3,2,1,0:T(8,128)(2,1)S(1)} custom-call(s32[1]{0:T(128)} %bitcast.half_ref, bf16[256,3072]{1,0:T(8,128)(2,1)S(1)} %bitcast.10, bf16[128,3072]{1,0:T(8,128)(2,1)} %bitcast.2.raised_ref, bf16[128,3072]{1,0:T(8,128)(2,1)S(1)} %bitcast.12, bf16[4,8,8,384]{3,2,1,0:T(8,128)(2,1)S(1)} %shard_map.38.part_ref), custom_call_target="tpu_custom_call" | custom-call | tf_op jit(solution)/shard_map/pallas_call | solution.py:152
  45.1 28.6 %all_to_all.15 = bf16[64,8,384]{2,1,0:T(8,128)(2,1)S(1)} all-to-all(bf16[64,8,384]{2,1,0:T(8,128)(2,1)S(1)} %bitcast.13), channel_id=1, replica_groups=mesh['space'=64,'eig'=8] {'space'}, dimensions={0} | all-to-all | bytes 786432 | tf_op jit(solution)/shard_map/all_to_all | solution.py:195
  73.7 0.1 convert_reduce_fusion
  73.8 0.1 reshape.33
  73.9 0.6 copy.4
  (2 shorter events, 0.0 us)
Async XLA Ops:
  0.0 17.6 %copy-start.1 = (s32[4,3]{1,0:T(4,128)S(1)}, s32[4,3]{1,0:T(4,128)}, u32[]{:S(2)}) copy-start(s32[4,3]{1,0:T(4,128)} %param.5) | copy-start | bytes 148
  0.0 17.6 %copy-start = (f32[3,3,3,2,1,512]{5,4,3,2,1,0:T(1,128)S(1)}, f32[3,3,3,2,1,512]{5,4,3,2,1,0:T(1,128)}, u32[]{:S(2)}) copy-start(f32[3,3,3,2,1,512]{5,4,3,2,1,0:T(1,128)} %link_ref.1) | copy-start | bytes 331780
  1.1 19.3 %collective-permute-start = (bf16[32,3072]{1,0:T(8,128)(2,1)S(1)}, bf16[32,3072]{1,0:T(8,128)(2,1)S(1)}, u32[]{:S(2)}, u32[]{:S(2)}) collective-permute-start(bf16[32,3072]{1,0:T(8,128)(2,1)S(1)} %reshape.27.block_ref), channel_id=1, source_target_pairs={{0,1},{1,0},{2,3},{3,2},{4,5},{5,4},{6,7},{7,6},{8,9},{9,8},{10,11... | collective-permute-start | bytes 589832 | tf_op jit(solution)/shard_map/ppermute | solution.py:183
  13.5 15.1 %all-to-all-start.1 = ((bf16[4,32,3072]{2,1,0:T(8,128)(2,1)}), bf16[4,32,3072]{2,1,0:T(8,128)(2,1)S(1)}, u32[]{:S(2)}, u32[]{:S(2)}) async-start(bf16[4,32,3072]{2,1,0:T(8,128)(2,1)} %broadcast_in_dim.22), calls=%async_computation.1 | async-start | bytes 1572864 | tf_op jit(solution)/shard_map/all_to_all | solution.py:178
  20.4 14.6 %collective-permute-start.1 = (bf16[4,32,3072]{2,1,0:T(8,128)(2,1)}, bf16[4,32,3072]{2,1,0:T(8,128)(2,1)}, u32[]{:S(2)}, u32[]{:S(2)}) collective-permute-start(bf16[4,32,3072]{2,1,0:T(8,128)(2,1)} %get-tuple-element.13), channel_id=1, source_target_pairs={{0,8},{8,16},{16,24},{24,32},{32,40},{40,48},{48,56},{56,64},{64,7... | collective-permute-start | bytes 2359304 | tf_op jit(solution)/shard_map/ppermute | solution.py:188
  29.6 13.3 %all-to-all-start = ((bf16[4,32,3072]{2,1,0:T(8,128)(2,1)}), bf16[4,32,3072]{2,1,0:T(8,128)(2,1)S(1)}, u32[]{:S(2)}, u32[]{:S(2)}) async-start(bf16[4,32,3072]{2,1,0:T(8,128)(2,1)} %broadcast_in_dim.21), calls=%async_computation | async-start | bytes 1572864 | tf_op jit(solution)/shard_map/all_to_all | solution.py:178

commit v10 on v6

--- a/solution.py
+++ b/solution.py
@@ -156,17 +156,17 @@
     half = (e & 1).astype(jnp.int32).reshape(1)
     groups = [list(range(0, eig, 2)), list(range(1, eig, 2))]
 
-    def around_x(value):
-        return lax.all_gather(value, "eig", axis_index_groups=groups, tiled=True)
-
     partner = lax.ppermute(block, "eig", [(a, a ^ 1) for a in range(eig)])
-    near = around_x(block)
-    near, plane = lax.optimization_barrier((near, plane))
+    copies = jnp.broadcast_to(block[None], (eig // 2, ROWS, DEPTH))
+    near = lax.all_to_all(
+        copies, "eig", split_axis=0, concat_axis=0, axis_index_groups=groups, tiled=True
+    ).reshape(eig // 2 * ROWS, DEPTH)
     left, raised = left_operand(plane, block, gauge_links)
 
-    partner, near, left, raised = lax.optimization_barrier((partner, near, left, raised))
+    partner, left, raised = lax.optimization_barrier((partner, left, raised))
     raised = lax.ppermute(raised, "space", [(a, (a + 1) % space) for a in range(space)])
-    far = around_x(partner)
+    partner, near = lax.optimization_barrier((partner, near))
+    far = lax.all_gather(partner, "eig", axis_index_groups=groups, tiled=True)
     left, raised = left.reshape(8 * ROWS, DEPTH), raised.reshape(4 * ROWS, DEPTH)
     chunks = products(half, left, raised, near, far).reshape(space, 8, 12 * ROWS)
     got = lax.all_to_all(chunks, "space", split_axis=0, concat_axis=0, tiled=True)

time: 76.1 us -> 72.8 us (0.957)
  blocking collectives: 50.9 us -> 41.2 us
  starting transfers between devices: 16.7 us -> 20.8 us
  waiting for transfers between devices: 0.01 us -> 2.89 us
    all_gather x2 -> x1, blocking collectives: 25.4 us -> 12 us  [body(): far = lax.all_gather(partner, 'eig', axis_index_groups=groups, tiled=True)]
    all_to_all x0 -> x1, starting transfers between devices: none -> 4.01 us  [body(): lax.all_to_all(copies, 'eig', split_axis=0, concat_axis=0, axis_index_gro...]
    all_to_all x1, blocking collectives: 25.5 us -> 29.3 us  [body(): lax.all_to_all(chunks, 'space', split_axis=0, concat_axis=0, tiled=True)]
    all_to_all x0 -> x1, waiting for transfers between devices: none -> 2.89 us  [body(): lax.all_to_all(copies, 'eig', split_axis=0, concat_axis=0, axis_index_gro...]
    broadcast_in_dim x0 -> x1, local copies, waits for them, and re-layouts: none -> 0.98 us  [body(): copies = jnp.broadcast_to(block[None], (eig // 2, ROWS, DEPTH))]
    unnamed x2 -> x4, local copies, waits for them, and re-layouts: 0.9 us -> 0.01 us
  transfers between devices with their start and end apart: 2 -> 3, of which waited for: 0 -> 1; matrix products, arithmetic and copies ran while one was open for 1% -> 1% of each run, Pallas kernels for 4% -> 4%
where the time goes in v10:
time: 72.8 us; the launch traced here: 72.5 us
  blocking collectives  41.2 us (57%)
  starting transfers between devices  20.8 us (29%)
  Pallas kernels  4.58 us (6%)
  waiting for transfers between devices  2.89 us (4%)
  local copies, waits for them, and re-layouts  2.79 us (4%)
    all_to_all x1, blocking collectives, body(): lax.all_to_all(chunks, 'space', split_axis=0, concat_axis=0, tiled=True)  29.3 us
    all_gather x1, blocking collectives, body(): far = lax.all_gather(partner, 'eig', axis_index_groups=groups, tiled=True)  12 us
    ppermute x1, starting transfers between devices, body(): partner = lax.ppermute(block, 'eig', [(a, a ^ 1) for a in range(eig)])  11.5 us
    ppermute x1, starting transfers between devices, body(): lax.ppermute(raised, 'space', [(a, (a + 1) % space) for a in range(space)])  5.31 us
    all_to_all x1, starting transfers between devices, body(): lax.all_to_all(copies, 'eig', split_axis=0, concat_axis=0, axis_index_gro...  4.01 us
    all_to_all x1, waiting for transfers between devices, body(): lax.all_to_all(copies, 'eig', split_axis=0, concat_axis=0, axis_index_gro...  2.89 us
    pallas_call x1, Pallas kernels, left_operand(): pl.pallas_call(left_kernel, out_shape=[jax.ShapeDtypeStruct((8, ROWS, DEP...  2.77 us
    pallas_call x1, Pallas kernels, products(): pl.pallas_call(product_kernel, out_shape=jax.ShapeDtypeStruct((4, 2, 8, 8...  1.8 us
  transfers between devices with their start and end apart: 3, of which 1 were waited for; matrix products, arithmetic and copies ran while one was open for 1% of the time, Pallas kernels for 4%

profile of v10, /device:TPU:1, one launch (start us, length us, event | category | flops | bytes accessed | tf_op | source)
XLA Modules:
  0.0 72.5 jit_solution(3813776787287770839)
XLA Ops:
  0.0 0.0 copy-start.1
  0.0 0.0 copy-start
  0.0 1.1 %reshape.23.block_ref = bf16[32,3072]{1,0:T(8,128)(2,1)S(1)} reshape(bf16[32,3,2,1,512]{4,2,3,1,0:T(2,128)(2,1)} %param.3) | data formatting | bytes 393216 | tf_op jit(solution)/shard_map/reshape | solution.py:151
  1.1 11.5 %collective-permute-start = (bf16[32,3072]{1,0:T(8,128)(2,1)S(1)}, bf16[32,3072]{1,0:T(8,128)(2,1)S(1)}, u32[]{:S(2)}, u32[]{:S(2)}) collective-permute-start(bf16[32,3072]{1,0:T(8,128)(2,1)S(1)} %reshape.23.block_ref), channel_id=1, source_target_pairs={{0,1},{1,0},{2,3},{3,2},{4,5},{5,4},{6,7},{7,6},{8,9},{9,8},{10,11... | collective-permute-start | bytes 589832 | tf_op jit(solution)/shard_map/ppermute | solution.py:159
  12.6 1.0 %broadcast_in_dim.15 = bf16[4,32,3072]{2,1,0:T(8,128)(2,1)} broadcast(bf16[32,3072]{1,0:T(8,128)(2,1)S(1)} %reshape.23.block_ref), dimensions={1,2} | broadcast | bytes 983040 | tf_op jit(solution)/shard_map/broadcast_in_dim | solution.py:160
  13.5 4.0 %all-to-all-start = ((bf16[4,32,3072]{2,1,0:T(8,128)(2,1)}), bf16[4,32,3072]{2,1,0:T(8,128)(2,1)S(1)}, u32[]{:S(2)}, u32[]{:S(2)}) async-start(bf16[4,32,3072]{2,1,0:T(8,128)(2,1)} %broadcast_in_dim.15), calls=%async_computation | async-start | bytes 1572864 | tf_op jit(solution)/shard_map/all_to_all | solution.py:161
  17.6 0.0 copy-done.1
  17.6 0.1 pad_select_fusion.plane_ref
  17.7 0.0 copy-done
  17.7 2.8 %shard_map.37 = (bf16[8,32,3072]{2,1,0:T(8,128)(2,1)S(1)}, bf16[4,32,3072]{2,1,0:T(8,128)(2,1)}) custom-call(s32[5,3]{1,0:T(8,128)S(1)} %pad_select_fusion.plane_ref, bf16[32,3072]{1,0:T(8,128)(2,1)S(1)} %reshape.23.block_ref, f32[3,3,3,2,1,512]{5,4,3,2,1,0:T(1,128)S(1)} %copy-done), custom_call_target="tpu_custom_call" | custom-call | tf_op jit(solution)/shard_map/pallas_call | solution.py:85
  20.4 0.0 collective-permute-done
  20.4 5.3 %collective-permute-start.1 = (bf16[4,32,3072]{2,1,0:T(8,128)(2,1)}, bf16[4,32,3072]{2,1,0:T(8,128)(2,1)S(1)}, u32[]{:S(2)}, u32[]{:S(2)}) collective-permute-start(bf16[4,32,3072]{2,1,0:T(8,128)(2,1)} %get-tuple-element.15), channel_id=1, source_target_pairs={{0,8},{8,16},{16,24},{24,32},{32,40},{40,48},{48,56},{56,64},{64,7... | collective-permute-start | bytes 2359304 | tf_op jit(solution)/shard_map/ppermute | solution.py:167
  25.8 2.9 %all-to-all-done = bf16[4,32,3072]{2,1,0:T(8,128)(2,1)S(1)} async-done(((bf16[4,32,3072]{2,1,0:T(8,128)(2,1)}), bf16[4,32,3072]{2,1,0:T(8,128)(2,1)S(1)}, u32[]{:S(2)}, u32[]{:S(2)}) %all-to-all-start) | async-done | bytes 786464 | tf_op jit(solution)/shard_map/all_to_all | solution.py:161
  28.6 12.0 %all_gather.3.far_ref = bf16[128,3072]{1,0:T(8,128)(2,1)S(1)} all-gather(bf16[32,3072]{1,0:T(8,128)(2,1)S(1)} %collective-permute-done), channel_id=1, replica_groups={{0,2,4,6},{1,3,5,7},{8,10,12,14},{9,11,13,15},{16,18,20,22},{17,19,21,2..., dimensions={0}, use_global_device_ids=true | all-gather | bytes 983040 | tf_op jit(solution)/shard_map/all_gather | solution.py:169
  40.6 0.0 collective-permute-done.1
  40.6 1.8 %shard_map.38 = bf16[4,2,8,8,384]{4,3,2,1,0:T(8,128)(2,1)S(1)} custom-call(s32[1]{0:T(128)} %bitcast.half_ref, bf16[256,3072]{1,0:T(8,128)(2,1)S(1)} %bitcast.9, bf16[128,3072]{1,0:T(8,128)(2,1)S(1)} %bitcast.11, bf16[128,3072]{1,0:T(8,128)(2,1)S(1)} %bitcast.8, bf16[128,3072]{1,0:T(8,128)(2,1)S(1)} %all_gather.3.far_ref), custom_call_target="tpu_custom_call" | custom-call | tf_op jit(solution)/shard_map/pallas_call | solution.py:135
  42.4 29.3 %all_to_all.10 = bf16[64,8,384]{2,1,0:T(8,128)(2,1)S(1)} all-to-all(bf16[64,8,384]{2,1,0:T(8,128)(2,1)S(1)} %bitcast.10), channel_id=1, replica_groups=mesh['space'=64,'eig'=8] {'space'}, dimensions={0} | all-to-all | bytes 786432 | tf_op jit(solution)/shard_map/all_to_all | solution.py:172
  71.7 0.1 convert_reduce_fusion
  71.8 0.1 reshape.28
  71.9 0.6 copy.4
  (2 shorter events, 0.0 us)
Async XLA Ops:
  0.0 17.6 %copy-start.1 = (s32[4,3]{1,0:T(4,128)S(1)}, s32[4,3]{1,0:T(4,128)}, u32[]{:S(2)}) copy-start(s32[4,3]{1,0:T(4,128)} %param.5) | copy-start | bytes 148
  0.0 17.7 %copy-start = (f32[3,3,3,2,1,512]{5,4,3,2,1,0:T(1,128)S(1)}, f32[3,3,3,2,1,512]{5,4,3,2,1,0:T(1,128)}, u32[]{:S(2)}) copy-start(f32[3,3,3,2,1,512]{5,4,3,2,1,0:T(1,128)} %link_ref.1) | copy-start | bytes 331780
  1.1 19.3 %collective-permute-start = (bf16[32,3072]{1,0:T(8,128)(2,1)S(1)}, bf16[32,3072]{1,0:T(8,128)(2,1)S(1)}, u32[]{:S(2)}, u32[]{:S(2)}) collective-permute-start(bf16[32,3072]{1,0:T(8,128)(2,1)S(1)} %reshape.23.block_ref), channel_id=1, source_target_pairs={{0,1},{1,0},{2,3},{3,2},{4,5},{5,4},{6,7},{7,6},{8,9},{9,8},{10,11... | collective-permute-start | bytes 589832 | tf_op jit(solution)/shard_map/ppermute | solution.py:159
  13.5 15.1 %all-to-all-start = ((bf16[4,32,3072]{2,1,0:T(8,128)(2,1)}), bf16[4,32,3072]{2,1,0:T(8,128)(2,1)S(1)}, u32[]{:S(2)}, u32[]{:S(2)}) async-start(bf16[4,32,3072]{2,1,0:T(8,128)(2,1)} %broadcast_in_dim.15), calls=%async_computation | async-start | bytes 1572864 | tf_op jit(solution)/shard_map/all_to_all | solution.py:161
  20.4 20.2 %collective-permute-start.1 = (bf16[4,32,3072]{2,1,0:T(8,128)(2,1)}, bf16[4,32,3072]{2,1,0:T(8,128)(2,1)S(1)}, u32[]{:S(2)}, u32[]{:S(2)}) collective-permute-start(bf16[4,32,3072]{2,1,0:T(8,128)(2,1)} %get-tuple-element.15), channel_id=1, source_target_pairs={{0,8},{8,16},{16,24},{24,32},{32,40},{40,48},{48,56},{56,64},{64,7... | collective-permute-start | bytes 2359304 | tf_op jit(solution)/shard_map/ppermute | solution.py:167

commit v11 on v5

v11 whole, which is shorter than its diff:
```python
import math

import jax
import jax.numpy as jnp
from jax import lax
from jax.experimental import pallas as pl
from jax.experimental.pallas import tpu as pltpu
from jax.sharding import PartitionSpec as P

LX = 64
LY = 8
SITES = LX * LY
ROWS = 32
DEPTH = 6 * SITES
VMEM_BYTES = 40 * 1024 * 1024


def moved_across(field):
    lane = lax.broadcasted_iota(jnp.int32, field.shape, 1)
    return jnp.where(
        lane % LX == 0, pltpu.roll(field, SITES - LX + 1, 1), pltpu.roll(field, 1, 1)
    )


def moved_along(field):
    return pltpu.roll(field, LX, 1)


MOVES = (moved_across, moved_along, lambda field: field)


def left_kernel(plane_ref, which_ref, block_ref, below_ref, link_ref, link_below_ref, left_ref, table_ref):
    row = lax.broadcasted_iota(jnp.int32, (8, SITES), 0) % 4
    site = lax.broadcasted_iota(jnp.int32, (8, SITES), 1)

    def component(k):
        value = jnp.full((8, SITES), plane_ref[3, k], jnp.int32)
        for p in range(3):
            value = jnp.where(row == p, plane_ref[p, k], value)
        return value

    x_frac = ((component(0) * (site % LX)) & (LX - 1)).astype(jnp.float32) / LX
    y_frac = ((component(1) * (site // LX)) & (LY - 1)).astype(jnp.float32) / LY
    extent = plane_ref[4, 1]
    first = lax.broadcasted_iota(jnp.int32, (8, SITES), 0) < 4

    def plane_table(height):
        z_frac = ((component(2) * height) & (extent - 1)).astype(jnp.float32)
        z_frac = z_frac / extent.astype(jnp.float32)
        angles = 2.0 * math.pi * (x_frac + y_frac + z_frac)
        return jnp.where(first, jnp.cos(angles), jnp.sin(angles))

    here = plane_table(plane_ref[4, 0])
    table_ref[0] = moved_across(here)
    table_ref[1] = moved_along(here)
    table_ref[2] = plane_table((plane_ref[4, 0] - 1) & (extent - 1))

    here_ref = block_ref.at[which_ref[0]] if len(block_ref.shape) == 3 else block_ref

    def rows_of(group, carry):
        rows = pl.ds(pl.multiple_of(group * 16, 16), 16)
        for d in range(3):
            source_ref = below_ref if d == 2 else here_ref
            for out_colour in range(3):
                real_base = jnp.zeros((16, SITES), jnp.float32)
                imag_base = jnp.zeros((16, SITES), jnp.float32)
                for colour in range(3):
                    at = 2 * SITES * colour
                    real_vec = source_ref[rows, at : at + SITES].astype(jnp.float32)
                    imag_vec = source_ref[rows, at + SITES : at + 2 * SITES].astype(jnp.float32)
                    if d == 2:
                        real_link = link_below_ref[2, colour, out_colour, 0]
                        imag_link = link_below_ref[2, colour, out_colour, 1]
                    else:
                        real_link = link_ref[d, colour, out_colour, 0]
                        imag_link = link_ref[d, colour, out_colour, 1]
                    real_base += real_vec * real_link + imag_vec * imag_link
                    imag_base += real_vec * imag_link - imag_vec * real_link
                real_base, imag_base = MOVES[d](real_base), MOVES[d](imag_base)
                at = 2 * SITES * out_colour
                for p in range(4):
                    cosine = table_ref[d, p : p + 1, :]
                    sine = table_ref[d, p + 4 : p + 5, :]
                    left_ref[4 * d + p, rows, at : at + SITES] = (
                        real_base * cosine + imag_base * sine
                    ).astype(jnp.bfloat16)
                    left_ref[4 * d + p, rows, at + SITES : at + 2 * SITES] = (
                        imag_base * cosine - real_base * sine
                    ).astype(jnp.bfloat16)
        return carry

    lax.fori_loop(0, ROWS // 16, rows_of, 0)


def left_operand(plane, which, blocks, below, links, links_below):
    return pl.pallas_call(
        left_kernel,
        out_shape=jax.ShapeDtypeStruct((12, ROWS, DEPTH), jnp.bfloat16),
        in_specs=[pl.BlockSpec(memory_space=pltpu.SMEM)] * 2
        + [pl.BlockSpec(memory_space=pltpu.VMEM)] * 4,
        out_specs=pl.BlockSpec(memory_space=pltpu.VMEM),
        scratch_shapes=[pltpu.VMEM((3, 8, SITES), jnp.float32)],
        compiler_params=pltpu.CompilerParams(vmem_limit_bytes=VMEM_BYTES),
    )(plane, which, blocks, below, links, links_below)


def product_kernel(where_ref, own_ref, other_ref, near_ref, far_ref, far_next_ref, out_ref, both_ref):
    def spread(source_ref, to, shift, rows):
        real_rows = slice(to, to + rows)
        imag_rows = slice(to + shift, to + shift + rows)
        for colour in range(3):
            at = 2 * SITES * colour
            real_vec = source_ref[:, at : at + SITES]
            imag_vec = source_ref[:, at + SITES : at + 2 * SITES]
            both_ref[real_rows, at : at + SITES] = real_vec
            both_ref[real_rows, at + SITES : at + 2 * SITES] = -imag_vec
            both_ref[imag_rows, at : at + SITES] = imag_vec
            both_ref[imag_rows, at + SITES : at + 2 * SITES] = real_vec

    def multiply(left_ref, columns, half, places):
        product = lax.dot_general(
            both_ref[0 : 2 * columns],
            left_ref[...],
            (((1,), (1,)), ((), ())),
            preferred_element_type=jnp.float32,
        )
        shape = (columns // 8, 8, 12 * ROWS)
        real_part = product[0:columns].reshape(shape)
        imag_part = product[columns : 2 * columns].reshape(shape)
        upper = lax.broadcasted_iota(jnp.int32, shape, 1) < 4
        even = jnp.where(upper, real_part, pltpu.roll(imag_part, 4, 1)).astype(jnp.bfloat16)
        odd = jnp.where(upper, pltpu.roll(real_part, 4, 1), imag_part).astype(jnp.bfloat16)
        for block, place in enumerate(places):
            for pair in range(4):
                out_ref[place, half, 2 * pair] = even[4 * block + pair]
                out_ref[place, half, 2 * pair + 1] = odd[4 * block + pair]

    half, x = where_ref[0], where_ref[1]
    spread(near_ref, 0, 128, 128)
    multiply(own_ref, 128, half, (0, 1, 2, 3))
    spread(far_ref, 0, 64, ROWS)
    spread(far_next_ref, ROWS, 64, ROWS)
    multiply(own_ref, 64, 1 - half, (x, x ^ 3))
    multiply(other_ref, 64, 1 - half, (x ^ 1, x ^ 2))


def products(where, own, other, near, far, far_next):
    return pl.pallas_call(
        product_kernel,
        out_shape=jax.ShapeDtypeStruct((4, 2, 8, 8, 12 * ROWS), jnp.bfloat16),
        in_specs=[pl.BlockSpec(memory_space=pltpu.SMEM)]
        + [pl.BlockSpec(memory_space=pltpu.VMEM)] * 5,
        out_specs=pl.BlockSpec(memory_space=pltpu.VMEM),
        scratch_shapes=[pltpu.VMEM((256, DEPTH), jnp.bfloat16)],
        compiler_params=pltpu.CompilerParams(vmem_limit_bytes=VMEM_BYTES),
    )(where, own, other, near, far, far_next)


def body(eigenvectors, gauge_links, momenta):
    space = lax.axis_size("space")
    eig = lax.axis_size("eig")
    s = lax.axis_index("space")
    e = lax.axis_index("eig")
    block = eigenvectors.reshape(ROWS, DEPTH)
    row = lax.broadcasted_iota(jnp.int32, (5, 3), 0)
    column = lax.broadcasted_iota(jnp.int32, (5, 3), 1)
    plane = jnp.where(column == 0, s, space).astype(jnp.int32)
    plane = jnp.where(row < 4, jnp.pad(momenta, ((0, 1), (0, 0))), plane)
    zh, x = e & 1, e >> 1
    where = jnp.stack([zh, x]).astype(jnp.int32)
    other_x = (x ^ 1).astype(jnp.int32).reshape(1)
    groups = [list(range(0, eig, 2)), list(range(1, eig, 2))]
    everywhere = [(a, b) for a in range(space) for b in range(eig)]

    def at(a, b):
        return a % space * eig + b

    def from_below(value):
        return lax.ppermute(value, "space", [(a, (a + 1) % space) for a in range(space)])

    partner = lax.ppermute(block, "eig", [(a, a ^ 1) for a in range(eig)])
    links_below = from_below(gauge_links)
    later, links_below = lax.optimization_barrier((block, links_below))
    copies = jnp.broadcast_to(later[None], (eig // 2, ROWS, DEPTH))
    near = lax.all_to_all(
        copies, "eig", split_axis=0, concat_axis=0, axis_index_groups=groups, tiled=True
    )
    below = from_below(later)
    below_other = lax.ppermute(
        later, ("space", "eig"), [(at(a, b), at(a + 1, b ^ 2)) for a, b in everywhere]
    )
    own = left_operand(plane, other_x, block, below, gauge_links, links_below)
    partner, own = lax.optimization_barrier((partner, own))
    far = lax.ppermute(partner, "eig", [(a, a ^ 6) for a in range(eig)])
    other = left_operand(plane, other_x, near, below_other, gauge_links, links_below)
    own, other = own.reshape(12 * ROWS, DEPTH), other.reshape(12 * ROWS, DEPTH)
    chunks = products(where, own, other, near.reshape(4 * ROWS, DEPTH), partner, far)
    chunks = chunks.reshape(space, 8, 12 * ROWS)
    got = lax.all_to_all(chunks, "space", split_axis=0, concat_axis=0, tiled=True)
    total = jnp.sum(got.astype(jnp.float32), axis=0)
    y = s // 8
    held = ((y & 1) != zh) & ((y >> 1 != x) & (y >> 1 != x ^ 3))
    pairs = [
        (at(a, b), at(a ^ 16, b ^ 2))
        for a, b in everywhere
        if (a >> 3) & 1 != b & 1 and (a >> 4) not in (b >> 1, (b >> 1) ^ 3)
    ]
    swapped = lax.ppermute(total, ("space", "eig"), pairs)
    total = jnp.where(held, swapped, total)
    return total.reshape(2, 4, 3, 4, ROWS).transpose(2, 3, 0, 4, 1)


def solution(mesh):
    return jax.shard_map(
        body,
        mesh=mesh,
        in_specs=(
            P("eig", None, None, "space", None),
            P(None, None, None, None, "space", None),
            P(),
        ),
        out_specs=P(None, None, None, "eig", "space"),
        check_vma=False,
    )
```

time: 80.6 us -> 76.2 us (0.945)
  the two profiles are of different devices: /device:TPU:1 before, /device:TPU:30 now
where the time goes in v11:
time: 76.2 us; the launch traced here: 75.7 us
  starting transfers between devices  27.9 us (37%)
  blocking collectives  22.7 us (30%)
  waiting for transfers between devices  12.4 us (16%)
  Pallas kernels  7.75 us (10%)
  local copies, waits for them, and re-layouts  4.54 us (6%)
    all_to_all x1, blocking collectives, body(): lax.all_to_all(chunks, 'space', split_axis=0, concat_axis=0, tiled=True)  22.7 us
    ppermute x1, starting transfers between devices, body(): partner = lax.ppermute(block, 'eig', [(a, a ^ 1) for a in range(eig)])  10.9 us
    ppermute x1, waiting for transfers between devices, body(): swapped = lax.ppermute(total, ('space', 'eig'), pairs)  4.91 us
    all_to_all x1, starting transfers between devices, body(): lax.all_to_all(copies, 'eig', split_axis=0, concat_axis=0, axis_index_gro...  4.77 us
    ppermute x2, starting transfers between devices, from_below(): lax.ppermute(value, 'space', [(a, (a + 1) % space) for a in range(space)])  4.68 us
    pallas_call x2, Pallas kernels, left_operand(): pl.pallas_call(left_kernel, out_shape=jax.ShapeDtypeStruct((12, ROWS, DEP...  4.5 us
    ppermute x1, waiting for transfers between devices, body(): far = lax.ppermute(partner, 'eig', [(a, a ^ 6) for a in range(eig)])  3.75 us
    ppermute x2, waiting for transfers between devices, from_below(): lax.ppermute(value, 'space', [(a, (a + 1) % space) for a in range(space)])  3.73 us
  transfers between devices with their start and end apart: 7, of which 3 were waited for; matrix products, arithmetic and copies ran while one was open for 3% of the time, Pallas kernels for 6%

profile of v11, /device:TPU:30, one launch (start us, length us, event | category | flops | bytes accessed | tf_op | source)
XLA Modules:
  0.0 75.7 jit_solution(12728159580184611314)
XLA Ops:
  0.0 0.0 copy-start
  0.0 2.0 %collective-permute-start.1 = (f32[3,3,3,2,1,512]{5,4,3,2,1,0:T(1,128)}, f32[3,3,3,2,1,512]{5,4,3,2,1,0:T(1,128)S(1)}, u32[]{:S(2)}, u32[]{:S(2)}) collective-permute-start(f32[3,3,3,2,1,512]{5,4,3,2,1,0:T(1,128)} %link_ref.3), channel_id=1, source_target_pairs={{0,8},{8,16},{16,24},{24,32},{32,40},{40,48},{48,56},{56,64},{64,7... | collective-permute-start | bytes 331784 | tf_op jit(solution)/shard_map/ppermute | solution.py:179
  2.1 1.1 %reshape.22.block_ref = bf16[32,3072]{1,0:T(8,128)(2,1)S(1)} reshape(bf16[32,3,2,1,512]{4,2,3,1,0:T(2,128)(2,1)} %param.3) | data formatting | bytes 393216 | tf_op jit(solution)/shard_map/reshape | solution.py:164
  3.1 10.9 %collective-permute-start = (bf16[32,3072]{1,0:T(8,128)(2,1)S(1)}, bf16[32,3072]{1,0:T(8,128)(2,1)}, u32[]{:S(2)}, u32[]{:S(2)}) collective-permute-start(bf16[32,3072]{1,0:T(8,128)(2,1)S(1)} %reshape.22.block_ref), channel_id=1, source_target_pairs={{0,1},{1,0},{2,3},{3,2},{4,5},{5,4},{6,7},{7,6},{8,9},{9,8},{10,11... | collective-permute-start | bytes 589832 | tf_op jit(solution)/shard_map/ppermute | solution.py:181
  14.0 0.0 collective-permute-done.1.link_below_ref
  14.1 0.0 copy-start.1
  14.1 1.0 %broadcast_in_dim.16 = bf16[4,32,3072]{2,1,0:T(8,128)(2,1)} broadcast(bf16[32,3072]{1,0:T(8,128)(2,1)S(1)} %reshape.22.block_ref), dimensions={1,2} | broadcast | bytes 983040 | tf_op jit(solution)/shard_map/broadcast_in_dim | solution.py:184
  15.0 4.8 %all-to-all-start = ((bf16[4,32,3072]{2,1,0:T(8,128)(2,1)}), bf16[4,32,3072]{2,1,0:T(8,128)(2,1)S(1)}, u32[]{:S(2)}, u32[]{:S(2)}) async-start(bf16[4,32,3072]{2,1,0:T(8,128)(2,1)} %broadcast_in_dim.16), calls=%async_computation | async-start | bytes 1572864 | tf_op jit(solution)/shard_map/all_to_all | solution.py:185
  19.8 2.6 %collective-permute-start.2 = (bf16[32,3072]{1,0:T(8,128)(2,1)S(1)}, bf16[32,3072]{1,0:T(8,128)(2,1)S(1)}, u32[]{:S(2)}, u32[]{:S(2)}) collective-permute-start(bf16[32,3072]{1,0:T(8,128)(2,1)S(1)} %reshape.22.block_ref), channel_id=1, source_target_pairs={{0,8},{8,16},{16,24},{24,32},{32,40},{40,48},{48,56},{56,64},{64,7... | collective-permute-start | bytes 589832 | tf_op jit(solution)/shard_map/ppermute | solution.py:179
  22.5 0.0 copy-done.4
  22.5 0.1 pad_select_fusion.plane_ref
  22.5 3.2 %collective-permute-start.3 = (bf16[32,3072]{1,0:T(8,128)(2,1)S(1)}, bf16[32,3072]{1,0:T(8,128)(2,1)}, u32[]{:S(2)}, u32[]{:S(2)}) collective-permute-start(bf16[32,3072]{1,0:T(8,128)(2,1)S(1)} %reshape.22.block_ref), channel_id=1, source_target_pairs={{0,10},{1,11},{2,8},{3,9},{4,14},{5,15},{6,12},{7,13},{8,18},{9,19... | collective-permute-start | bytes 589832 | tf_op jit(solution)/shard_map/ppermute | solution.py:189
  25.8 3.7 %collective-permute-done.2.below_ref = bf16[32,3072]{1,0:T(8,128)(2,1)S(1)} collective-permute-done((bf16[32,3072]{1,0:T(8,128)(2,1)S(1)}, bf16[32,3072]{1,0:T(8,128)(2,1)S(1)}, u32[]{:S(2)}, u32[]{:S(2)}) %collective-permute-start.2) | collective-permute-done | bytes 196640 | tf_op jit(solution)/shard_map/ppermute | solution.py:179
  29.5 0.0 copy-done.1
  29.5 0.0 copy-done
  29.5 0.9 %copy-done.2 = f32[3,3,3,2,1,512]{5,4,3,2,1,0:T(1,128)S(1)} copy-done((f32[3,3,3,2,1,512]{5,4,3,2,1,0:T(1,128)S(1)}, f32[3,3,3,2,1,512]{5,4,3,2,1,0:T(1,128)}, u32[]{:S(2)}) %copy-start.2) | copy-done | bytes 110616
  30.4 2.1 %shard_map.37 = bf16[12,32,3072]{2,1,0:T(8,128)(2,1)S(1)} custom-call(s32[5,3]{1,0:T(8,128)S(1)} %pad_select_fusion.plane_ref, s32[1]{0:T(128)} %bitcast.2.which_ref, bf16[32,3072]{1,0:T(8,128)(2,1)S(1)} %reshape.22.block_ref, bf16[32,3072]{1,0:T(8,128)(2,1)S(1)} %collective-permute-done.2.below_ref, f32[3,3,3,2,1,512]{5,4,3,2,1,0:T(1,128)S(1)} %copy-done, ...), custom_call_target="tpu_custom_call" | custom-call | tf_op jit(solution)/shard_map/pallas_call | solution.py:96
  32.5 0.0 collective-permute-done.far_ref
  32.5 1.9 %collective-permute-start.4 = (bf16[32,3072]{1,0:T(8,128)(2,1)}, bf16[32,3072]{1,0:T(8,128)(2,1)}, u32[]{:S(2)}, u32[]{:S(2)}) collective-permute-start(bf16[32,3072]{1,0:T(8,128)(2,1)} %collective-permute-done.far_ref), channel_id=1, source_target_pairs={{0,6},{1,7},{2,4},{3,5},{4,2},{5,3},{6,0},{7,1},{8,14},{9,15},{10,... | collective-permute-start | bytes 589832 | tf_op jit(solution)/shard_map/ppermute | solution.py:194
  34.4 0.1 pad_add_fusion.where_ref
  34.5 0.0 collective-permute-done.3.below_ref
  34.5 0.0 all-to-all-done.block_ref
  34.5 0.9 %copy-done.3 = f32[3,3,3,2,1,512]{5,4,3,2,1,0:T(1,128)S(1)} copy-done((f32[3,3,3,2,1,512]{5,4,3,2,1,0:T(1,128)S(1)}, f32[3,3,3,2,1,512]{5,4,3,2,1,0:T(1,128)}, u32[]{:S(2)}) %copy-start.3) | copy-done | bytes 110616
  35.4 2.4 %shard_map.38 = bf16[12,32,3072]{2,1,0:T(8,128)(2,1)S(1)} custom-call(s32[5,3]{1,0:T(8,128)S(1)} %pad_select_fusion.plane_ref, s32[1]{0:T(128)} %bitcast.2.which_ref, bf16[4,32,3072]{2,1,0:T(8,128)(2,1)S(1)} %all-to-all-done.block_ref, bf16[32,3072]{1,0:T(8,128)(2,1)} %collective-permute-done.3.below_ref, f32[3,3,3,2,1,512]{5,4,3,2,1,0:T(1,128)S(1)} %copy-done, ...), custom_call_target="tpu_custom_call" | custom-call | tf_op jit(solution)/shard_map/pallas_call | solution.py:96
  37.8 3.8 %collective-permute-done.4.far_next_ref = bf16[32,3072]{1,0:T(8,128)(2,1)} collective-permute-done((bf16[32,3072]{1,0:T(8,128)(2,1)}, bf16[32,3072]{1,0:T(8,128)(2,1)}, u32[]{:S(2)}, u32[]{:S(2)}) %collective-permute-start.4) | collective-permute-done | bytes 196640 | tf_op jit(solution)/shard_map/ppermute | solution.py:194
  41.6 3.2 %shard_map.39 = bf16[4,2,8,8,384]{4,3,2,1,0:T(8,128)(2,1)S(1)} custom-call(s32[2]{0:T(128)S(1)} %pad_add_fusion.where_ref, bf16[384,3072]{1,0:T(8,128)(2,1)S(1)} %bitcast.10, bf16[384,3072]{1,0:T(8,128)(2,1)S(1)} %bitcast.11, bf16[128,3072]{1,0:T(8,128)(2,1)S(1)} %bitcast.12, bf16[32,3072]{1,0:T(8,128)(2,1)} %collective-permute-done.far_ref, ...), custom_call_target="tpu_custom_call" | custom-call | tf_op jit(solution)/shard_map/pallas_call | solution.py:148
  44.8 22.7 %all_to_all.10 = bf16[64,8,384]{2,1,0:T(8,128)(2,1)S(1)} all-to-all(bf16[64,8,384]{2,1,0:T(8,128)(2,1)S(1)} %bitcast.13), channel_id=1, replica_groups=mesh['space'=64,'eig'=8] {'space'}, dimensions={0} | all-to-all | bytes 786432 | tf_op jit(solution)/shard_map/all_to_all | solution.py:199
  67.5 0.1 convert_reduce_fusion
  67.6 2.4 %collective-permute-start.5 = (f32[8,384]{1,0:T(8,128)S(1)}, f32[8,384]{1,0:T(8,128)S(1)}, u32[]{:S(2)}, u32[]{:S(2)}) collective-permute-start(f32[8,384]{1,0:T(8,128)S(1)} %convert_reduce_fusion), channel_id=1, source_target_pairs={{3,129},{5,135},{11,137},{13,143},{19,145},{21,151},{27,153},{29,1... | collective-permute-start | bytes 36872 | tf_op jit(solution)/shard_map/ppermute | solution.py:208
  70.1 4.9 %collective-permute-done.5 = f32[8,384]{1,0:T(8,128)S(1)} collective-permute-done((f32[8,384]{1,0:T(8,128)S(1)}, f32[8,384]{1,0:T(8,128)S(1)}, u32[]{:S(2)}, u32[]{:S(2)}) %collective-permute-start.5) | collective-permute-done | bytes 12320 | tf_op jit(solution)/shard_map/ppermute | solution.py:208
  75.0 0.1 reshape.28
  75.1 0.6 copy.4
  (6 shorter events, 0.0 us)
Async XLA Ops:
  0.0 29.5 %copy-start = (f32[3,3,3,2,1,512]{5,4,3,2,1,0:T(1,128)S(1)}, f32[3,3,3,2,1,512]{5,4,3,2,1,0:T(1,128)}, u32[]{:S(2)}) copy-start(f32[3,3,3,2,1,512]{5,4,3,2,1,0:T(1,128)} %link_ref.3) | copy-start | bytes 331780
  0.0 22.4 %copy-start.4 = (s32[4,3]{1,0:T(4,128)S(1)}, s32[4,3]{1,0:T(4,128)}, u32[]{:S(2)}) copy-start(s32[4,3]{1,0:T(4,128)} %param.5) | copy-start | bytes 148
  0.0 14.0 %collective-permute-start.1 = (f32[3,3,3,2,1,512]{5,4,3,2,1,0:T(1,128)}, f32[3,3,3,2,1,512]{5,4,3,2,1,0:T(1,128)S(1)}, u32[]{:S(2)}, u32[]{:S(2)}) collective-permute-start(f32[3,3,3,2,1,512]{5,4,3,2,1,0:T(1,128)} %link_ref.3), channel_id=1, source_target_pairs={{0,8},{8,16},{16,24},{24,32},{32,40},{40,48},{48,56},{56,64},{64,7... | collective-permute-start | bytes 331784 | tf_op jit(solution)/shard_map/ppermute | solution.py:179
  3.1 29.4 %collective-permute-start = (bf16[32,3072]{1,0:T(8,128)(2,1)S(1)}, bf16[32,3072]{1,0:T(8,128)(2,1)}, u32[]{:S(2)}, u32[]{:S(2)}) collective-permute-start(bf16[32,3072]{1,0:T(8,128)(2,1)S(1)} %reshape.22.block_ref), channel_id=1, source_target_pairs={{0,1},{1,0},{2,3},{3,2},{4,5},{5,4},{6,7},{7,6},{8,9},{9,8},{10,11... | collective-permute-start | bytes 589832 | tf_op jit(solution)/shard_map/ppermute | solution.py:181
  14.1 15.4 %copy-start.1 = (f32[3,3,3,2,1,512]{5,4,3,2,1,0:T(1,128)}, f32[3,3,3,2,1,512]{5,4,3,2,1,0:T(1,128)S(1)}, u32[]{:S(2)}) copy-start(f32[3,3,3,2,1,512]{5,4,3,2,1,0:T(1,128)S(1)} %collective-permute-done.1.link_below_ref) | copy-start | bytes 331780
  15.0 19.5 %all-to-all-start = ((bf16[4,32,3072]{2,1,0:T(8,128)(2,1)}), bf16[4,32,3072]{2,1,0:T(8,128)(2,1)S(1)}, u32[]{:S(2)}, u32[]{:S(2)}) async-start(bf16[4,32,3072]{2,1,0:T(8,128)(2,1)} %broadcast_in_dim.16), calls=%async_computation | async-start | bytes 1572864 | tf_op jit(solution)/shard_map/all_to_all | solution.py:185
  19.8 9.7 %collective-permute-start.2 = (bf16[32,3072]{1,0:T(8,128)(2,1)S(1)}, bf16[32,3072]{1,0:T(8,128)(2,1)S(1)}, u32[]{:S(2)}, u32[]{:S(2)}) collective-permute-start(bf16[32,3072]{1,0:T(8,128)(2,1)S(1)} %reshape.22.block_ref), channel_id=1, source_target_pairs={{0,8},{8,16},{16,24},{24,32},{32,40},{40,48},{48,56},{56,64},{64,7... | collective-permute-start | bytes 589832 | tf_op jit(solution)/shard_map/ppermute | solution.py:179
  22.5 12.0 %collective-permute-start.3 = (bf16[32,3072]{1,0:T(8,128)(2,1)S(1)}, bf16[32,3072]{1,0:T(8,128)(2,1)}, u32[]{:S(2)}, u32[]{:S(2)}) collective-permute-start(bf16[32,3072]{1,0:T(8,128)(2,1)S(1)} %reshape.22.block_ref), channel_id=1, source_target_pairs={{0,10},{1,11},{2,8},{3,9},{4,14},{5,15},{6,12},{7,13},{8,18},{9,19... | collective-permute-start | bytes 589832 | tf_op jit(solution)/shard_map/ppermute | solution.py:189
  29.5 0.9 %copy-start.2 = (f32[3,3,3,2,1,512]{5,4,3,2,1,0:T(1,128)S(1)}, f32[3,3,3,2,1,512]{5,4,3,2,1,0:T(1,128)}, u32[]{:S(2)}) copy-start(f32[3,3,3,2,1,512]{5,4,3,2,1,0:T(1,128)} %copy-done.1) | copy-start | bytes 331780
  32.5 9.1 %collective-permute-start.4 = (bf16[32,3072]{1,0:T(8,128)(2,1)}, bf16[32,3072]{1,0:T(8,128)(2,1)}, u32[]{:S(2)}, u32[]{:S(2)}) collective-permute-start(bf16[32,3072]{1,0:T(8,128)(2,1)} %collective-permute-done.far_ref), channel_id=1, source_target_pairs={{0,6},{1,7},{2,4},{3,5},{4,2},{5,3},{6,0},{7,1},{8,14},{9,15},{10,... | collective-permute-start | bytes 589832 | tf_op jit(solution)/shard_map/ppermute | solution.py:194
  34.5 0.9 %copy-start.3 = (f32[3,3,3,2,1,512]{5,4,3,2,1,0:T(1,128)S(1)}, f32[3,3,3,2,1,512]{5,4,3,2,1,0:T(1,128)}, u32[]{:S(2)}) copy-start(f32[3,3,3,2,1,512]{5,4,3,2,1,0:T(1,128)} %copy-done.1) | copy-start | bytes 331780
  67.6 7.4 %collective-permute-start.5 = (f32[8,384]{1,0:T(8,128)S(1)}, f32[8,384]{1,0:T(8,128)S(1)}, u32[]{:S(2)}, u32[]{:S(2)}) collective-permute-start(f32[8,384]{1,0:T(8,128)S(1)} %convert_reduce_fusion), channel_id=1, source_target_pairs={{3,129},{5,135},{11,137},{13,143},{19,145},{21,151},{27,153},{29,1... | collective-permute-start | bytes 36872 | tf_op jit(solution)/shard_map/ppermute | solution.py:208

commit v12 on v10

--- a/solution.py
+++ b/solution.py
@@ -97,17 +97,18 @@
 
 
 def product_kernel(half_ref, left_ref, raised_ref, near_ref, far_ref, out_ref, both_ref):
-    def spread(source_ref):
+    def spread(source_ref, to):
+        real_rows, imag_rows = slice(to, to + 128), slice(to + 256, to + 384)
         for colour in range(3):
             at = 2 * SITES * colour
             real_vec = source_ref[:, at : at + SITES]
             imag_vec = source_ref[:, at + SITES : at + 2 * SITES]
-            both_ref[0:128, at : at + SITES] = real_vec
-            both_ref[0:128, at + SITES : at + 2 * SITES] = -imag_vec
-            both_ref[128:256, at : at + SITES] = imag_vec
-            both_ref[128:256, at + SITES : at + 2 * SITES] = real_vec
+            both_ref[real_rows, at : at + SITES] = real_vec
+            both_ref[real_rows, at + SITES : at + 2 * SITES] = -imag_vec
+            both_ref[imag_rows, at : at + SITES] = imag_vec
+            both_ref[imag_rows, at + SITES : at + 2 * SITES] = real_vec
 
-    def multiply(source_ref, half, least, most):
+    def multiply(source_ref, least, most):
         product = lax.dot_general(
             both_ref[...],
             source_ref[...],
@@ -115,20 +116,21 @@
             preferred_element_type=jnp.float32,
         )
         width = most - least
-        real_part = product[0:128].reshape(16, 8, width)
-        imag_part = product[128:256].reshape(16, 8, width)
-        upper = lax.broadcasted_iota(jnp.int32, (16, 8, width), 1) < 4
+        real_part = product[0:256].reshape(32, 8, width)
+        imag_part = product[256:512].reshape(32, 8, width)
+        upper = lax.broadcasted_iota(jnp.int32, (32, 8, width), 1) < 4
         even = jnp.where(upper, real_part, pltpu.roll(imag_part, 4, 1)).astype(jnp.bfloat16)
         odd = jnp.where(upper, pltpu.roll(real_part, 4, 1), imag_part).astype(jnp.bfloat16)
-        for block in range(4):
+        for block in range(8):
+            half = half_ref[0] if block < 4 else 1 - half_ref[0]
             for pair in range(4):
-                out_ref[block, half, 2 * pair, :, least:most] = even[4 * block + pair]
-                out_ref[block, half, 2 * pair + 1, :, least:most] = odd[4 * block + pair]
+                out_ref[block % 4, half, 2 * pair, :, least:most] = even[4 * block + pair]
+                out_ref[block % 4, half, 2 * pair + 1, :, least:most] = odd[4 * block + pair]
 
-    for source_ref, half in ((near_ref, half_ref[0]), (far_ref, 1 - half_ref[0])):
-        spread(source_ref)
-        multiply(left_ref, half, 0, 8 * ROWS)
-        multiply(raised_ref, half, 8 * ROWS, 12 * ROWS)
+    spread(near_ref, 0)
+    spread(far_ref, 128)
+    multiply(left_ref, 0, 8 * ROWS)
+    multiply(raised_ref, 8 * ROWS, 12 * ROWS)
 
 
 def products(half, left, raised, near, far):
@@ -138,7 +140,7 @@
         in_specs=[pl.BlockSpec(memory_space=pltpu.SMEM)]
         + [pl.BlockSpec(memory_space=pltpu.VMEM)] * 4,
         out_specs=pl.BlockSpec(memory_space=pltpu.VMEM),
-        scratch_shapes=[pltpu.VMEM((256, DEPTH), jnp.bfloat16)],
+        scratch_shapes=[pltpu.VMEM((512, DEPTH), jnp.bfloat16)],
         compiler_params=pltpu.CompilerParams(vmem_limit_bytes=VMEM_BYTES),
     )(half, left, raised, near, far)
 

time: 72.8 us -> 72.8 us (level)
  no operation moved by 1% of the time
where the time goes in v12:
time: 72.8 us; the launch traced here: 72.5 us
  blocking collectives  41.2 us (57%)
  starting transfers between devices  20.8 us (29%)
  Pallas kernels  4.61 us (6%)
  waiting for transfers between devices  2.89 us (4%)
  local copies, waits for them, and re-layouts  2.79 us (4%)
    all_to_all x1, blocking collectives, body(): lax.all_to_all(chunks, 'space', split_axis=0, concat_axis=0, tiled=True)  29.3 us
    all_gather x1, blocking collectives, body(): far = lax.all_gather(partner, 'eig', axis_index_groups=groups, tiled=True)  12 us
    ppermute x1, starting transfers between devices, body(): partner = lax.ppermute(block, 'eig', [(a, a ^ 1) for a in range(eig)])  11.5 us
    ppermute x1, starting transfers between devices, body(): lax.ppermute(raised, 'space', [(a, (a + 1) % space) for a in range(space)])  5.31 us
    all_to_all x1, starting transfers between devices, body(): lax.all_to_all(copies, 'eig', split_axis=0, concat_axis=0, axis_index_gro...  4.01 us
    all_to_all x1, waiting for transfers between devices, body(): lax.all_to_all(copies, 'eig', split_axis=0, concat_axis=0, axis_index_gro...  2.89 us
    pallas_call x1, Pallas kernels, left_operand(): pl.pallas_call(left_kernel, out_shape=[jax.ShapeDtypeStruct((8, ROWS, DEP...  2.77 us
    pallas_call x1, Pallas kernels, products(): pl.pallas_call(product_kernel, out_shape=jax.ShapeDtypeStruct((4, 2, 8, 8...  1.84 us
  transfers between devices with their start and end apart: 3, of which 1 were waited for; matrix products, arithmetic and copies ran while one was open for 1% of the time, Pallas kernels for 4%

profile of v12, /device:TPU:1, one launch (start us, length us, event | category | flops | bytes accessed | tf_op | source)
XLA Modules:
  0.0 72.5 jit_solution(704771095950264666)
XLA Ops:
  0.0 0.0 copy-start.1
  0.0 0.0 copy-start
  0.0 1.1 %reshape.23.block_ref = bf16[32,3072]{1,0:T(8,128)(2,1)S(1)} reshape(bf16[32,3,2,1,512]{4,2,3,1,0:T(2,128)(2,1)} %param.3) | data formatting | bytes 393216 | tf_op jit(solution)/shard_map/reshape | solution.py:153
  1.1 11.5 %collective-permute-start = (bf16[32,3072]{1,0:T(8,128)(2,1)S(1)}, bf16[32,3072]{1,0:T(8,128)(2,1)S(1)}, u32[]{:S(2)}, u32[]{:S(2)}) collective-permute-start(bf16[32,3072]{1,0:T(8,128)(2,1)S(1)} %reshape.23.block_ref), channel_id=1, source_target_pairs={{0,1},{1,0},{2,3},{3,2},{4,5},{5,4},{6,7},{7,6},{8,9},{9,8},{10,11... | collective-permute-start | bytes 589832 | tf_op jit(solution)/shard_map/ppermute | solution.py:161
  12.6 1.0 %broadcast_in_dim.15 = bf16[4,32,3072]{2,1,0:T(8,128)(2,1)} broadcast(bf16[32,3072]{1,0:T(8,128)(2,1)S(1)} %reshape.23.block_ref), dimensions={1,2} | broadcast | bytes 983040 | tf_op jit(solution)/shard_map/broadcast_in_dim | solution.py:162
  13.5 4.0 %all-to-all-start = ((bf16[4,32,3072]{2,1,0:T(8,128)(2,1)}), bf16[4,32,3072]{2,1,0:T(8,128)(2,1)S(1)}, u32[]{:S(2)}, u32[]{:S(2)}) async-start(bf16[4,32,3072]{2,1,0:T(8,128)(2,1)} %broadcast_in_dim.15), calls=%async_computation | async-start | bytes 1572864 | tf_op jit(solution)/shard_map/all_to_all | solution.py:163
  17.6 0.0 copy-done.1
  17.6 0.1 pad_select_fusion.plane_ref
  17.7 0.0 copy-done
  17.7 2.8 %shard_map.37 = (bf16[8,32,3072]{2,1,0:T(8,128)(2,1)S(1)}, bf16[4,32,3072]{2,1,0:T(8,128)(2,1)}) custom-call(s32[5,3]{1,0:T(8,128)S(1)} %pad_select_fusion.plane_ref, bf16[32,3072]{1,0:T(8,128)(2,1)S(1)} %reshape.23.block_ref, f32[3,3,3,2,1,512]{5,4,3,2,1,0:T(1,128)S(1)} %copy-done), custom_call_target="tpu_custom_call" | custom-call | tf_op jit(solution)/shard_map/pallas_call | solution.py:85
  20.4 0.0 collective-permute-done
  20.4 5.3 %collective-permute-start.1 = (bf16[4,32,3072]{2,1,0:T(8,128)(2,1)}, bf16[4,32,3072]{2,1,0:T(8,128)(2,1)S(1)}, u32[]{:S(2)}, u32[]{:S(2)}) collective-permute-start(bf16[4,32,3072]{2,1,0:T(8,128)(2,1)} %get-tuple-element.15), channel_id=1, source_target_pairs={{0,8},{8,16},{16,24},{24,32},{32,40},{40,48},{48,56},{56,64},{64,7... | collective-permute-start | bytes 2359304 | tf_op jit(solution)/shard_map/ppermute | solution.py:169
  25.8 2.9 %all-to-all-done = bf16[4,32,3072]{2,1,0:T(8,128)(2,1)S(1)} async-done(((bf16[4,32,3072]{2,1,0:T(8,128)(2,1)}), bf16[4,32,3072]{2,1,0:T(8,128)(2,1)S(1)}, u32[]{:S(2)}, u32[]{:S(2)}) %all-to-all-start) | async-done | bytes 786464 | tf_op jit(solution)/shard_map/all_to_all | solution.py:163
  28.6 12.0 %all_gather.3.far_ref = bf16[128,3072]{1,0:T(8,128)(2,1)S(1)} all-gather(bf16[32,3072]{1,0:T(8,128)(2,1)S(1)} %collective-permute-done), channel_id=1, replica_groups={{0,2,4,6},{1,3,5,7},{8,10,12,14},{9,11,13,15},{16,18,20,22},{17,19,21,2..., dimensions={0}, use_global_device_ids=true | all-gather | bytes 983040 | tf_op jit(solution)/shard_map/all_gather | solution.py:171
  40.6 0.0 collective-permute-done.1
  40.6 1.8 %shard_map.38 = bf16[4,2,8,8,384]{4,3,2,1,0:T(8,128)(2,1)S(1)} custom-call(s32[1]{0:T(128)} %bitcast.half_ref, bf16[256,3072]{1,0:T(8,128)(2,1)S(1)} %bitcast.9, bf16[128,3072]{1,0:T(8,128)(2,1)S(1)} %bitcast.11, bf16[128,3072]{1,0:T(8,128)(2,1)S(1)} %bitcast.8, bf16[128,3072]{1,0:T(8,128)(2,1)S(1)} %all_gather.3.far_ref), custom_call_target="tpu_custom_call" | custom-call | tf_op jit(solution)/shard_map/pallas_call | solution.py:137
  42.4 29.3 %all_to_all.10 = bf16[64,8,384]{2,1,0:T(8,128)(2,1)S(1)} all-to-all(bf16[64,8,384]{2,1,0:T(8,128)(2,1)S(1)} %bitcast.10), channel_id=1, replica_groups=mesh['space'=64,'eig'=8] {'space'}, dimensions={0} | all-to-all | bytes 786432 | tf_op jit(solution)/shard_map/all_to_all | solution.py:174
  71.7 0.1 convert_reduce_fusion
  71.8 0.1 reshape.28
  71.9 0.6 copy.4
  (2 shorter events, 0.0 us)
Async XLA Ops:
  0.0 17.6 %copy-start.1 = (s32[4,3]{1,0:T(4,128)S(1)}, s32[4,3]{1,0:T(4,128)}, u32[]{:S(2)}) copy-start(s32[4,3]{1,0:T(4,128)} %param.5) | copy-start | bytes 148
  0.0 17.7 %copy-start = (f32[3,3,3,2,1,512]{5,4,3,2,1,0:T(1,128)S(1)}, f32[3,3,3,2,1,512]{5,4,3,2,1,0:T(1,128)}, u32[]{:S(2)}) copy-start(f32[3,3,3,2,1,512]{5,4,3,2,1,0:T(1,128)} %link_ref.1) | copy-start | bytes 331780
  1.1 19.3 %collective-permute-start = (bf16[32,3072]{1,0:T(8,128)(2,1)S(1)}, bf16[32,3072]{1,0:T(8,128)(2,1)S(1)}, u32[]{:S(2)}, u32[]{:S(2)}) collective-permute-start(bf16[32,3072]{1,0:T(8,128)(2,1)S(1)} %reshape.23.block_ref), channel_id=1, source_target_pairs={{0,1},{1,0},{2,3},{3,2},{4,5},{5,4},{6,7},{7,6},{8,9},{9,8},{10,11... | collective-permute-start | bytes 589832 | tf_op jit(solution)/shard_map/ppermute | solution.py:161
  13.5 15.1 %all-to-all-start = ((bf16[4,32,3072]{2,1,0:T(8,128)(2,1)}), bf16[4,32,3072]{2,1,0:T(8,128)(2,1)S(1)}, u32[]{:S(2)}, u32[]{:S(2)}) async-start(bf16[4,32,3072]{2,1,0:T(8,128)(2,1)} %broadcast_in_dim.15), calls=%async_computation | async-start | bytes 1572864 | tf_op jit(solution)/shard_map/all_to_all | solution.py:163
  20.4 20.2 %collective-permute-start.1 = (bf16[4,32,3072]{2,1,0:T(8,128)(2,1)}, bf16[4,32,3072]{2,1,0:T(8,128)(2,1)S(1)}, u32[]{:S(2)}, u32[]{:S(2)}) collective-permute-start(bf16[4,32,3072]{2,1,0:T(8,128)(2,1)} %get-tuple-element.15), channel_id=1, source_target_pairs={{0,8},{8,16},{16,24},{24,32},{32,40},{40,48},{48,56},{56,64},{64,7... | collective-permute-start | bytes 2359304 | tf_op jit(solution)/shard_map/ppermute | solution.py:169

commit v13 on v12

--- a/solution.py
+++ b/solution.py
@@ -12,6 +12,7 @@
 SITES = LX * LY
 ROWS = 32
 DEPTH = 6 * SITES
+NEAR_ORDER = (1, 3, 0, 2)
 VMEM_BYTES = 40 * 1024 * 1024
 
 
@@ -122,10 +123,12 @@
         even = jnp.where(upper, real_part, pltpu.roll(imag_part, 4, 1)).astype(jnp.bfloat16)
         odd = jnp.where(upper, pltpu.roll(real_part, 4, 1), imag_part).astype(jnp.bfloat16)
         for block in range(8):
-            half = half_ref[0] if block < 4 else 1 - half_ref[0]
+            near = block < 4
+            half = half_ref[0] if near else 1 - half_ref[0]
+            place = NEAR_ORDER[block] if near else block - 4
             for pair in range(4):
-                out_ref[block % 4, half, 2 * pair, :, least:most] = even[4 * block + pair]
-                out_ref[block % 4, half, 2 * pair + 1, :, least:most] = odd[4 * block + pair]
+                out_ref[place, half, 2 * pair, :, least:most] = even[4 * block + pair]
+                out_ref[place, half, 2 * pair + 1, :, least:most] = odd[4 * block + pair]
 
     spread(near_ref, 0)
     spread(far_ref, 128)
@@ -160,8 +163,9 @@
 
     partner = lax.ppermute(block, "eig", [(a, a ^ 1) for a in range(eig)])
     copies = jnp.broadcast_to(block[None], (eig // 2, ROWS, DEPTH))
+    near_groups = [[2 * x + h for x in NEAR_ORDER] for h in range(2)]
     near = lax.all_to_all(
-        copies, "eig", split_axis=0, concat_axis=0, axis_index_groups=groups, tiled=True
+        copies, "eig", split_axis=0, concat_axis=0, axis_index_groups=near_groups, tiled=True
     ).reshape(eig // 2 * ROWS, DEPTH)
     left, raised = left_operand(plane, block, gauge_links)
 

time: 72.8 us -> 72.6 us (level)
  blocking collectives: 41.2 us -> 39.8 us
  waiting for transfers between devices: 2.89 us -> 4.04 us
    all_to_all x1, waiting for transfers between devices: 2.89 us -> 4.04 us  [body(): lax.all_to_all(copies, 'eig', split_axis=0, concat_axis=0, axis_index_gro...]
    all_gather x1, blocking collectives: 12 us -> 11.1 us  [body(): far = lax.all_gather(partner, 'eig', axis_index_groups=groups, tiled=True)]
where the time goes in v13:
time: 72.6 us; the launch traced here: 72.3 us
  blocking collectives  39.8 us (55%)
  starting transfers between devices  20.8 us (29%)
  Pallas kernels  4.61 us (6%)
  waiting for transfers between devices  4.04 us (6%)
  local copies, waits for them, and re-layouts  2.79 us (4%)
    all_to_all x1, blocking collectives, body(): lax.all_to_all(chunks, 'space', split_axis=0, concat_axis=0, tiled=True)  28.7 us
    ppermute x1, starting transfers between devices, body(): partner = lax.ppermute(block, 'eig', [(a, a ^ 1) for a in range(eig)])  11.5 us
    all_gather x1, blocking collectives, body(): far = lax.all_gather(partner, 'eig', axis_index_groups=groups, tiled=True)  11.1 us
    all_to_all x1, starting transfers between devices, body(): lax.all_to_all(copies, 'eig', split_axis=0, concat_axis=0, axis_index_gro...  4.67 us
    ppermute x1, starting transfers between devices, body(): lax.ppermute(raised, 'space', [(a, (a + 1) % space) for a in range(space)])  4.65 us
    all_to_all x1, waiting for transfers between devices, body(): lax.all_to_all(copies, 'eig', split_axis=0, concat_axis=0, axis_index_gro...  4.04 us
    pallas_call x1, Pallas kernels, left_operand(): pl.pallas_call(left_kernel, out_shape=[jax.ShapeDtypeStruct((8, ROWS, DEP...  2.77 us
    pallas_call x1, Pallas kernels, products(): pl.pallas_call(product_kernel, out_shape=jax.ShapeDtypeStruct((4, 2, 8, 8...  1.84 us
  transfers between devices with their start and end apart: 3, of which 1 were waited for; matrix products, arithmetic and copies ran while one was open for 1% of the time, Pallas kernels for 4%

profile of v13, /device:TPU:1, one launch (start us, length us, event | category | flops | bytes accessed | tf_op | source)
XLA Modules:
  0.0 72.3 jit_solution(13190901652992490845)
XLA Ops:
  0.0 0.0 copy-start.1
  0.0 0.0 copy-start
  0.0 1.1 %reshape.23.block_ref = bf16[32,3072]{1,0:T(8,128)(2,1)S(1)} reshape(bf16[32,3,2,1,512]{4,2,3,1,0:T(2,128)(2,1)} %param.3) | data formatting | bytes 393216 | tf_op jit(solution)/shard_map/reshape | solution.py:156
  1.1 11.5 %collective-permute-start = (bf16[32,3072]{1,0:T(8,128)(2,1)S(1)}, bf16[32,3072]{1,0:T(8,128)(2,1)S(1)}, u32[]{:S(2)}, u32[]{:S(2)}) collective-permute-start(bf16[32,3072]{1,0:T(8,128)(2,1)S(1)} %reshape.23.block_ref), channel_id=1, source_target_pairs={{0,1},{1,0},{2,3},{3,2},{4,5},{5,4},{6,7},{7,6},{8,9},{9,8},{10,11... | collective-permute-start | bytes 589832 | tf_op jit(solution)/shard_map/ppermute | solution.py:164
  12.6 1.0 %broadcast_in_dim.15 = bf16[4,32,3072]{2,1,0:T(8,128)(2,1)} broadcast(bf16[32,3072]{1,0:T(8,128)(2,1)S(1)} %reshape.23.block_ref), dimensions={1,2} | broadcast | bytes 983040 | tf_op jit(solution)/shard_map/broadcast_in_dim | solution.py:165
  13.5 4.7 %all-to-all-start = ((bf16[4,32,3072]{2,1,0:T(8,128)(2,1)}), bf16[4,32,3072]{2,1,0:T(8,128)(2,1)S(1)}, u32[]{:S(2)}, u32[]{:S(2)}) async-start(bf16[4,32,3072]{2,1,0:T(8,128)(2,1)} %broadcast_in_dim.15), calls=%async_computation | async-start | bytes 1572864 | tf_op jit(solution)/shard_map/all_to_all | solution.py:167
  18.2 0.0 copy-done.1
  18.2 0.1 pad_select_fusion.plane_ref
  18.3 0.0 copy-done
  18.3 2.8 %shard_map.37 = (bf16[8,32,3072]{2,1,0:T(8,128)(2,1)S(1)}, bf16[4,32,3072]{2,1,0:T(8,128)(2,1)}) custom-call(s32[5,3]{1,0:T(8,128)S(1)} %pad_select_fusion.plane_ref, bf16[32,3072]{1,0:T(8,128)(2,1)S(1)} %reshape.23.block_ref, f32[3,3,3,2,1,512]{5,4,3,2,1,0:T(1,128)S(1)} %copy-done), custom_call_target="tpu_custom_call" | custom-call | tf_op jit(solution)/shard_map/pallas_call | solution.py:86
  21.1 0.0 collective-permute-done
  21.1 4.6 %collective-permute-start.1 = (bf16[4,32,3072]{2,1,0:T(8,128)(2,1)}, bf16[4,32,3072]{2,1,0:T(8,128)(2,1)S(1)}, u32[]{:S(2)}, u32[]{:S(2)}) collective-permute-start(bf16[4,32,3072]{2,1,0:T(8,128)(2,1)} %get-tuple-element.15), channel_id=1, source_target_pairs={{0,8},{8,16},{16,24},{24,32},{32,40},{40,48},{48,56},{56,64},{64,7... | collective-permute-start | bytes 2359304 | tf_op jit(solution)/shard_map/ppermute | solution.py:173
  25.8 4.0 %all-to-all-done = bf16[4,32,3072]{2,1,0:T(8,128)(2,1)S(1)} async-done(((bf16[4,32,3072]{2,1,0:T(8,128)(2,1)}), bf16[4,32,3072]{2,1,0:T(8,128)(2,1)S(1)}, u32[]{:S(2)}, u32[]{:S(2)}) %all-to-all-start) | async-done | bytes 786464 | tf_op jit(solution)/shard_map/all_to_all | solution.py:167
  29.8 11.1 %all_gather.3.far_ref = bf16[128,3072]{1,0:T(8,128)(2,1)S(1)} all-gather(bf16[32,3072]{1,0:T(8,128)(2,1)S(1)} %collective-permute-done), channel_id=1, replica_groups={{0,2,4,6},{1,3,5,7},{8,10,12,14},{9,11,13,15},{16,18,20,22},{17,19,21,2..., dimensions={0}, use_global_device_ids=true | all-gather | bytes 983040 | tf_op jit(solution)/shard_map/all_gather | solution.py:175
  40.9 0.0 collective-permute-done.1
  40.9 1.8 %shard_map.38 = bf16[4,2,8,8,384]{4,3,2,1,0:T(8,128)(2,1)S(1)} custom-call(s32[1]{0:T(128)} %bitcast.half_ref, bf16[256,3072]{1,0:T(8,128)(2,1)S(1)} %bitcast.9, bf16[128,3072]{1,0:T(8,128)(2,1)S(1)} %bitcast.11, bf16[128,3072]{1,0:T(8,128)(2,1)S(1)} %bitcast.8, bf16[128,3072]{1,0:T(8,128)(2,1)S(1)} %all_gather.3.far_ref), custom_call_target="tpu_custom_call" | custom-call | tf_op jit(solution)/shard_map/pallas_call | solution.py:140
  42.7 28.7 %all_to_all.10 = bf16[64,8,384]{2,1,0:T(8,128)(2,1)S(1)} all-to-all(bf16[64,8,384]{2,1,0:T(8,128)(2,1)S(1)} %bitcast.10), channel_id=1, replica_groups=mesh['space'=64,'eig'=8] {'space'}, dimensions={0} | all-to-all | bytes 786432 | tf_op jit(solution)/shard_map/all_to_all | solution.py:178
  71.5 0.1 convert_reduce_fusion
  71.6 0.1 reshape.28
  71.7 0.6 copy.4
  (2 shorter events, 0.0 us)
Async XLA Ops:
  0.0 18.2 %copy-start.1 = (s32[4,3]{1,0:T(4,128)S(1)}, s32[4,3]{1,0:T(4,128)}, u32[]{:S(2)}) copy-start(s32[4,3]{1,0:T(4,128)} %param.5) | copy-start | bytes 148
  0.0 18.3 %copy-start = (f32[3,3,3,2,1,512]{5,4,3,2,1,0:T(1,128)S(1)}, f32[3,3,3,2,1,512]{5,4,3,2,1,0:T(1,128)}, u32[]{:S(2)}) copy-start(f32[3,3,3,2,1,512]{5,4,3,2,1,0:T(1,128)} %link_ref.1) | copy-start | bytes 331780
  1.1 20.0 %collective-permute-start = (bf16[32,3072]{1,0:T(8,128)(2,1)S(1)}, bf16[32,3072]{1,0:T(8,128)(2,1)S(1)}, u32[]{:S(2)}, u32[]{:S(2)}) collective-permute-start(bf16[32,3072]{1,0:T(8,128)(2,1)S(1)} %reshape.23.block_ref), channel_id=1, source_target_pairs={{0,1},{1,0},{2,3},{3,2},{4,5},{5,4},{6,7},{7,6},{8,9},{9,8},{10,11... | collective-permute-start | bytes 589832 | tf_op jit(solution)/shard_map/ppermute | solution.py:164
  13.5 16.2 %all-to-all-start = ((bf16[4,32,3072]{2,1,0:T(8,128)(2,1)}), bf16[4,32,3072]{2,1,0:T(8,128)(2,1)S(1)}, u32[]{:S(2)}, u32[]{:S(2)}) async-start(bf16[4,32,3072]{2,1,0:T(8,128)(2,1)} %broadcast_in_dim.15), calls=%async_computation | async-start | bytes 1572864 | tf_op jit(solution)/shard_map/all_to_all | solution.py:167
  21.1 19.8 %collective-permute-start.1 = (bf16[4,32,3072]{2,1,0:T(8,128)(2,1)}, bf16[4,32,3072]{2,1,0:T(8,128)(2,1)S(1)}, u32[]{:S(2)}, u32[]{:S(2)}) collective-permute-start(bf16[4,32,3072]{2,1,0:T(8,128)(2,1)} %get-tuple-element.15), channel_id=1, source_target_pairs={{0,8},{8,16},{16,24},{24,32},{32,40},{40,48},{48,56},{56,64},{64,7... | collective-permute-start | bytes 2359304 | tf_op jit(solution)/shard_map/ppermute | solution.py:173

commit v14 on v13

--- a/solution.py
+++ b/solution.py
@@ -12,7 +12,7 @@
 SITES = LX * LY
 ROWS = 32
 DEPTH = 6 * SITES
-NEAR_ORDER = (1, 3, 0, 2)
+NEAR_ORDER = (0, 1, 3, 2)
 VMEM_BYTES = 40 * 1024 * 1024
 
 

time: 72.6 us -> 73 us (level)
  no operation moved by 1% of the time
where the time goes in v14:
time: 73 us; the launch traced here: 72.7 us
  blocking collectives  40.4 us (55%)
  starting transfers between devices  20.8 us (28%)
  Pallas kernels  4.61 us (6%)
  waiting for transfers between devices  3.9 us (5%)
  local copies, waits for them, and re-layouts  2.79 us (4%)
    all_to_all x1, blocking collectives, body(): lax.all_to_all(chunks, 'space', split_axis=0, concat_axis=0, tiled=True)  29.4 us
    ppermute x1, starting transfers between devices, body(): partner = lax.ppermute(block, 'eig', [(a, a ^ 1) for a in range(eig)])  11.5 us
    all_gather x1, blocking collectives, body(): far = lax.all_gather(partner, 'eig', axis_index_groups=groups, tiled=True)  11 us
    ppermute x1, starting transfers between devices, body(): lax.ppermute(raised, 'space', [(a, (a + 1) % space) for a in range(space)])  5.31 us
    all_to_all x1, starting transfers between devices, body(): lax.all_to_all(copies, 'eig', split_axis=0, concat_axis=0, axis_index_gro...  4.01 us
    all_to_all x1, waiting for transfers between devices, body(): lax.all_to_all(copies, 'eig', split_axis=0, concat_axis=0, axis_index_gro...  3.9 us
    pallas_call x1, Pallas kernels, left_operand(): pl.pallas_call(left_kernel, out_shape=[jax.ShapeDtypeStruct((8, ROWS, DEP...  2.77 us
    pallas_call x1, Pallas kernels, products(): pl.pallas_call(product_kernel, out_shape=jax.ShapeDtypeStruct((4, 2, 8, 8...  1.84 us
  transfers between devices with their start and end apart: 3, of which 1 were waited for; matrix products, arithmetic and copies ran while one was open for 1% of the time, Pallas kernels for 4%

profile of v14, /device:TPU:1, one launch (start us, length us, event | category | flops | bytes accessed | tf_op | source)
XLA Modules:
  0.0 72.7 jit_solution(50499206049365639)
XLA Ops:
  0.0 0.0 copy-start.1
  0.0 0.0 copy-start
  0.0 1.1 %reshape.23.block_ref = bf16[32,3072]{1,0:T(8,128)(2,1)S(1)} reshape(bf16[32,3,2,1,512]{4,2,3,1,0:T(2,128)(2,1)} %param.3) | data formatting | bytes 393216 | tf_op jit(solution)/shard_map/reshape | solution.py:156
  1.1 11.5 %collective-permute-start = (bf16[32,3072]{1,0:T(8,128)(2,1)S(1)}, bf16[32,3072]{1,0:T(8,128)(2,1)S(1)}, u32[]{:S(2)}, u32[]{:S(2)}) collective-permute-start(bf16[32,3072]{1,0:T(8,128)(2,1)S(1)} %reshape.23.block_ref), channel_id=1, source_target_pairs={{0,1},{1,0},{2,3},{3,2},{4,5},{5,4},{6,7},{7,6},{8,9},{9,8},{10,11... | collective-permute-start | bytes 589832 | tf_op jit(solution)/shard_map/ppermute | solution.py:164
  12.6 1.0 %broadcast_in_dim.15 = bf16[4,32,3072]{2,1,0:T(8,128)(2,1)} broadcast(bf16[32,3072]{1,0:T(8,128)(2,1)S(1)} %reshape.23.block_ref), dimensions={1,2} | broadcast | bytes 983040 | tf_op jit(solution)/shard_map/broadcast_in_dim | solution.py:165
  13.5 4.0 %all-to-all-start = ((bf16[4,32,3072]{2,1,0:T(8,128)(2,1)}), bf16[4,32,3072]{2,1,0:T(8,128)(2,1)S(1)}, u32[]{:S(2)}, u32[]{:S(2)}) async-start(bf16[4,32,3072]{2,1,0:T(8,128)(2,1)} %broadcast_in_dim.15), calls=%async_computation | async-start | bytes 1572864 | tf_op jit(solution)/shard_map/all_to_all | solution.py:167
  17.6 0.0 copy-done.1
  17.6 0.1 pad_select_fusion.plane_ref
  17.7 0.0 copy-done
  17.7 2.8 %shard_map.37 = (bf16[8,32,3072]{2,1,0:T(8,128)(2,1)S(1)}, bf16[4,32,3072]{2,1,0:T(8,128)(2,1)}) custom-call(s32[5,3]{1,0:T(8,128)S(1)} %pad_select_fusion.plane_ref, bf16[32,3072]{1,0:T(8,128)(2,1)S(1)} %reshape.23.block_ref, f32[3,3,3,2,1,512]{5,4,3,2,1,0:T(1,128)S(1)} %copy-done), custom_call_target="tpu_custom_call" | custom-call | tf_op jit(solution)/shard_map/pallas_call | solution.py:86
  20.4 0.0 collective-permute-done
  20.4 5.3 %collective-permute-start.1 = (bf16[4,32,3072]{2,1,0:T(8,128)(2,1)}, bf16[4,32,3072]{2,1,0:T(8,128)(2,1)S(1)}, u32[]{:S(2)}, u32[]{:S(2)}) collective-permute-start(bf16[4,32,3072]{2,1,0:T(8,128)(2,1)} %get-tuple-element.15), channel_id=1, source_target_pairs={{0,8},{8,16},{16,24},{24,32},{32,40},{40,48},{48,56},{56,64},{64,7... | collective-permute-start | bytes 2359304 | tf_op jit(solution)/shard_map/ppermute | solution.py:173
  25.8 3.9 %all-to-all-done = bf16[4,32,3072]{2,1,0:T(8,128)(2,1)S(1)} async-done(((bf16[4,32,3072]{2,1,0:T(8,128)(2,1)}), bf16[4,32,3072]{2,1,0:T(8,128)(2,1)S(1)}, u32[]{:S(2)}, u32[]{:S(2)}) %all-to-all-start) | async-done | bytes 786464 | tf_op jit(solution)/shard_map/all_to_all | solution.py:167
  29.7 11.0 %all_gather.3.far_ref = bf16[128,3072]{1,0:T(8,128)(2,1)S(1)} all-gather(bf16[32,3072]{1,0:T(8,128)(2,1)S(1)} %collective-permute-done), channel_id=1, replica_groups={{0,2,4,6},{1,3,5,7},{8,10,12,14},{9,11,13,15},{16,18,20,22},{17,19,21,2..., dimensions={0}, use_global_device_ids=true | all-gather | bytes 983040 | tf_op jit(solution)/shard_map/all_gather | solution.py:175
  40.7 0.0 collective-permute-done.1
  40.7 1.8 %shard_map.38 = bf16[4,2,8,8,384]{4,3,2,1,0:T(8,128)(2,1)S(1)} custom-call(s32[1]{0:T(128)} %bitcast.half_ref, bf16[256,3072]{1,0:T(8,128)(2,1)S(1)} %bitcast.9, bf16[128,3072]{1,0:T(8,128)(2,1)S(1)} %bitcast.11, bf16[128,3072]{1,0:T(8,128)(2,1)S(1)} %bitcast.8, bf16[128,3072]{1,0:T(8,128)(2,1)S(1)} %all_gather.3.far_ref), custom_call_target="tpu_custom_call" | custom-call | tf_op jit(solution)/shard_map/pallas_call | solution.py:140
  42.5 29.4 %all_to_all.10 = bf16[64,8,384]{2,1,0:T(8,128)(2,1)S(1)} all-to-all(bf16[64,8,384]{2,1,0:T(8,128)(2,1)S(1)} %bitcast.10), channel_id=1, replica_groups=mesh['space'=64,'eig'=8] {'space'}, dimensions={0} | all-to-all | bytes 786432 | tf_op jit(solution)/shard_map/all_to_all | solution.py:178
  71.9 0.1 convert_reduce_fusion
  72.0 0.1 reshape.28
  72.1 0.6 copy.4
  (2 shorter events, 0.0 us)
Async XLA Ops:
  0.0 17.6 %copy-start.1 = (s32[4,3]{1,0:T(4,128)S(1)}, s32[4,3]{1,0:T(4,128)}, u32[]{:S(2)}) copy-start(s32[4,3]{1,0:T(4,128)} %param.5) | copy-start | bytes 148
  0.0 17.7 %copy-start = (f32[3,3,3,2,1,512]{5,4,3,2,1,0:T(1,128)S(1)}, f32[3,3,3,2,1,512]{5,4,3,2,1,0:T(1,128)}, u32[]{:S(2)}) copy-start(f32[3,3,3,2,1,512]{5,4,3,2,1,0:T(1,128)} %link_ref.1) | copy-start | bytes 331780
  1.1 19.3 %collective-permute-start = (bf16[32,3072]{1,0:T(8,128)(2,1)S(1)}, bf16[32,3072]{1,0:T(8,128)(2,1)S(1)}, u32[]{:S(2)}, u32[]{:S(2)}) collective-permute-start(bf16[32,3072]{1,0:T(8,128)(2,1)S(1)} %reshape.23.block_ref), channel_id=1, source_target_pairs={{0,1},{1,0},{2,3},{3,2},{4,5},{5,4},{6,7},{7,6},{8,9},{9,8},{10,11... | collective-permute-start | bytes 589832 | tf_op jit(solution)/shard_map/ppermute | solution.py:164
  13.5 16.1 %all-to-all-start = ((bf16[4,32,3072]{2,1,0:T(8,128)(2,1)}), bf16[4,32,3072]{2,1,0:T(8,128)(2,1)S(1)}, u32[]{:S(2)}, u32[]{:S(2)}) async-start(bf16[4,32,3072]{2,1,0:T(8,128)(2,1)} %broadcast_in_dim.15), calls=%async_computation | async-start | bytes 1572864 | tf_op jit(solution)/shard_map/all_to_all | solution.py:167
  20.4 20.2 %collective-permute-start.1 = (bf16[4,32,3072]{2,1,0:T(8,128)(2,1)}, bf16[4,32,3072]{2,1,0:T(8,128)(2,1)S(1)}, u32[]{:S(2)}, u32[]{:S(2)}) collective-permute-start(bf16[4,32,3072]{2,1,0:T(8,128)(2,1)} %get-tuple-element.15), channel_id=1, source_target_pairs={{0,8},{8,16},{16,24},{24,32},{32,40},{40,48},{48,56},{56,64},{64,7... | collective-permute-start | bytes 2359304 | tf_op jit(solution)/shard_map/ppermute | solution.py:173

commit v15 on v13

--- a/solution.py
+++ b/solution.py
@@ -12,6 +12,7 @@
 SITES = LX * LY
 ROWS = 32
 DEPTH = 6 * SITES
+PAD = 1024
 NEAR_ORDER = (1, 3, 0, 2)
 VMEM_BYTES = 40 * 1024 * 1024
 
@@ -162,16 +163,16 @@
     groups = [list(range(0, eig, 2)), list(range(1, eig, 2))]
 
     partner = lax.ppermute(block, "eig", [(a, a ^ 1) for a in range(eig)])
-    copies = jnp.broadcast_to(block[None], (eig // 2, ROWS, DEPTH))
+    copies = jnp.pad(block, ((0, 0), (0, PAD)))
+    copies = jnp.broadcast_to(copies[None], (eig // 2, ROWS, DEPTH + PAD))
     near_groups = [[2 * x + h for x in NEAR_ORDER] for h in range(2)]
     near = lax.all_to_all(
         copies, "eig", split_axis=0, concat_axis=0, axis_index_groups=near_groups, tiled=True
-    ).reshape(eig // 2 * ROWS, DEPTH)
+    ).reshape(eig // 2 * ROWS, DEPTH + PAD)
     left, raised = left_operand(plane, block, gauge_links)
 
     partner, left, raised = lax.optimization_barrier((partner, left, raised))
     raised = lax.ppermute(raised, "space", [(a, (a + 1) % space) for a in range(space)])
-    partner, near = lax.optimization_barrier((partner, near))
     far = lax.all_gather(partner, "eig", axis_index_groups=groups, tiled=True)
     left, raised = left.reshape(8 * ROWS, DEPTH), raised.reshape(4 * ROWS, DEPTH)
     chunks = products(half, left, raised, near, far).reshape(space, 8, 12 * ROWS)

time: 72.6 us -> 71.9 us (level)
  waiting for transfers between devices: 4.04 us -> 0.01 us
  blocking collectives: 39.8 us -> 42 us
  Pallas kernels: 4.61 us -> 5.76 us
    all_gather x1, blocking collectives: 11.1 us -> 15.3 us  [body(): far = lax.all_gather(partner, 'eig', axis_index_groups=groups, tiled=True)]
    all_to_all x1, waiting for transfers between devices: 4.04 us -> 0.01 us  [body(): lax.all_to_all(copies, 'eig', split_axis=0, concat_axis=0, axis_index_gro...]
    all_to_all x1, blocking collectives: 28.7 us -> 26.7 us  [body(): lax.all_to_all(chunks, 'space', split_axis=0, concat_axis=0, tiled=True)]
    pallas_call x1, Pallas kernels: 1.84 us -> 2.96 us  [products(): pl.pallas_call(product_kernel, out_shape=jax.ShapeDtypeStruct((4, 2, 8, 8...]
  transfers between devices with their start and end apart: 3 -> 3, of which waited for: 1 -> 0; matrix products, arithmetic and copies ran while one was open for 1% -> 2% of each run, Pallas kernels for 4% -> 4%
where the time goes in v15:
time: 71.9 us; the launch traced here: 71.6 us
  blocking collectives  42 us (58%)
  starting transfers between devices  20.6 us (29%)
  Pallas kernels  5.76 us (8%)
  local copies, waits for them, and re-layouts  2.89 us (4%)
    all_to_all x1, blocking collectives, body(): lax.all_to_all(chunks, 'space', split_axis=0, concat_axis=0, tiled=True)  26.7 us
    all_gather x1, blocking collectives, body(): far = lax.all_gather(partner, 'eig', axis_index_groups=groups, tiled=True)  15.3 us
    ppermute x1, starting transfers between devices, body(): partner = lax.ppermute(block, 'eig', [(a, a ^ 1) for a in range(eig)])  11.5 us
    all_to_all x1, starting transfers between devices, body(): lax.all_to_all(copies, 'eig', split_axis=0, concat_axis=0, axis_index_gro...  4.7 us
    ppermute x1, starting transfers between devices, body(): lax.ppermute(raised, 'space', [(a, (a + 1) % space) for a in range(space)])  4.45 us
    pallas_call x1, Pallas kernels, products(): pl.pallas_call(product_kernel, out_shape=jax.ShapeDtypeStruct((4, 2, 8, 8...  2.96 us
    pallas_call x1, Pallas kernels, left_operand(): pl.pallas_call(left_kernel, out_shape=[jax.ShapeDtypeStruct((8, ROWS, DEP...  2.8 us
  transfers between devices with their start and end apart: 3, of which 0 were waited for; matrix products, arithmetic and copies ran while one was open for 2% of the time, Pallas kernels for 4%

profile of v15, /device:TPU:1, one launch (start us, length us, event | category | flops | bytes accessed | tf_op | source)
XLA Modules:
  0.0 71.6 jit_solution(15339314537541371161)
XLA Ops:
  0.0 1.1 %reshape.23.block_ref = bf16[32,3072]{1,0:T(8,128)(2,1)S(1)} reshape(bf16[32,3,2,1,512]{4,2,3,1,0:T(2,128)(2,1)} %param.3) | data formatting | bytes 393216 | tf_op jit(solution)/shard_map/reshape | solution.py:157
  1.1 11.5 %collective-permute-start = (bf16[32,3072]{1,0:T(8,128)(2,1)S(1)}, bf16[32,3072]{1,0:T(8,128)(2,1)S(1)}, u32[]{:S(2)}, u32[]{:S(2)}) collective-permute-start(bf16[32,3072]{1,0:T(8,128)(2,1)S(1)} %reshape.23.block_ref), channel_id=1, source_target_pairs={{0,1},{1,0},{2,3},{3,2},{4,5},{5,4},{6,7},{7,6},{8,9},{9,8},{10,11... | collective-permute-start | bytes 589832 | tf_op jit(solution)/shard_map/ppermute | solution.py:165
  12.6 0.0 copy-start.2
  12.6 0.0 copy-start
  12.6 1.1 %broadcast_in_dim.16 = bf16[4,32,4096]{2,1,0:T(8,128)(2,1)} broadcast(bf16[32,4096]{1,0:T(8,128)(2,1)S(1)} %pad.9), dimensions={1,2} | broadcast | bytes 1310720 | tf_op jit(solution)/shard_map/broadcast_in_dim | solution.py:167
  13.7 4.7 %all-to-all-start = ((bf16[4,32,4096]{2,1,0:T(8,128)(2,1)}), bf16[4,32,4096]{2,1,0:T(8,128)(2,1)S(1)}, u32[]{:S(2)}, u32[]{:S(2)}) async-start(bf16[4,32,4096]{2,1,0:T(8,128)(2,1)} %broadcast_in_dim.16), calls=%async_computation | async-start | bytes 2097152 | tf_op jit(solution)/shard_map/all_to_all | solution.py:169
  18.4 0.0 copy-done.2
  18.4 0.1 pad_select_fusion.plane_ref
  18.4 0.0 copy-done
  18.5 2.8 %shard_map.37 = (bf16[8,32,3072]{2,1,0:T(8,128)(2,1)S(1)}, bf16[4,32,3072]{2,1,0:T(8,128)(2,1)}) custom-call(s32[5,3]{1,0:T(8,128)S(1)} %pad_select_fusion.plane_ref, bf16[32,3072]{1,0:T(8,128)(2,1)S(1)} %reshape.23.block_ref, f32[3,3,3,2,1,512]{5,4,3,2,1,0:T(1,128)S(1)} %copy-done), custom_call_target="tpu_custom_call" | custom-call | tf_op jit(solution)/shard_map/pallas_call | solution.py:87
  21.3 0.0 collective-permute-done
  21.3 0.0 copy-start.1
  21.3 4.4 %collective-permute-start.1 = (bf16[4,32,3072]{2,1,0:T(8,128)(2,1)}, bf16[4,32,3072]{2,1,0:T(8,128)(2,1)}, u32[]{:S(2)}, u32[]{:S(2)}) collective-permute-start(bf16[4,32,3072]{2,1,0:T(8,128)(2,1)} %get-tuple-element.13), channel_id=1, source_target_pairs={{0,8},{8,16},{16,24},{24,32},{32,40},{40,48},{48,56},{56,64},{64,7... | collective-permute-start | bytes 2359304 | tf_op jit(solution)/shard_map/ppermute | solution.py:175
  25.7 0.0 copy-done.1
  25.7 15.3 %all_gather.3.far_ref = bf16[128,3072]{1,0:T(8,128)(2,1)S(1)} all-gather(bf16[32,3072]{1,0:T(8,128)(2,1)} %copy-done.1), channel_id=1, replica_groups={{0,2,4,6},{1,3,5,7},{8,10,12,14},{9,11,13,15},{16,18,20,22},{17,19,21,2..., dimensions={0}, use_global_device_ids=true | all-gather | bytes 983040 | tf_op jit(solution)/shard_map/all_gather | solution.py:176
  41.1 0.0 all-to-all-done
  41.1 0.0 collective-permute-done.1
  41.1 3.0 %shard_map.38 = bf16[4,2,8,8,384]{4,3,2,1,0:T(8,128)(2,1)S(1)} custom-call(s32[1]{0:T(128)} %bitcast.half_ref, bf16[256,3072]{1,0:T(8,128)(2,1)S(1)} %bitcast.9, bf16[128,3072]{1,0:T(8,128)(2,1)} %bitcast.2.raised_ref, bf16[128,4096]{1,0:T(8,128)(2,1)S(1)} %bitcast.8, bf16[128,3072]{1,0:T(8,128)(2,1)S(1)} %all_gather.3.far_ref), custom_call_target="tpu_custom_call" | custom-call | tf_op jit(solution)/shard_map/pallas_call | solution.py:141
  44.0 26.7 %all_to_all.10 = bf16[64,8,384]{2,1,0:T(8,128)(2,1)S(1)} all-to-all(bf16[64,8,384]{2,1,0:T(8,128)(2,1)S(1)} %bitcast.10), channel_id=1, replica_groups=mesh['space'=64,'eig'=8] {'space'}, dimensions={0} | all-to-all | bytes 786432 | tf_op jit(solution)/shard_map/all_to_all | solution.py:179
  70.8 0.1 convert_reduce_fusion
  70.8 0.1 reshape.28
  70.9 0.6 copy.4
  (3 shorter events, 0.0 us)
Async XLA Ops:
  1.1 20.2 %collective-permute-start = (bf16[32,3072]{1,0:T(8,128)(2,1)S(1)}, bf16[32,3072]{1,0:T(8,128)(2,1)S(1)}, u32[]{:S(2)}, u32[]{:S(2)}) collective-permute-start(bf16[32,3072]{1,0:T(8,128)(2,1)S(1)} %reshape.23.block_ref), channel_id=1, source_target_pairs={{0,1},{1,0},{2,3},{3,2},{4,5},{5,4},{6,7},{7,6},{8,9},{9,8},{10,11... | collective-permute-start | bytes 589832 | tf_op jit(solution)/shard_map/ppermute | solution.py:165
  12.6 5.8 %copy-start.2 = (s32[4,3]{1,0:T(4,128)S(1)}, s32[4,3]{1,0:T(4,128)}, u32[]{:S(2)}) copy-start(s32[4,3]{1,0:T(4,128)} %param.5) | copy-start | bytes 148
  12.6 5.9 %copy-start = (f32[3,3,3,2,1,512]{5,4,3,2,1,0:T(1,128)S(1)}, f32[3,3,3,2,1,512]{5,4,3,2,1,0:T(1,128)}, u32[]{:S(2)}) copy-start(f32[3,3,3,2,1,512]{5,4,3,2,1,0:T(1,128)} %link_ref.1) | copy-start | bytes 331780
  13.7 27.4 %all-to-all-start = ((bf16[4,32,4096]{2,1,0:T(8,128)(2,1)}), bf16[4,32,4096]{2,1,0:T(8,128)(2,1)S(1)}, u32[]{:S(2)}, u32[]{:S(2)}) async-start(bf16[4,32,4096]{2,1,0:T(8,128)(2,1)} %broadcast_in_dim.16), calls=%async_computation | async-start | bytes 2097152 | tf_op jit(solution)/shard_map/all_to_all | solution.py:169
  21.3 4.5 %copy-start.1 = (bf16[32,3072]{1,0:T(8,128)(2,1)}, bf16[32,3072]{1,0:T(8,128)(2,1)S(1)}, u32[]{:S(2)}) copy-start(bf16[32,3072]{1,0:T(8,128)(2,1)S(1)} %collective-permute-done) | copy-start | bytes 589828
  21.3 19.8 %collective-permute-start.1 = (bf16[4,32,3072]{2,1,0:T(8,128)(2,1)}, bf16[4,32,3072]{2,1,0:T(8,128)(2,1)}, u32[]{:S(2)}, u32[]{:S(2)}) collective-permute-start(bf16[4,32,3072]{2,1,0:T(8,128)(2,1)} %get-tuple-element.13), channel_id=1, source_target_pairs={{0,8},{8,16},{16,24},{24,32},{32,40},{40,48},{48,56},{56,64},{64,7... | collective-permute-start | bytes 2359304 | tf_op jit(solution)/shard_map/ppermute | solution.py:175

commit v16 on v15

--- a/solution.py
+++ b/solution.py
@@ -98,7 +98,12 @@
     )(plane, block, links)
 
 
-def product_kernel(half_ref, left_ref, raised_ref, near_ref, far_ref, out_ref, both_ref):
+def product_kernel(
+    half_ref, left_ref, raised_in, near_ref, far_ref, out_ref, both_ref, raised_ref, raised_sem
+):
+    raised_copy = pltpu.make_async_copy(raised_in, raised_ref, raised_sem)
+    raised_copy.start()
+
     def spread(source_ref, to):
         real_rows, imag_rows = slice(to, to + 128), slice(to + 256, to + 384)
         for colour in range(3):
@@ -134,6 +139,7 @@
     spread(near_ref, 0)
     spread(far_ref, 128)
     multiply(left_ref, 0, 8 * ROWS)
+    raised_copy.wait()
     multiply(raised_ref, 8 * ROWS, 12 * ROWS)
 
 
@@ -141,10 +147,19 @@
     return pl.pallas_call(
         product_kernel,
         out_shape=jax.ShapeDtypeStruct((4, 2, 8, 8, 12 * ROWS), jnp.bfloat16),
-        in_specs=[pl.BlockSpec(memory_space=pltpu.SMEM)]
-        + [pl.BlockSpec(memory_space=pltpu.VMEM)] * 4,
+        in_specs=[
+            pl.BlockSpec(memory_space=pltpu.SMEM),
+            pl.BlockSpec(memory_space=pltpu.VMEM),
+            pl.BlockSpec(memory_space=pl.ANY),
+            pl.BlockSpec(memory_space=pltpu.VMEM),
+            pl.BlockSpec(memory_space=pltpu.VMEM),
+        ],
         out_specs=pl.BlockSpec(memory_space=pltpu.VMEM),
-        scratch_shapes=[pltpu.VMEM((512, DEPTH), jnp.bfloat16)],
+        scratch_shapes=[
+            pltpu.VMEM((512, DEPTH), jnp.bfloat16),
+            pltpu.VMEM((4 * ROWS, DEPTH), jnp.bfloat16),
+            pltpu.SemaphoreType.DMA,
+        ],
         compiler_params=pltpu.CompilerParams(vmem_limit_bytes=VMEM_BYTES),
     )(half, left, raised, near, far)
 

time: 71.9 us -> 72.5 us (level)
  no operation moved by 1% of the time
where the time goes in v16:
time: 72.5 us; the launch traced here: 72.2 us
  blocking collectives  42 us (58%)
  starting transfers between devices  20.6 us (28%)
  Pallas kernels  6.39 us (9%)
  local copies, waits for them, and re-layouts  2.89 us (4%)
    all_to_all x1, blocking collectives, body(): lax.all_to_all(chunks, 'space', split_axis=0, concat_axis=0, tiled=True)  26.7 us
    all_gather x1, blocking collectives, body(): far = lax.all_gather(partner, 'eig', axis_index_groups=groups, tiled=True)  15.3 us
    ppermute x1, starting transfers between devices, body(): partner = lax.ppermute(block, 'eig', [(a, a ^ 1) for a in range(eig)])  11.5 us
    all_to_all x1, starting transfers between devices, body(): lax.all_to_all(copies, 'eig', split_axis=0, concat_axis=0, axis_index_gro...  4.7 us
    ppermute x1, starting transfers between devices, body(): lax.ppermute(raised, 'space', [(a, (a + 1) % space) for a in range(space)])  4.45 us
    pallas_call x1, Pallas kernels, products(): pl.pallas_call(product_kernel, out_shape=jax.ShapeDtypeStruct((4, 2, 8, 8...  3.59 us
    pallas_call x1, Pallas kernels, left_operand(): pl.pallas_call(left_kernel, out_shape=[jax.ShapeDtypeStruct((8, ROWS, DEP...  2.8 us
  transfers between devices with their start and end apart: 3, of which 0 were waited for; matrix products, arithmetic and copies ran while one was open for 2% of the time, Pallas kernels for 4%

profile of v16, /device:TPU:1, one launch (start us, length us, event | category | flops | bytes accessed | tf_op | source)
XLA Modules:
  0.0 72.2 jit_solution(11962161583834108072)
XLA Ops:
  0.0 1.1 %reshape.23.block_ref = bf16[32,3072]{1,0:T(8,128)(2,1)S(1)} reshape(bf16[32,3,2,1,512]{4,2,3,1,0:T(2,128)(2,1)} %param.3) | data formatting | bytes 393216 | tf_op jit(solution)/shard_map/reshape | solution.py:172
  1.1 11.5 %collective-permute-start = (bf16[32,3072]{1,0:T(8,128)(2,1)S(1)}, bf16[32,3072]{1,0:T(8,128)(2,1)S(1)}, u32[]{:S(2)}, u32[]{:S(2)}) collective-permute-start(bf16[32,3072]{1,0:T(8,128)(2,1)S(1)} %reshape.23.block_ref), channel_id=1, source_target_pairs={{0,1},{1,0},{2,3},{3,2},{4,5},{5,4},{6,7},{7,6},{8,9},{9,8},{10,11... | collective-permute-start | bytes 589832 | tf_op jit(solution)/shard_map/ppermute | solution.py:180
  12.6 0.0 copy-start.2
  12.6 0.0 copy-start
  12.6 1.1 %broadcast_in_dim.16 = bf16[4,32,4096]{2,1,0:T(8,128)(2,1)} broadcast(bf16[32,4096]{1,0:T(8,128)(2,1)S(1)} %pad.9), dimensions={1,2} | broadcast | bytes 1310720 | tf_op jit(solution)/shard_map/broadcast_in_dim | solution.py:182
  13.7 4.7 %all-to-all-start = ((bf16[4,32,4096]{2,1,0:T(8,128)(2,1)}), bf16[4,32,4096]{2,1,0:T(8,128)(2,1)S(1)}, u32[]{:S(2)}, u32[]{:S(2)}) async-start(bf16[4,32,4096]{2,1,0:T(8,128)(2,1)} %broadcast_in_dim.16), calls=%async_computation | async-start | bytes 2097152 | tf_op jit(solution)/shard_map/all_to_all | solution.py:184
  18.4 0.0 copy-done.2
  18.4 0.1 pad_select_fusion.plane_ref
  18.4 0.0 copy-done
  18.5 2.8 %shard_map.37 = (bf16[8,32,3072]{2,1,0:T(8,128)(2,1)S(1)}, bf16[4,32,3072]{2,1,0:T(8,128)(2,1)}) custom-call(s32[5,3]{1,0:T(8,128)S(1)} %pad_select_fusion.plane_ref, bf16[32,3072]{1,0:T(8,128)(2,1)S(1)} %reshape.23.block_ref, f32[3,3,3,2,1,512]{5,4,3,2,1,0:T(1,128)S(1)} %copy-done), custom_call_target="tpu_custom_call" | custom-call | tf_op jit(solution)/shard_map/pallas_call | solution.py:87
  21.3 0.0 collective-permute-done
  21.3 0.0 copy-start.1
  21.3 4.4 %collective-permute-start.1 = (bf16[4,32,3072]{2,1,0:T(8,128)(2,1)}, bf16[4,32,3072]{2,1,0:T(8,128)(2,1)}, u32[]{:S(2)}, u32[]{:S(2)}) collective-permute-start(bf16[4,32,3072]{2,1,0:T(8,128)(2,1)} %get-tuple-element.13), channel_id=1, source_target_pairs={{0,8},{8,16},{16,24},{24,32},{32,40},{40,48},{48,56},{56,64},{64,7... | collective-permute-start | bytes 2359304 | tf_op jit(solution)/shard_map/ppermute | solution.py:190
  25.7 0.0 copy-done.1
  25.7 15.3 %all_gather.3.far_ref = bf16[128,3072]{1,0:T(8,128)(2,1)S(1)} all-gather(bf16[32,3072]{1,0:T(8,128)(2,1)} %copy-done.1), channel_id=1, replica_groups={{0,2,4,6},{1,3,5,7},{8,10,12,14},{9,11,13,15},{16,18,20,22},{17,19,21,2..., dimensions={0}, use_global_device_ids=true | all-gather | bytes 983040 | tf_op jit(solution)/shard_map/all_gather | solution.py:191
  41.1 0.0 all-to-all-done
  41.1 0.0 collective-permute-done.1
  41.1 3.6 %shard_map.38 = bf16[4,2,8,8,384]{4,3,2,1,0:T(8,128)(2,1)S(1)} custom-call(s32[1]{0:T(128)} %bitcast.half_ref, bf16[256,3072]{1,0:T(8,128)(2,1)S(1)} %bitcast.9, bf16[128,3072]{1,0:T(8,128)(2,1)} %bitcast.2.raised_in, bf16[128,4096]{1,0:T(8,128)(2,1)S(1)} %bitcast.8, bf16[128,3072]{1,0:T(8,128)(2,1)S(1)} %all_gather.3.far_ref), custom_call_target="tpu_custom_call" | custom-call | tf_op jit(solution)/shard_map/pallas_call | solution.py:147
  44.7 26.7 %all_to_all.10 = bf16[64,8,384]{2,1,0:T(8,128)(2,1)S(1)} all-to-all(bf16[64,8,384]{2,1,0:T(8,128)(2,1)S(1)} %bitcast.10), channel_id=1, replica_groups=mesh['space'=64,'eig'=8] {'space'}, dimensions={0} | all-to-all | bytes 786432 | tf_op jit(solution)/shard_map/all_to_all | solution.py:194
  71.4 0.1 convert_reduce_fusion
  71.5 0.1 reshape.28
  71.6 0.6 copy.4
  (3 shorter events, 0.0 us)
Async XLA Ops:
  1.1 20.2 %collective-permute-start = (bf16[32,3072]{1,0:T(8,128)(2,1)S(1)}, bf16[32,3072]{1,0:T(8,128)(2,1)S(1)}, u32[]{:S(2)}, u32[]{:S(2)}) collective-permute-start(bf16[32,3072]{1,0:T(8,128)(2,1)S(1)} %reshape.23.block_ref), channel_id=1, source_target_pairs={{0,1},{1,0},{2,3},{3,2},{4,5},{5,4},{6,7},{7,6},{8,9},{9,8},{10,11... | collective-permute-start | bytes 589832 | tf_op jit(solution)/shard_map/ppermute | solution.py:180
  12.6 5.8 %copy-start.2 = (s32[4,3]{1,0:T(4,128)S(1)}, s32[4,3]{1,0:T(4,128)}, u32[]{:S(2)}) copy-start(s32[4,3]{1,0:T(4,128)} %param.5) | copy-start | bytes 148
  12.6 5.9 %copy-start = (f32[3,3,3,2,1,512]{5,4,3,2,1,0:T(1,128)S(1)}, f32[3,3,3,2,1,512]{5,4,3,2,1,0:T(1,128)}, u32[]{:S(2)}) copy-start(f32[3,3,3,2,1,512]{5,4,3,2,1,0:T(1,128)} %link_ref.1) | copy-start | bytes 331780
  13.7 27.4 %all-to-all-start = ((bf16[4,32,4096]{2,1,0:T(8,128)(2,1)}), bf16[4,32,4096]{2,1,0:T(8,128)(2,1)S(1)}, u32[]{:S(2)}, u32[]{:S(2)}) async-start(bf16[4,32,4096]{2,1,0:T(8,128)(2,1)} %broadcast_in_dim.16), calls=%async_computation | async-start | bytes 2097152 | tf_op jit(solution)/shard_map/all_to_all | solution.py:184
  21.3 4.5 %copy-start.1 = (bf16[32,3072]{1,0:T(8,128)(2,1)}, bf16[32,3072]{1,0:T(8,128)(2,1)S(1)}, u32[]{:S(2)}) copy-start(bf16[32,3072]{1,0:T(8,128)(2,1)S(1)} %collective-permute-done) | copy-start | bytes 589828
  21.3 19.8 %collective-permute-start.1 = (bf16[4,32,3072]{2,1,0:T(8,128)(2,1)}, bf16[4,32,3072]{2,1,0:T(8,128)(2,1)}, u32[]{:S(2)}, u32[]{:S(2)}) collective-permute-start(bf16[4,32,3072]{2,1,0:T(8,128)(2,1)} %get-tuple-element.13), channel_id=1, source_target_pairs={{0,8},{8,16},{16,24},{24,32},{32,40},{40,48},{48,56},{56,64},{64,7... | collective-permute-start | bytes 2359304 | tf_op jit(solution)/shard_map/ppermute | solution.py:190

commit v17 on v16

--- a/solution.py
+++ b/solution.py
@@ -101,8 +101,13 @@
 def product_kernel(
     half_ref, left_ref, raised_in, near_ref, far_ref, out_ref, both_ref, raised_ref, raised_sem
 ):
-    raised_copy = pltpu.make_async_copy(raised_in, raised_ref, raised_sem)
-    raised_copy.start()
+    copies = []
+    for piece in range(8):
+        rows = pl.ds(16 * piece, 16)
+        copies.append(
+            pltpu.make_async_copy(raised_in.at[rows], raised_ref.at[rows], raised_sem.at[piece])
+        )
+        copies[piece].start()
 
     def spread(source_ref, to):
         real_rows, imag_rows = slice(to, to + 128), slice(to + 256, to + 384)
@@ -139,7 +144,8 @@
     spread(near_ref, 0)
     spread(far_ref, 128)
     multiply(left_ref, 0, 8 * ROWS)
-    raised_copy.wait()
+    for copy in copies:
+        copy.wait()
     multiply(raised_ref, 8 * ROWS, 12 * ROWS)
 
 
@@ -158,7 +164,7 @@
         scratch_shapes=[
             pltpu.VMEM((512, DEPTH), jnp.bfloat16),
             pltpu.VMEM((4 * ROWS, DEPTH), jnp.bfloat16),
-            pltpu.SemaphoreType.DMA,
+            pltpu.SemaphoreType.DMA((8,)),
         ],
         compiler_params=pltpu.CompilerParams(vmem_limit_bytes=VMEM_BYTES),
     )(half, left, raised, near, far)

time: 72.5 us -> 73.3 us (1.011)
  Pallas kernels: 6.39 us -> 7.16 us
    pallas_call x1, Pallas kernels: 3.59 us -> 4.37 us  [products(): pl.pallas_call(product_kernel, out_shape=jax.ShapeDtypeStruct((4, 2, 8, 8...]
where the time goes in v17:
time: 73.3 us; the launch traced here: 73 us
  blocking collectives  42 us (57%)
  starting transfers between devices  20.6 us (28%)
  Pallas kernels  7.16 us (10%)
  local copies, waits for them, and re-layouts  2.89 us (4%)
    all_to_all x1, blocking collectives, body(): lax.all_to_all(chunks, 'space', split_axis=0, concat_axis=0, tiled=True)  26.7 us
    all_gather x1, blocking collectives, body(): far = lax.all_gather(partner, 'eig', axis_index_groups=groups, tiled=True)  15.3 us
    ppermute x1, starting transfers between devices, body(): partner = lax.ppermute(block, 'eig', [(a, a ^ 1) for a in range(eig)])  11.5 us
    all_to_all x1, starting transfers between devices, body(): lax.all_to_all(copies, 'eig', split_axis=0, concat_axis=0, axis_index_gro...  4.7 us
    ppermute x1, starting transfers between devices, body(): lax.ppermute(raised, 'space', [(a, (a + 1) % space) for a in range(space)])  4.45 us
    pallas_call x1, Pallas kernels, products(): pl.pallas_call(product_kernel, out_shape=jax.ShapeDtypeStruct((4, 2, 8, 8...  4.37 us
    pallas_call x1, Pallas kernels, left_operand(): pl.pallas_call(left_kernel, out_shape=[jax.ShapeDtypeStruct((8, ROWS, DEP...  2.8 us
  transfers between devices with their start and end apart: 3, of which 0 were waited for; matrix products, arithmetic and copies ran while one was open for 2% of the time, Pallas kernels for 4%

profile of v17, /device:TPU:1, one launch (start us, length us, event | category | flops | bytes accessed | tf_op | source)
XLA Modules:
  0.0 73.0 jit_solution(1064377260565366341)
XLA Ops:
  0.0 1.1 %reshape.23.block_ref = bf16[32,3072]{1,0:T(8,128)(2,1)S(1)} reshape(bf16[32,3,2,1,512]{4,2,3,1,0:T(2,128)(2,1)} %param.3) | data formatting | bytes 393216 | tf_op jit(solution)/shard_map/reshape | solution.py:178
  1.1 11.5 %collective-permute-start = (bf16[32,3072]{1,0:T(8,128)(2,1)S(1)}, bf16[32,3072]{1,0:T(8,128)(2,1)S(1)}, u32[]{:S(2)}, u32[]{:S(2)}) collective-permute-start(bf16[32,3072]{1,0:T(8,128)(2,1)S(1)} %reshape.23.block_ref), channel_id=1, source_target_pairs={{0,1},{1,0},{2,3},{3,2},{4,5},{5,4},{6,7},{7,6},{8,9},{9,8},{10,11... | collective-permute-start | bytes 589832 | tf_op jit(solution)/shard_map/ppermute | solution.py:186
  12.6 0.0 copy-start.2
  12.6 0.0 copy-start
  12.6 1.1 %broadcast_in_dim.16 = bf16[4,32,4096]{2,1,0:T(8,128)(2,1)} broadcast(bf16[32,4096]{1,0:T(8,128)(2,1)S(1)} %pad.9), dimensions={1,2} | broadcast | bytes 1310720 | tf_op jit(solution)/shard_map/broadcast_in_dim | solution.py:188
  13.7 4.7 %all-to-all-start = ((bf16[4,32,4096]{2,1,0:T(8,128)(2,1)}), bf16[4,32,4096]{2,1,0:T(8,128)(2,1)S(1)}, u32[]{:S(2)}, u32[]{:S(2)}) async-start(bf16[4,32,4096]{2,1,0:T(8,128)(2,1)} %broadcast_in_dim.16), calls=%async_computation | async-start | bytes 2097152 | tf_op jit(solution)/shard_map/all_to_all | solution.py:190
  18.4 0.0 copy-done.2
  18.4 0.1 pad_select_fusion.plane_ref
  18.4 0.0 copy-done
  18.5 2.8 %shard_map.37 = (bf16[8,32,3072]{2,1,0:T(8,128)(2,1)S(1)}, bf16[4,32,3072]{2,1,0:T(8,128)(2,1)}) custom-call(s32[5,3]{1,0:T(8,128)S(1)} %pad_select_fusion.plane_ref, bf16[32,3072]{1,0:T(8,128)(2,1)S(1)} %reshape.23.block_ref, f32[3,3,3,2,1,512]{5,4,3,2,1,0:T(1,128)S(1)} %copy-done), custom_call_target="tpu_custom_call" | custom-call | tf_op jit(solution)/shard_map/pallas_call | solution.py:87
  21.3 0.0 collective-permute-done
  21.3 0.0 copy-start.1
  21.3 4.4 %collective-permute-start.1 = (bf16[4,32,3072]{2,1,0:T(8,128)(2,1)}, bf16[4,32,3072]{2,1,0:T(8,128)(2,1)}, u32[]{:S(2)}, u32[]{:S(2)}) collective-permute-start(bf16[4,32,3072]{2,1,0:T(8,128)(2,1)} %get-tuple-element.13), channel_id=1, source_target_pairs={{0,8},{8,16},{16,24},{24,32},{32,40},{40,48},{48,56},{56,64},{64,7... | collective-permute-start | bytes 2359304 | tf_op jit(solution)/shard_map/ppermute | solution.py:196
  25.7 0.0 copy-done.1
  25.7 15.3 %all_gather.3.far_ref = bf16[128,3072]{1,0:T(8,128)(2,1)S(1)} all-gather(bf16[32,3072]{1,0:T(8,128)(2,1)} %copy-done.1), channel_id=1, replica_groups={{0,2,4,6},{1,3,5,7},{8,10,12,14},{9,11,13,15},{16,18,20,22},{17,19,21,2..., dimensions={0}, use_global_device_ids=true | all-gather | bytes 983040 | tf_op jit(solution)/shard_map/all_gather | solution.py:197
  41.1 0.0 all-to-all-done
  41.1 0.0 collective-permute-done.1
  41.1 4.4 %shard_map.38 = bf16[4,2,8,8,384]{4,3,2,1,0:T(8,128)(2,1)S(1)} custom-call(s32[1]{0:T(128)} %bitcast.half_ref, bf16[256,3072]{1,0:T(8,128)(2,1)S(1)} %bitcast.9, bf16[128,3072]{1,0:T(8,128)(2,1)} %bitcast.2.raised_in, bf16[128,4096]{1,0:T(8,128)(2,1)S(1)} %bitcast.8, bf16[128,3072]{1,0:T(8,128)(2,1)S(1)} %all_gather.3.far_ref), custom_call_target="tpu_custom_call" | custom-call | tf_op jit(solution)/shard_map/pallas_call | solution.py:153
  45.4 26.7 %all_to_all.10 = bf16[64,8,384]{2,1,0:T(8,128)(2,1)S(1)} all-to-all(bf16[64,8,384]{2,1,0:T(8,128)(2,1)S(1)} %bitcast.10), channel_id=1, replica_groups=mesh['space'=64,'eig'=8] {'space'}, dimensions={0} | all-to-all | bytes 786432 | tf_op jit(solution)/shard_map/all_to_all | solution.py:200
  72.2 0.1 convert_reduce_fusion
  72.2 0.1 reshape.28
  72.3 0.6 copy.4
  (3 shorter events, 0.0 us)
Async XLA Ops:
  1.1 20.2 %collective-permute-start = (bf16[32,3072]{1,0:T(8,128)(2,1)S(1)}, bf16[32,3072]{1,0:T(8,128)(2,1)S(1)}, u32[]{:S(2)}, u32[]{:S(2)}) collective-permute-start(bf16[32,3072]{1,0:T(8,128)(2,1)S(1)} %reshape.23.block_ref), channel_id=1, source_target_pairs={{0,1},{1,0},{2,3},{3,2},{4,5},{5,4},{6,7},{7,6},{8,9},{9,8},{10,11... | collective-permute-start | bytes 589832 | tf_op jit(solution)/shard_map/ppermute | solution.py:186
  12.6 5.8 %copy-start.2 = (s32[4,3]{1,0:T(4,128)S(1)}, s32[4,3]{1,0:T(4,128)}, u32[]{:S(2)}) copy-start(s32[4,3]{1,0:T(4,128)} %param.5) | copy-start | bytes 148
  12.6 5.9 %copy-start = (f32[3,3,3,2,1,512]{5,4,3,2,1,0:T(1,128)S(1)}, f32[3,3,3,2,1,512]{5,4,3,2,1,0:T(1,128)}, u32[]{:S(2)}) copy-start(f32[3,3,3,2,1,512]{5,4,3,2,1,0:T(1,128)} %link_ref.1) | copy-start | bytes 331780
  13.7 27.4 %all-to-all-start = ((bf16[4,32,4096]{2,1,0:T(8,128)(2,1)}), bf16[4,32,4096]{2,1,0:T(8,128)(2,1)S(1)}, u32[]{:S(2)}, u32[]{:S(2)}) async-start(bf16[4,32,4096]{2,1,0:T(8,128)(2,1)} %broadcast_in_dim.16), calls=%async_computation | async-start | bytes 2097152 | tf_op jit(solution)/shard_map/all_to_all | solution.py:190
  21.3 4.5 %copy-start.1 = (bf16[32,3072]{1,0:T(8,128)(2,1)}, bf16[32,3072]{1,0:T(8,128)(2,1)S(1)}, u32[]{:S(2)}) copy-start(bf16[32,3072]{1,0:T(8,128)(2,1)S(1)} %collective-permute-done) | copy-start | bytes 589828
  21.3 19.8 %collective-permute-start.1 = (bf16[4,32,3072]{2,1,0:T(8,128)(2,1)}, bf16[4,32,3072]{2,1,0:T(8,128)(2,1)}, u32[]{:S(2)}, u32[]{:S(2)}) collective-permute-start(bf16[4,32,3072]{2,1,0:T(8,128)(2,1)} %get-tuple-element.13), channel_id=1, source_target_pairs={{0,8},{8,16},{16,24},{24,32},{32,40},{40,48},{48,56},{56,64},{64,7... | collective-permute-start | bytes 2359304 | tf_op jit(solution)/shard_map/ppermute | solution.py:196

commit v18 on v15

--- a/solution.py
+++ b/solution.py
@@ -13,7 +13,7 @@
 ROWS = 32
 DEPTH = 6 * SITES
 PAD = 1024
-NEAR_ORDER = (1, 3, 0, 2)
+NEAR_ORDER = (0, 1, 2, 3)
 VMEM_BYTES = 40 * 1024 * 1024
 
 

time: 71.9 us -> 72.3 us (level)
  no operation moved by 1% of the time
where the time goes in v18:
time: 72.3 us; the launch traced here: 71.9 us
  blocking collectives  42.4 us (59%)
  starting transfers between devices  20.6 us (28%)
  Pallas kernels  5.76 us (8%)
  local copies, waits for them, and re-layouts  2.89 us (4%)
    all_to_all x1, blocking collectives, body(): lax.all_to_all(chunks, 'space', split_axis=0, concat_axis=0, tiled=True)  27 us
    all_gather x1, blocking collectives, body(): far = lax.all_gather(partner, 'eig', axis_index_groups=groups, tiled=True)  15.4 us
    ppermute x1, starting transfers between devices, body(): partner = lax.ppermute(block, 'eig', [(a, a ^ 1) for a in range(eig)])  11.5 us
    ppermute x1, starting transfers between devices, body(): lax.ppermute(raised, 'space', [(a, (a + 1) % space) for a in range(space)])  5.13 us
    all_to_all x1, starting transfers between devices, body(): lax.all_to_all(copies, 'eig', split_axis=0, concat_axis=0, axis_index_gro...  4.01 us
    pallas_call x1, Pallas kernels, products(): pl.pallas_call(product_kernel, out_shape=jax.ShapeDtypeStruct((4, 2, 8, 8...  2.96 us
    pallas_call x1, Pallas kernels, left_operand(): pl.pallas_call(left_kernel, out_shape=[jax.ShapeDtypeStruct((8, ROWS, DEP...  2.8 us
  transfers between devices with their start and end apart: 3, of which 0 were waited for; matrix products, arithmetic and copies ran while one was open for 2% of the time, Pallas kernels for 4%

profile of v18, /device:TPU:1, one launch (start us, length us, event | category | flops | bytes accessed | tf_op | source)
XLA Modules:
  0.0 71.9 jit_solution(16714913994150482056)
XLA Ops:
  0.0 1.1 %reshape.23.block_ref = bf16[32,3072]{1,0:T(8,128)(2,1)S(1)} reshape(bf16[32,3,2,1,512]{4,2,3,1,0:T(2,128)(2,1)} %param.3) | data formatting | bytes 393216 | tf_op jit(solution)/shard_map/reshape | solution.py:157
  1.1 11.5 %collective-permute-start = (bf16[32,3072]{1,0:T(8,128)(2,1)S(1)}, bf16[32,3072]{1,0:T(8,128)(2,1)S(1)}, u32[]{:S(2)}, u32[]{:S(2)}) collective-permute-start(bf16[32,3072]{1,0:T(8,128)(2,1)S(1)} %reshape.23.block_ref), channel_id=1, source_target_pairs={{0,1},{1,0},{2,3},{3,2},{4,5},{5,4},{6,7},{7,6},{8,9},{9,8},{10,11... | collective-permute-start | bytes 589832 | tf_op jit(solution)/shard_map/ppermute | solution.py:165
  12.6 0.0 copy-start.2
  12.6 0.0 copy-start
  12.6 1.1 %broadcast_in_dim.16 = bf16[4,32,4096]{2,1,0:T(8,128)(2,1)} broadcast(bf16[32,4096]{1,0:T(8,128)(2,1)S(1)} %pad.9), dimensions={1,2} | broadcast | bytes 1310720 | tf_op jit(solution)/shard_map/broadcast_in_dim | solution.py:167
  13.7 4.0 %all-to-all-start = ((bf16[4,32,4096]{2,1,0:T(8,128)(2,1)}), bf16[4,32,4096]{2,1,0:T(8,128)(2,1)S(1)}, u32[]{:S(2)}, u32[]{:S(2)}) async-start(bf16[4,32,4096]{2,1,0:T(8,128)(2,1)} %broadcast_in_dim.16), calls=%async_computation | async-start | bytes 2097152 | tf_op jit(solution)/shard_map/all_to_all | solution.py:169
  17.7 0.0 copy-done.2
  17.7 0.1 pad_select_fusion.plane_ref
  17.8 0.0 copy-done
  17.8 2.8 %shard_map.37 = (bf16[8,32,3072]{2,1,0:T(8,128)(2,1)S(1)}, bf16[4,32,3072]{2,1,0:T(8,128)(2,1)}) custom-call(s32[5,3]{1,0:T(8,128)S(1)} %pad_select_fusion.plane_ref, bf16[32,3072]{1,0:T(8,128)(2,1)S(1)} %reshape.23.block_ref, f32[3,3,3,2,1,512]{5,4,3,2,1,0:T(1,128)S(1)} %copy-done), custom_call_target="tpu_custom_call" | custom-call | tf_op jit(solution)/shard_map/pallas_call | solution.py:87
  20.6 0.0 collective-permute-done
  20.6 0.0 copy-start.1
  20.6 5.1 %collective-permute-start.1 = (bf16[4,32,3072]{2,1,0:T(8,128)(2,1)}, bf16[4,32,3072]{2,1,0:T(8,128)(2,1)}, u32[]{:S(2)}, u32[]{:S(2)}) collective-permute-start(bf16[4,32,3072]{2,1,0:T(8,128)(2,1)} %get-tuple-element.13), channel_id=1, source_target_pairs={{0,8},{8,16},{16,24},{24,32},{32,40},{40,48},{48,56},{56,64},{64,7... | collective-permute-start | bytes 2359304 | tf_op jit(solution)/shard_map/ppermute | solution.py:175
  25.7 0.0 copy-done.1
  25.7 15.4 %all_gather.3.far_ref = bf16[128,3072]{1,0:T(8,128)(2,1)S(1)} all-gather(bf16[32,3072]{1,0:T(8,128)(2,1)} %copy-done.1), channel_id=1, replica_groups={{0,2,4,6},{1,3,5,7},{8,10,12,14},{9,11,13,15},{16,18,20,22},{17,19,21,2..., dimensions={0}, use_global_device_ids=true | all-gather | bytes 983040 | tf_op jit(solution)/shard_map/all_gather | solution.py:176
  41.1 0.0 all-to-all-done
  41.2 0.0 collective-permute-done.1
  41.2 3.0 %shard_map.38 = bf16[4,2,8,8,384]{4,3,2,1,0:T(8,128)(2,1)S(1)} custom-call(s32[1]{0:T(128)} %bitcast.half_ref, bf16[256,3072]{1,0:T(8,128)(2,1)S(1)} %bitcast.9, bf16[128,3072]{1,0:T(8,128)(2,1)} %bitcast.2.raised_ref, bf16[128,4096]{1,0:T(8,128)(2,1)S(1)} %bitcast.8, bf16[128,3072]{1,0:T(8,128)(2,1)S(1)} %all_gather.3.far_ref), custom_call_target="tpu_custom_call" | custom-call | tf_op jit(solution)/shard_map/pallas_call | solution.py:141
  44.1 27.0 %all_to_all.10 = bf16[64,8,384]{2,1,0:T(8,128)(2,1)S(1)} all-to-all(bf16[64,8,384]{2,1,0:T(8,128)(2,1)S(1)} %bitcast.10), channel_id=1, replica_groups=mesh['space'=64,'eig'=8] {'space'}, dimensions={0} | all-to-all | bytes 786432 | tf_op jit(solution)/shard_map/all_to_all | solution.py:179
  71.1 0.1 convert_reduce_fusion
  71.2 0.1 reshape.28
  71.3 0.6 copy.4
  (3 shorter events, 0.0 us)
Async XLA Ops:
  1.1 19.5 %collective-permute-start = (bf16[32,3072]{1,0:T(8,128)(2,1)S(1)}, bf16[32,3072]{1,0:T(8,128)(2,1)S(1)}, u32[]{:S(2)}, u32[]{:S(2)}) collective-permute-start(bf16[32,3072]{1,0:T(8,128)(2,1)S(1)} %reshape.23.block_ref), channel_id=1, source_target_pairs={{0,1},{1,0},{2,3},{3,2},{4,5},{5,4},{6,7},{7,6},{8,9},{9,8},{10,11... | collective-permute-start | bytes 589832 | tf_op jit(solution)/shard_map/ppermute | solution.py:165
  12.6 5.1 %copy-start.2 = (s32[4,3]{1,0:T(4,128)S(1)}, s32[4,3]{1,0:T(4,128)}, u32[]{:S(2)}) copy-start(s32[4,3]{1,0:T(4,128)} %param.5) | copy-start | bytes 148
  12.6 5.2 %copy-start = (f32[3,3,3,2,1,512]{5,4,3,2,1,0:T(1,128)S(1)}, f32[3,3,3,2,1,512]{5,4,3,2,1,0:T(1,128)}, u32[]{:S(2)}) copy-start(f32[3,3,3,2,1,512]{5,4,3,2,1,0:T(1,128)} %link_ref.1) | copy-start | bytes 331780
  13.7 27.5 %all-to-all-start = ((bf16[4,32,4096]{2,1,0:T(8,128)(2,1)}), bf16[4,32,4096]{2,1,0:T(8,128)(2,1)S(1)}, u32[]{:S(2)}, u32[]{:S(2)}) async-start(bf16[4,32,4096]{2,1,0:T(8,128)(2,1)} %broadcast_in_dim.16), calls=%async_computation | async-start | bytes 2097152 | tf_op jit(solution)/shard_map/all_to_all | solution.py:169
  20.6 5.1 %copy-start.1 = (bf16[32,3072]{1,0:T(8,128)(2,1)}, bf16[32,3072]{1,0:T(8,128)(2,1)S(1)}, u32[]{:S(2)}) copy-start(bf16[32,3072]{1,0:T(8,128)(2,1)S(1)} %collective-permute-done) | copy-start | bytes 589828
  20.6 20.6 %collective-permute-start.1 = (bf16[4,32,3072]{2,1,0:T(8,128)(2,1)}, bf16[4,32,3072]{2,1,0:T(8,128)(2,1)}, u32[]{:S(2)}, u32[]{:S(2)}) collective-permute-start(bf16[4,32,3072]{2,1,0:T(8,128)(2,1)} %get-tuple-element.13), channel_id=1, source_target_pairs={{0,8},{8,16},{16,24},{24,32},{32,40},{40,48},{48,56},{56,64},{64,7... | collective-permute-start | bytes 2359304 | tf_op jit(solution)/shard_map/ppermute | solution.py:175

commit v19 on v18

--- a/solution.py
+++ b/solution.py
@@ -13,7 +13,7 @@
 ROWS = 32
 DEPTH = 6 * SITES
 PAD = 1024
-NEAR_ORDER = (0, 1, 2, 3)
+NEAR_ORDER = (2, 0, 3, 1)
 VMEM_BYTES = 40 * 1024 * 1024
 
 

time: 72.3 us -> 71.4 us (0.988)
  blocking collectives: 42.4 us -> 40.3 us
  starting transfers between devices: 20.6 us -> 21.9 us
    all_to_all x1, starting transfers between devices: 4.01 us -> 6.23 us  [body(): lax.all_to_all(copies, 'eig', split_axis=0, concat_axis=0, axis_index_gro...]
    all_gather x1, blocking collectives: 15.4 us -> 14.1 us  [body(): far = lax.all_gather(partner, 'eig', axis_index_groups=groups, tiled=True)]
    ppermute x1, starting transfers between devices: 5.13 us -> 4.21 us  [body(): lax.ppermute(raised, 'space', [(a, (a + 1) % space) for a in range(space)])]
    all_to_all x1, blocking collectives: 27 us -> 26.2 us  [body(): lax.all_to_all(chunks, 'space', split_axis=0, concat_axis=0, tiled=True)]
where the time goes in v19:
time: 71.4 us; the launch traced here: 71.1 us
  blocking collectives  40.3 us (56%)
  starting transfers between devices  21.9 us (31%)
  Pallas kernels  5.76 us (8%)
  local copies, waits for them, and re-layouts  2.89 us (4%)
    all_to_all x1, blocking collectives, body(): lax.all_to_all(chunks, 'space', split_axis=0, concat_axis=0, tiled=True)  26.2 us
    all_gather x1, blocking collectives, body(): far = lax.all_gather(partner, 'eig', axis_index_groups=groups, tiled=True)  14.1 us
    ppermute x1, starting transfers between devices, body(): partner = lax.ppermute(block, 'eig', [(a, a ^ 1) for a in range(eig)])  11.5 us
    all_to_all x1, starting transfers between devices, body(): lax.all_to_all(copies, 'eig', split_axis=0, concat_axis=0, axis_index_gro...  6.23 us
    ppermute x1, starting transfers between devices, body(): lax.ppermute(raised, 'space', [(a, (a + 1) % space) for a in range(space)])  4.21 us
    pallas_call x1, Pallas kernels, products(): pl.pallas_call(product_kernel, out_shape=jax.ShapeDtypeStruct((4, 2, 8, 8...  2.96 us
    pallas_call x1, Pallas kernels, left_operand(): pl.pallas_call(left_kernel, out_shape=[jax.ShapeDtypeStruct((8, ROWS, DEP...  2.8 us
  transfers between devices with their start and end apart: 3, of which 0 were waited for; matrix products, arithmetic and copies ran while one was open for 2% of the time, Pallas kernels for 4%

profile of v19, /device:TPU:1, one launch (start us, length us, event | category | flops | bytes accessed | tf_op | source)
XLA Modules:
  0.0 71.1 jit_solution(4298992470894293236)
XLA Ops:
  0.0 1.1 %reshape.23.block_ref = bf16[32,3072]{1,0:T(8,128)(2,1)S(1)} reshape(bf16[32,3,2,1,512]{4,2,3,1,0:T(2,128)(2,1)} %param.3) | data formatting | bytes 393216 | tf_op jit(solution)/shard_map/reshape | solution.py:157
  1.1 11.5 %collective-permute-start = (bf16[32,3072]{1,0:T(8,128)(2,1)S(1)}, bf16[32,3072]{1,0:T(8,128)(2,1)S(1)}, u32[]{:S(2)}, u32[]{:S(2)}) collective-permute-start(bf16[32,3072]{1,0:T(8,128)(2,1)S(1)} %reshape.23.block_ref), channel_id=1, source_target_pairs={{0,1},{1,0},{2,3},{3,2},{4,5},{5,4},{6,7},{7,6},{8,9},{9,8},{10,11... | collective-permute-start | bytes 589832 | tf_op jit(solution)/shard_map/ppermute | solution.py:165
  12.6 0.0 copy-start.2
  12.6 0.0 copy-start
  12.6 1.1 %broadcast_in_dim.16 = bf16[4,32,4096]{2,1,0:T(8,128)(2,1)} broadcast(bf16[32,4096]{1,0:T(8,128)(2,1)S(1)} %pad.9), dimensions={1,2} | broadcast | bytes 1310720 | tf_op jit(solution)/shard_map/broadcast_in_dim | solution.py:167
  13.7 6.2 %all-to-all-start = ((bf16[4,32,4096]{2,1,0:T(8,128)(2,1)}), bf16[4,32,4096]{2,1,0:T(8,128)(2,1)S(1)}, u32[]{:S(2)}, u32[]{:S(2)}) async-start(bf16[4,32,4096]{2,1,0:T(8,128)(2,1)} %broadcast_in_dim.16), calls=%async_computation | async-start | bytes 2097152 | tf_op jit(solution)/shard_map/all_to_all | solution.py:169
  19.9 0.0 copy-done.2
  19.9 0.1 pad_select_fusion.plane_ref
  20.0 0.0 copy-done
  20.0 2.8 %shard_map.37 = (bf16[8,32,3072]{2,1,0:T(8,128)(2,1)S(1)}, bf16[4,32,3072]{2,1,0:T(8,128)(2,1)}) custom-call(s32[5,3]{1,0:T(8,128)S(1)} %pad_select_fusion.plane_ref, bf16[32,3072]{1,0:T(8,128)(2,1)S(1)} %reshape.23.block_ref, f32[3,3,3,2,1,512]{5,4,3,2,1,0:T(1,128)S(1)} %copy-done), custom_call_target="tpu_custom_call" | custom-call | tf_op jit(solution)/shard_map/pallas_call | solution.py:87
  22.8 0.0 collective-permute-done
  22.8 0.0 copy-start.1
  22.8 4.2 %collective-permute-start.1 = (bf16[4,32,3072]{2,1,0:T(8,128)(2,1)}, bf16[4,32,3072]{2,1,0:T(8,128)(2,1)}, u32[]{:S(2)}, u32[]{:S(2)}) collective-permute-start(bf16[4,32,3072]{2,1,0:T(8,128)(2,1)} %get-tuple-element.13), channel_id=1, source_target_pairs={{0,8},{8,16},{16,24},{24,32},{32,40},{40,48},{48,56},{56,64},{64,7... | collective-permute-start | bytes 2359304 | tf_op jit(solution)/shard_map/ppermute | solution.py:175
  27.0 0.0 copy-done.1
  27.0 14.1 %all_gather.3.far_ref = bf16[128,3072]{1,0:T(8,128)(2,1)S(1)} all-gather(bf16[32,3072]{1,0:T(8,128)(2,1)} %copy-done.1), channel_id=1, replica_groups={{0,2,4,6},{1,3,5,7},{8,10,12,14},{9,11,13,15},{16,18,20,22},{17,19,21,2..., dimensions={0}, use_global_device_ids=true | all-gather | bytes 983040 | tf_op jit(solution)/shard_map/all_gather | solution.py:176
  41.1 0.0 all-to-all-done
  41.1 0.0 collective-permute-done.1
  41.1 3.0 %shard_map.38 = bf16[4,2,8,8,384]{4,3,2,1,0:T(8,128)(2,1)S(1)} custom-call(s32[1]{0:T(128)} %bitcast.half_ref, bf16[256,3072]{1,0:T(8,128)(2,1)S(1)} %bitcast.9, bf16[128,3072]{1,0:T(8,128)(2,1)} %bitcast.2.raised_ref, bf16[128,4096]{1,0:T(8,128)(2,1)S(1)} %bitcast.8, bf16[128,3072]{1,0:T(8,128)(2,1)S(1)} %all_gather.3.far_ref), custom_call_target="tpu_custom_call" | custom-call | tf_op jit(solution)/shard_map/pallas_call | solution.py:141
  44.1 26.2 %all_to_all.10 = bf16[64,8,384]{2,1,0:T(8,128)(2,1)S(1)} all-to-all(bf16[64,8,384]{2,1,0:T(8,128)(2,1)S(1)} %bitcast.10), channel_id=1, replica_groups=mesh['space'=64,'eig'=8] {'space'}, dimensions={0} | all-to-all | bytes 786432 | tf_op jit(solution)/shard_map/all_to_all | solution.py:179
  70.3 0.1 convert_reduce_fusion
  70.4 0.1 reshape.28
  70.5 0.6 copy.4
  (3 shorter events, 0.0 us)
Async XLA Ops:
  1.1 21.7 %collective-permute-start = (bf16[32,3072]{1,0:T(8,128)(2,1)S(1)}, bf16[32,3072]{1,0:T(8,128)(2,1)S(1)}, u32[]{:S(2)}, u32[]{:S(2)}) collective-permute-start(bf16[32,3072]{1,0:T(8,128)(2,1)S(1)} %reshape.23.block_ref), channel_id=1, source_target_pairs={{0,1},{1,0},{2,3},{3,2},{4,5},{5,4},{6,7},{7,6},{8,9},{9,8},{10,11... | collective-permute-start | bytes 589832 | tf_op jit(solution)/shard_map/ppermute | solution.py:165
  12.6 7.3 %copy-start.2 = (s32[4,3]{1,0:T(4,128)S(1)}, s32[4,3]{1,0:T(4,128)}, u32[]{:S(2)}) copy-start(s32[4,3]{1,0:T(4,128)} %param.5) | copy-start | bytes 148
  12.6 7.4 %copy-start = (f32[3,3,3,2,1,512]{5,4,3,2,1,0:T(1,128)S(1)}, f32[3,3,3,2,1,512]{5,4,3,2,1,0:T(1,128)}, u32[]{:S(2)}) copy-start(f32[3,3,3,2,1,512]{5,4,3,2,1,0:T(1,128)} %link_ref.1) | copy-start | bytes 331780
  13.7 27.4 %all-to-all-start = ((bf16[4,32,4096]{2,1,0:T(8,128)(2,1)}), bf16[4,32,4096]{2,1,0:T(8,128)(2,1)S(1)}, u32[]{:S(2)}, u32[]{:S(2)}) async-start(bf16[4,32,4096]{2,1,0:T(8,128)(2,1)} %broadcast_in_dim.16), calls=%async_computation | async-start | bytes 2097152 | tf_op jit(solution)/shard_map/all_to_all | solution.py:169
  22.8 4.2 %copy-start.1 = (bf16[32,3072]{1,0:T(8,128)(2,1)}, bf16[32,3072]{1,0:T(8,128)(2,1)S(1)}, u32[]{:S(2)}) copy-start(bf16[32,3072]{1,0:T(8,128)(2,1)S(1)} %collective-permute-done) | copy-start | bytes 589828
  22.8 18.3 %collective-permute-start.1 = (bf16[4,32,3072]{2,1,0:T(8,128)(2,1)}, bf16[4,32,3072]{2,1,0:T(8,128)(2,1)}, u32[]{:S(2)}, u32[]{:S(2)}) collective-permute-start(bf16[4,32,3072]{2,1,0:T(8,128)(2,1)} %get-tuple-element.13), channel_id=1, source_target_pairs={{0,8},{8,16},{16,24},{24,32},{32,40},{40,48},{48,56},{56,64},{64,7... | collective-permute-start | bytes 2359304 | tf_op jit(solution)/shard_map/ppermute | solution.py:175

commit v20 on v19

--- a/solution.py
+++ b/solution.py
@@ -13,7 +13,7 @@
 ROWS = 32
 DEPTH = 6 * SITES
 PAD = 1024
-NEAR_ORDER = (2, 0, 3, 1)
+NEAR_ORDER = (0, 2, 1, 3)
 VMEM_BYTES = 40 * 1024 * 1024
 
 

time: 71.4 us -> 72.4 us (1.014)
  blocking collectives: 40.3 us -> 42.6 us
  starting transfers between devices: 21.9 us -> 20.6 us
    all_to_all x1, starting transfers between devices: 6.23 us -> 4.01 us  [body(): lax.all_to_all(copies, 'eig', split_axis=0, concat_axis=0, axis_index_gro...]
    all_to_all x1, blocking collectives: 26.2 us -> 28 us  [body(): lax.all_to_all(chunks, 'space', split_axis=0, concat_axis=0, tiled=True)]
    ppermute x1, starting transfers between devices: 4.21 us -> 5.13 us  [body(): lax.ppermute(raised, 'space', [(a, (a + 1) % space) for a in range(space)])]
where the time goes in v20:
time: 72.4 us; the launch traced here: 72.1 us
  blocking collectives  42.6 us (59%)
  starting transfers between devices  20.6 us (28%)
  Pallas kernels  5.76 us (8%)
  local copies, waits for them, and re-layouts  2.89 us (4%)
    all_to_all x1, blocking collectives, body(): lax.all_to_all(chunks, 'space', split_axis=0, concat_axis=0, tiled=True)  28 us
    all_gather x1, blocking collectives, body(): far = lax.all_gather(partner, 'eig', axis_index_groups=groups, tiled=True)  14.6 us
    ppermute x1, starting transfers between devices, body(): partner = lax.ppermute(block, 'eig', [(a, a ^ 1) for a in range(eig)])  11.5 us
    ppermute x1, starting transfers between devices, body(): lax.ppermute(raised, 'space', [(a, (a + 1) % space) for a in range(space)])  5.13 us
    all_to_all x1, starting transfers between devices, body(): lax.all_to_all(copies, 'eig', split_axis=0, concat_axis=0, axis_index_gro...  4.01 us
    pallas_call x1, Pallas kernels, products(): pl.pallas_call(product_kernel, out_shape=jax.ShapeDtypeStruct((4, 2, 8, 8...  2.96 us
    pallas_call x1, Pallas kernels, left_operand(): pl.pallas_call(left_kernel, out_shape=[jax.ShapeDtypeStruct((8, ROWS, DEP...  2.8 us
  transfers between devices with their start and end apart: 3, of which 0 were waited for; matrix products, arithmetic and copies ran while one was open for 2% of the time, Pallas kernels for 4%

profile of v20, /device:TPU:1, one launch (start us, length us, event | category | flops | bytes accessed | tf_op | source)
XLA Modules:
  0.0 72.1 jit_solution(11091141681200882195)
XLA Ops:
  0.0 1.1 %reshape.23.block_ref = bf16[32,3072]{1,0:T(8,128)(2,1)S(1)} reshape(bf16[32,3,2,1,512]{4,2,3,1,0:T(2,128)(2,1)} %param.3) | data formatting | bytes 393216 | tf_op jit(solution)/shard_map/reshape | solution.py:157
  1.1 11.5 %collective-permute-start = (bf16[32,3072]{1,0:T(8,128)(2,1)S(1)}, bf16[32,3072]{1,0:T(8,128)(2,1)S(1)}, u32[]{:S(2)}, u32[]{:S(2)}) collective-permute-start(bf16[32,3072]{1,0:T(8,128)(2,1)S(1)} %reshape.23.block_ref), channel_id=1, source_target_pairs={{0,1},{1,0},{2,3},{3,2},{4,5},{5,4},{6,7},{7,6},{8,9},{9,8},{10,11... | collective-permute-start | bytes 589832 | tf_op jit(solution)/shard_map/ppermute | solution.py:165
  12.6 0.0 copy-start.2
  12.6 0.0 copy-start
  12.6 1.1 %broadcast_in_dim.16 = bf16[4,32,4096]{2,1,0:T(8,128)(2,1)} broadcast(bf16[32,4096]{1,0:T(8,128)(2,1)S(1)} %pad.9), dimensions={1,2} | broadcast | bytes 1310720 | tf_op jit(solution)/shard_map/broadcast_in_dim | solution.py:167
  13.7 4.0 %all-to-all-start = ((bf16[4,32,4096]{2,1,0:T(8,128)(2,1)}), bf16[4,32,4096]{2,1,0:T(8,128)(2,1)S(1)}, u32[]{:S(2)}, u32[]{:S(2)}) async-start(bf16[4,32,4096]{2,1,0:T(8,128)(2,1)} %broadcast_in_dim.16), calls=%async_computation | async-start | bytes 2097152 | tf_op jit(solution)/shard_map/all_to_all | solution.py:169
  17.7 0.0 copy-done.2
  17.7 0.1 pad_select_fusion.plane_ref
  17.8 0.0 copy-done
  17.8 2.8 %shard_map.37 = (bf16[8,32,3072]{2,1,0:T(8,128)(2,1)S(1)}, bf16[4,32,3072]{2,1,0:T(8,128)(2,1)}) custom-call(s32[5,3]{1,0:T(8,128)S(1)} %pad_select_fusion.plane_ref, bf16[32,3072]{1,0:T(8,128)(2,1)S(1)} %reshape.23.block_ref, f32[3,3,3,2,1,512]{5,4,3,2,1,0:T(1,128)S(1)} %copy-done), custom_call_target="tpu_custom_call" | custom-call | tf_op jit(solution)/shard_map/pallas_call | solution.py:87
  20.6 0.0 collective-permute-done
  20.6 0.0 copy-start.1
  20.6 5.1 %collective-permute-start.1 = (bf16[4,32,3072]{2,1,0:T(8,128)(2,1)}, bf16[4,32,3072]{2,1,0:T(8,128)(2,1)}, u32[]{:S(2)}, u32[]{:S(2)}) collective-permute-start(bf16[4,32,3072]{2,1,0:T(8,128)(2,1)} %get-tuple-element.13), channel_id=1, source_target_pairs={{0,8},{8,16},{16,24},{24,32},{32,40},{40,48},{48,56},{56,64},{64,7... | collective-permute-start | bytes 2359304 | tf_op jit(solution)/shard_map/ppermute | solution.py:175
  25.7 0.0 copy-done.1
  25.7 14.6 %all_gather.3.far_ref = bf16[128,3072]{1,0:T(8,128)(2,1)S(1)} all-gather(bf16[32,3072]{1,0:T(8,128)(2,1)} %copy-done.1), channel_id=1, replica_groups={{0,2,4,6},{1,3,5,7},{8,10,12,14},{9,11,13,15},{16,18,20,22},{17,19,21,2..., dimensions={0}, use_global_device_ids=true | all-gather | bytes 983040 | tf_op jit(solution)/shard_map/all_gather | solution.py:176
  40.4 0.0 all-to-all-done
  40.4 0.0 collective-permute-done.1
  40.4 3.0 %shard_map.38 = bf16[4,2,8,8,384]{4,3,2,1,0:T(8,128)(2,1)S(1)} custom-call(s32[1]{0:T(128)} %bitcast.half_ref, bf16[256,3072]{1,0:T(8,128)(2,1)S(1)} %bitcast.9, bf16[128,3072]{1,0:T(8,128)(2,1)} %bitcast.2.raised_ref, bf16[128,4096]{1,0:T(8,128)(2,1)S(1)} %bitcast.8, bf16[128,3072]{1,0:T(8,128)(2,1)S(1)} %all_gather.3.far_ref), custom_call_target="tpu_custom_call" | custom-call | tf_op jit(solution)/shard_map/pallas_call | solution.py:141
  43.3 28.0 %all_to_all.10 = bf16[64,8,384]{2,1,0:T(8,128)(2,1)S(1)} all-to-all(bf16[64,8,384]{2,1,0:T(8,128)(2,1)S(1)} %bitcast.10), channel_id=1, replica_groups=mesh['space'=64,'eig'=8] {'space'}, dimensions={0} | all-to-all | bytes 786432 | tf_op jit(solution)/shard_map/all_to_all | solution.py:179
  71.3 0.1 convert_reduce_fusion
  71.4 0.1 reshape.28
  71.5 0.6 copy.4
  (3 shorter events, 0.0 us)
Async XLA Ops:
  1.1 19.5 %collective-permute-start = (bf16[32,3072]{1,0:T(8,128)(2,1)S(1)}, bf16[32,3072]{1,0:T(8,128)(2,1)S(1)}, u32[]{:S(2)}, u32[]{:S(2)}) collective-permute-start(bf16[32,3072]{1,0:T(8,128)(2,1)S(1)} %reshape.23.block_ref), channel_id=1, source_target_pairs={{0,1},{1,0},{2,3},{3,2},{4,5},{5,4},{6,7},{7,6},{8,9},{9,8},{10,11... | collective-permute-start | bytes 589832 | tf_op jit(solution)/shard_map/ppermute | solution.py:165
  12.6 5.1 %copy-start.2 = (s32[4,3]{1,0:T(4,128)S(1)}, s32[4,3]{1,0:T(4,128)}, u32[]{:S(2)}) copy-start(s32[4,3]{1,0:T(4,128)} %param.5) | copy-start | bytes 148
  12.6 5.2 %copy-start = (f32[3,3,3,2,1,512]{5,4,3,2,1,0:T(1,128)S(1)}, f32[3,3,3,2,1,512]{5,4,3,2,1,0:T(1,128)}, u32[]{:S(2)}) copy-start(f32[3,3,3,2,1,512]{5,4,3,2,1,0:T(1,128)} %link_ref.1) | copy-start | bytes 331780
  13.7 26.7 %all-to-all-start = ((bf16[4,32,4096]{2,1,0:T(8,128)(2,1)}), bf16[4,32,4096]{2,1,0:T(8,128)(2,1)S(1)}, u32[]{:S(2)}, u32[]{:S(2)}) async-start(bf16[4,32,4096]{2,1,0:T(8,128)(2,1)} %broadcast_in_dim.16), calls=%async_computation | async-start | bytes 2097152 | tf_op jit(solution)/shard_map/all_to_all | solution.py:169
  20.6 5.1 %copy-start.1 = (bf16[32,3072]{1,0:T(8,128)(2,1)}, bf16[32,3072]{1,0:T(8,128)(2,1)S(1)}, u32[]{:S(2)}) copy-start(bf16[32,3072]{1,0:T(8,128)(2,1)S(1)} %collective-permute-done) | copy-start | bytes 589828
  20.6 19.8 %collective-permute-start.1 = (bf16[4,32,3072]{2,1,0:T(8,128)(2,1)}, bf16[4,32,3072]{2,1,0:T(8,128)(2,1)}, u32[]{:S(2)}, u32[]{:S(2)}) collective-permute-start(bf16[4,32,3072]{2,1,0:T(8,128)(2,1)} %get-tuple-element.13), channel_id=1, source_target_pairs={{0,8},{8,16},{16,24},{24,32},{32,40},{40,48},{48,56},{56,64},{64,7... | collective-permute-start | bytes 2359304 | tf_op jit(solution)/shard_map/ppermute | solution.py:175

commit v21 on v20

--- a/solution.py
+++ b/solution.py
@@ -13,7 +13,7 @@
 ROWS = 32
 DEPTH = 6 * SITES
 PAD = 1024
-NEAR_ORDER = (0, 2, 1, 3)
+NEAR_ORDER = (3, 1, 2, 0)
 VMEM_BYTES = 40 * 1024 * 1024
 
 

time: 72.4 us -> 71.9 us (level)
  blocking collectives: 42.6 us -> 41 us
  starting transfers between devices: 20.6 us -> 21.6 us
    all_to_all x1, starting transfers between devices: 4.01 us -> 5.97 us  [body(): lax.all_to_all(copies, 'eig', split_axis=0, concat_axis=0, axis_index_gro...]
    all_gather x1, blocking collectives: 14.6 us -> 13.5 us  [body(): far = lax.all_gather(partner, 'eig', axis_index_groups=groups, tiled=True)]
    ppermute x1, starting transfers between devices: 5.13 us -> 4.21 us  [body(): lax.ppermute(raised, 'space', [(a, (a + 1) % space) for a in range(space)])]
where the time goes in v21:
time: 71.9 us; the launch traced here: 71.6 us
  blocking collectives  41 us (57%)
  starting transfers between devices  21.6 us (30%)
  Pallas kernels  5.76 us (8%)
  local copies, waits for them, and re-layouts  2.89 us (4%)
    all_to_all x1, blocking collectives, body(): lax.all_to_all(chunks, 'space', split_axis=0, concat_axis=0, tiled=True)  27.6 us
    all_gather x1, blocking collectives, body(): far = lax.all_gather(partner, 'eig', axis_index_groups=groups, tiled=True)  13.5 us
    ppermute x1, starting transfers between devices, body(): partner = lax.ppermute(block, 'eig', [(a, a ^ 1) for a in range(eig)])  11.5 us
    all_to_all x1, starting transfers between devices, body(): lax.all_to_all(copies, 'eig', split_axis=0, concat_axis=0, axis_index_gro...  5.97 us
    ppermute x1, starting transfers between devices, body(): lax.ppermute(raised, 'space', [(a, (a + 1) % space) for a in range(space)])  4.21 us
    pallas_call x1, Pallas kernels, products(): pl.pallas_call(product_kernel, out_shape=jax.ShapeDtypeStruct((4, 2, 8, 8...  2.96 us
    pallas_call x1, Pallas kernels, left_operand(): pl.pallas_call(left_kernel, out_shape=[jax.ShapeDtypeStruct((8, ROWS, DEP...  2.8 us
  transfers between devices with their start and end apart: 3, of which 0 were waited for; matrix products, arithmetic and copies ran while one was open for 2% of the time, Pallas kernels for 4%

profile of v21, /device:TPU:1, one launch (start us, length us, event | category | flops | bytes accessed | tf_op | source)
XLA Modules:
  0.0 71.6 jit_solution(5031495351473419967)
XLA Ops:
  0.0 1.1 %reshape.23.block_ref = bf16[32,3072]{1,0:T(8,128)(2,1)S(1)} reshape(bf16[32,3,2,1,512]{4,2,3,1,0:T(2,128)(2,1)} %param.3) | data formatting | bytes 393216 | tf_op jit(solution)/shard_map/reshape | solution.py:157
  1.1 11.5 %collective-permute-start = (bf16[32,3072]{1,0:T(8,128)(2,1)S(1)}, bf16[32,3072]{1,0:T(8,128)(2,1)S(1)}, u32[]{:S(2)}, u32[]{:S(2)}) collective-permute-start(bf16[32,3072]{1,0:T(8,128)(2,1)S(1)} %reshape.23.block_ref), channel_id=1, source_target_pairs={{0,1},{1,0},{2,3},{3,2},{4,5},{5,4},{6,7},{7,6},{8,9},{9,8},{10,11... | collective-permute-start | bytes 589832 | tf_op jit(solution)/shard_map/ppermute | solution.py:165
  12.6 0.0 copy-start.2
  12.6 0.0 copy-start
  12.6 1.1 %broadcast_in_dim.16 = bf16[4,32,4096]{2,1,0:T(8,128)(2,1)} broadcast(bf16[32,4096]{1,0:T(8,128)(2,1)S(1)} %pad.9), dimensions={1,2} | broadcast | bytes 1310720 | tf_op jit(solution)/shard_map/broadcast_in_dim | solution.py:167
  13.7 6.0 %all-to-all-start = ((bf16[4,32,4096]{2,1,0:T(8,128)(2,1)}), bf16[4,32,4096]{2,1,0:T(8,128)(2,1)S(1)}, u32[]{:S(2)}, u32[]{:S(2)}) async-start(bf16[4,32,4096]{2,1,0:T(8,128)(2,1)} %broadcast_in_dim.16), calls=%async_computation | async-start | bytes 2097152 | tf_op jit(solution)/shard_map/all_to_all | solution.py:169
  19.6 0.0 copy-done.2
  19.6 0.1 pad_select_fusion.plane_ref
  19.7 0.0 copy-done
  19.7 2.8 %shard_map.37 = (bf16[8,32,3072]{2,1,0:T(8,128)(2,1)S(1)}, bf16[4,32,3072]{2,1,0:T(8,128)(2,1)}) custom-call(s32[5,3]{1,0:T(8,128)S(1)} %pad_select_fusion.plane_ref, bf16[32,3072]{1,0:T(8,128)(2,1)S(1)} %reshape.23.block_ref, f32[3,3,3,2,1,512]{5,4,3,2,1,0:T(1,128)S(1)} %copy-done), custom_call_target="tpu_custom_call" | custom-call | tf_op jit(solution)/shard_map/pallas_call | solution.py:87
  22.5 0.0 collective-permute-done
  22.5 0.0 copy-start.1
  22.5 4.2 %collective-permute-start.1 = (bf16[4,32,3072]{2,1,0:T(8,128)(2,1)}, bf16[4,32,3072]{2,1,0:T(8,128)(2,1)}, u32[]{:S(2)}, u32[]{:S(2)}) collective-permute-start(bf16[4,32,3072]{2,1,0:T(8,128)(2,1)} %get-tuple-element.13), channel_id=1, source_target_pairs={{0,8},{8,16},{16,24},{24,32},{32,40},{40,48},{48,56},{56,64},{64,7... | collective-permute-start | bytes 2359304 | tf_op jit(solution)/shard_map/ppermute | solution.py:175
  26.8 0.0 copy-done.1
  26.8 13.5 %all_gather.3.far_ref = bf16[128,3072]{1,0:T(8,128)(2,1)S(1)} all-gather(bf16[32,3072]{1,0:T(8,128)(2,1)} %copy-done.1), channel_id=1, replica_groups={{0,2,4,6},{1,3,5,7},{8,10,12,14},{9,11,13,15},{16,18,20,22},{17,19,21,2..., dimensions={0}, use_global_device_ids=true | all-gather | bytes 983040 | tf_op jit(solution)/shard_map/all_gather | solution.py:176
  40.2 0.0 all-to-all-done
  40.3 0.0 collective-permute-done.1
  40.3 3.0 %shard_map.38 = bf16[4,2,8,8,384]{4,3,2,1,0:T(8,128)(2,1)S(1)} custom-call(s32[1]{0:T(128)} %bitcast.half_ref, bf16[256,3072]{1,0:T(8,128)(2,1)S(1)} %bitcast.9, bf16[128,3072]{1,0:T(8,128)(2,1)} %bitcast.2.raised_ref, bf16[128,4096]{1,0:T(8,128)(2,1)S(1)} %bitcast.8, bf16[128,3072]{1,0:T(8,128)(2,1)S(1)} %all_gather.3.far_ref), custom_call_target="tpu_custom_call" | custom-call | tf_op jit(solution)/shard_map/pallas_call | solution.py:141
  43.2 27.6 %all_to_all.10 = bf16[64,8,384]{2,1,0:T(8,128)(2,1)S(1)} all-to-all(bf16[64,8,384]{2,1,0:T(8,128)(2,1)S(1)} %bitcast.10), channel_id=1, replica_groups=mesh['space'=64,'eig'=8] {'space'}, dimensions={0} | all-to-all | bytes 786432 | tf_op jit(solution)/shard_map/all_to_all | solution.py:179
  70.8 0.1 convert_reduce_fusion
  70.9 0.1 reshape.28
  71.0 0.6 copy.4
  (3 shorter events, 0.0 us)
Async XLA Ops:
  1.1 21.5 %collective-permute-start = (bf16[32,3072]{1,0:T(8,128)(2,1)S(1)}, bf16[32,3072]{1,0:T(8,128)(2,1)S(1)}, u32[]{:S(2)}, u32[]{:S(2)}) collective-permute-start(bf16[32,3072]{1,0:T(8,128)(2,1)S(1)} %reshape.23.block_ref), channel_id=1, source_target_pairs={{0,1},{1,0},{2,3},{3,2},{4,5},{5,4},{6,7},{7,6},{8,9},{9,8},{10,11... | collective-permute-start | bytes 589832 | tf_op jit(solution)/shard_map/ppermute | solution.py:165
  12.6 7.1 %copy-start.2 = (s32[4,3]{1,0:T(4,128)S(1)}, s32[4,3]{1,0:T(4,128)}, u32[]{:S(2)}) copy-start(s32[4,3]{1,0:T(4,128)} %param.5) | copy-start | bytes 148
  12.6 7.2 %copy-start = (f32[3,3,3,2,1,512]{5,4,3,2,1,0:T(1,128)S(1)}, f32[3,3,3,2,1,512]{5,4,3,2,1,0:T(1,128)}, u32[]{:S(2)}) copy-start(f32[3,3,3,2,1,512]{5,4,3,2,1,0:T(1,128)} %link_ref.1) | copy-start | bytes 331780
  13.7 26.6 %all-to-all-start = ((bf16[4,32,4096]{2,1,0:T(8,128)(2,1)}), bf16[4,32,4096]{2,1,0:T(8,128)(2,1)S(1)}, u32[]{:S(2)}, u32[]{:S(2)}) async-start(bf16[4,32,4096]{2,1,0:T(8,128)(2,1)} %broadcast_in_dim.16), calls=%async_computation | async-start | bytes 2097152 | tf_op jit(solution)/shard_map/all_to_all | solution.py:169
  22.5 4.2 %copy-start.1 = (bf16[32,3072]{1,0:T(8,128)(2,1)}, bf16[32,3072]{1,0:T(8,128)(2,1)S(1)}, u32[]{:S(2)}) copy-start(bf16[32,3072]{1,0:T(8,128)(2,1)S(1)} %collective-permute-done) | copy-start | bytes 589828
  22.5 17.7 %collective-permute-start.1 = (bf16[4,32,3072]{2,1,0:T(8,128)(2,1)}, bf16[4,32,3072]{2,1,0:T(8,128)(2,1)}, u32[]{:S(2)}, u32[]{:S(2)}) collective-permute-start(bf16[4,32,3072]{2,1,0:T(8,128)(2,1)} %get-tuple-element.13), channel_id=1, source_target_pairs={{0,8},{8,16},{16,24},{24,32},{32,40},{40,48},{48,56},{56,64},{64,7... | collective-permute-start | bytes 2359304 | tf_op jit(solution)/shard_map/ppermute | solution.py:175
